TPU v7x, 32 devices: a whole 2x2x4 slice. The times are simulated.
32 devices in a mesh: tilt: 4 (over x, core), tile: 8 (over z, y).
Axes of the slice: x: 2, y: 2, z: 4, core: 2. Of those that a mesh axis runs over, the one named last changes fastest.
Arguments:
- obj_re: float32 [4, 1024, 3072], P('tilt', None, 'tile'), may hold values from -6 to 6
- obj_im: float32 [4, 1024, 3072], P('tilt', None, 'tile'), may hold values from -6 to 6
- probe_re: float32 [256, 256], replicated, may hold values from -3 to 3
- probe_im: float32 [256, 256], replicated, may hold values from -3 to 3
- intensity: float32 [4, 64, 256, 256], P('tilt', 'tile'), may hold values from 0.25 to 4
- positions: int32 [4, 64, 2], P('tilt', 'tile'), may hold values from 0 to 768, as said below
- counts: int32 [4, 8], P('tilt', 'tile'), may hold values from 1 to 8, as said below
- row_shift: int32 [4], P('tilt'), may hold values from 0 to 1023
- slope: int32 [4], replicated, may hold values from -384 to 384
- volume: float32 [16, 1024, 3072], P(None, ('tilt', 'tile')), may hold values from -1.5 to 1.5
Outputs:
- volume_new: float32 [16, 1024, 3072], P(None, ('tilt', 'tile'))
- reprojection: float32 [4, 1024, 3072], P('tilt', None, 'tile')
- object_gradient: float32 [2, 4, 1024, 3072], P(None, 'tilt', None, 'tile')
Inputs may be any that keep to these rules, and one draw needn't show every extreme that they name: `positions`: each slot's row lies in 0 to 768 and its column in 0 to 256; slots from counts on are unused. `counts`: at least one tile uses all 8 slots.
All inputs are finite; a program needn't handle non-finite values.
Results may differ from a plain program's by a relative error of at most 0.0003.
Values sent between devices are 32-bit elements; how exact they have to be, the bound alone decides.
No kernel may reach another device: no remote copies, remote signals or barrier semaphores. Data moves between devices by JAX's collectives and lax.ppermute only.
A program may use at most 128 MiB of HBM per device.

v0:
```python
import functools
import math

import jax
import jax.numpy as jnp
import ml_dtypes
import numpy as np
from jax import lax
from jax.experimental import pallas as pl
from jax.experimental.pallas import tpu as pltpu
from jax.sharding import PartitionSpec as P

LANES = 128
SUBLANES = 8
VMEM_BYTES = 60 * 1024 * 1024
SPLIT = jnp.bfloat16
ANY = pl.BlockSpec(memory_space=pl.ANY)
SMEM = pl.BlockSpec(memory_space=pltpu.SMEM)
VMEM = pl.BlockSpec(memory_space=pltpu.VMEM)


def passed_along(block, axis, distance):
    devices = range(lax.axis_size(axis))
    route = [(i - distance, i) for i in devices if i - distance in devices]
    return lax.ppermute(block, axis, route)


def halves(table):
    high = table.astype(ml_dtypes.bfloat16)
    low = (table - high.astype(np.float64)).astype(ml_dtypes.bfloat16)
    return high, low


def dft_tables(length):
    half = length // 2
    index = np.arange(length)
    angle = (index[:, None] * index[None, :] % length) * (-2.0 * math.pi / length)
    wave = (np.cos(angle) + 1j * np.sin(angle)) / math.sqrt(length)
    tables = []
    for parity in (0, 1):
        part = wave[parity::2, :half]
        pair = np.block([[part.real, -part.imag], [part.imag, part.real]])
        tables += [*halves(pair), *halves(pair.T)]
    order = np.concatenate([index[0::2], index[1::2]])
    spread = np.zeros((length, length))
    spread[order, index] = 1.0
    return np.stack(tables), spread.astype(ml_dtypes.bfloat16)


def split(x):
    high = x.astype(SPLIT)
    return high, (x - high.astype(jnp.float32)).astype(SPLIT)


def dot(a, b):
    return jnp.dot(a, b, preferred_element_type=jnp.float32)


def dot3(ah, al, bh, bl):
    return dot(ah, bh) + dot(ah, bl) + dot(al, bh)


def lanes_of(shape):
    return lax.broadcasted_iota(jnp.int32, shape, len(shape) - 1)


def rows_of(shape):
    return lax.broadcasted_iota(jnp.int32, shape, len(shape) - 2)


def rolled(x, row, lane):
    size = x.shape[0]
    tiles = x.shape[1] // LANES
    cut = []
    for tile in range(tiles):
        part = x[:, tile * LANES : (tile + 1) * LANES].reshape(-1, SUBLANES, LANES)
        turned = pltpu.roll(part, row, axis=1)
        before = jnp.concatenate([turned[-1:], turned[:-1]], axis=0)
        part = jnp.where(rows_of(part.shape) < row, before, turned).reshape(size, LANES)
        cut.append(pltpu.roll(part, lane, axis=1))
    keep = lanes_of(cut[0].shape) >= lane
    return [jnp.where(keep, cut[tile], cut[tile - 1]) for tile in range(tiles)]


def probe_kernel(
    used_ref, positions_ref, shift_ref,
    tile_re, tile_im, edge_re, edge_im, probe_re, probe_im, intensity, tables, spread,
    grad_ref, spill_ref, routed_ref,
    ext, acc, measured, turned, uh, ul, vh, vl, residual, sems, slot_sems,
):
    height = ext.shape[2]
    tiles = ext.shape[1] - 1
    size = probe_re.shape[0]
    half = size // 2
    used = used_ref[0, 0]
    copies = []
    for part, (tile, edge) in enumerate(((tile_re, edge_re), (tile_im, edge_im))):
        for column in range(tiles):
            copies.append(
                pltpu.make_async_copy(
                    tile.at[:, pl.ds(column * LANES, LANES)],
                    ext.at[part, column],
                    sems.at[part * (tiles + 1) + column],
                )
            )
        copies.append(
            pltpu.make_async_copy(edge, ext.at[part, tiles], sems.at[part * (tiles + 1) + tiles])
        )
    for copy in copies:
        copy.start()

    def fetch(slot):
        return [
            pltpu.make_async_copy(
                intensity.at[slot, :, pl.ds(tile * LANES, LANES)],
                measured.at[slot, tile],
                slot_sems.at[slot, tile],
            )
            for tile in range(2)
        ]

    slots = measured.shape[0]
    for slot in range(slots):
        @pl.when(slot < used)
        def _():
            for copy in fetch(slot):
                copy.start()

    @pl.loop(0, height // size)
    def _(chunk):
        rows = pl.ds(chunk * size, size)
        for part in range(2):
            for column in range(tiles + 1):
                acc[part, column, rows, :] = jnp.zeros((size, LANES), jnp.float32)

    for copy in copies:
        copy.wait()

    le, let, lo, lot = 0, 2, 4, 6

    def table(which):
        return tables[which], tables[which + 1]

    @pl.loop(0, used)
    def _(slot):
        row = positions_ref[slot, 0]
        col = positions_ref[slot, 1]
        first = pl.multiple_of(row // SUBLANES * SUBLANES, SUBLANES)
        row_rest = row - first
        wrap = pl.multiple_of(jnp.minimum(first + size, height - SUBLANES), SUBLANES)
        column = col // LANES
        lane_rest = col - column * LANES
        wrap_column = jnp.minimum(column + 2, tiles)
        body = pl.ds(first, size)
        tail = pl.ds(wrap, SUBLANES)
        low_rows = rows_of((SUBLANES, LANES)) < row_rest
        low_lanes = lanes_of((size, LANES)) < lane_rest

        for part, probe in enumerate((probe_re, probe_im)):
            for tile, piece in enumerate(rolled(probe[...], row_rest, lane_rest)):
                turned[part, tile] = piece

        def window(part, at):
            block = ext[part, at, body, :]
            top = jnp.where(low_rows, ext[part, at, tail, :], block[:SUBLANES])
            return jnp.concatenate([top, block[SUBLANES:]], axis=0)

        psi = []
        for tile in range(2):
            if tile == 0:
                o_re, o_im = (
                    jnp.where(low_lanes, window(part, wrap_column), window(part, column))
                    for part in range(2)
                )
            else:
                o_re, o_im = (window(part, column + 1) for part in range(2))
            p_re, p_im = turned[0, tile], turned[1, tile]
            psi.append((p_re * o_re - p_im * o_im, p_re * o_im + p_im * o_re))
        for part in range(2):
            lanes = slice(part * LANES, (part + 1) * LANES)
            uh[:, lanes], ul[:, lanes] = split(psi[0][part] + psi[1][part])
            vh[:, lanes], vl[:, lanes] = split(psi[0][part] - psi[1][part])
        even = dot3(uh[...], ul[...], *table(let))
        odd = dot3(vh[...], vl[...], *table(lot))
        for part in range(2):
            rows = slice(part * half, (part + 1) * half)
            for tile, y in enumerate((even, odd)):
                lanes = slice(tile * LANES, (tile + 1) * LANES)
                y = y[:, part * LANES : (part + 1) * LANES]
                uh[rows, lanes], ul[rows, lanes] = split(y[:half] + y[half:])
                vh[rows, lanes], vl[rows, lanes] = split(y[:half] - y[half:])
        for copy in fetch(slot):
            copy.wait()
        for parity, (h, l, which) in enumerate(((uh, ul, le), (vh, vl, lo))):
            th, tl = table(which)
            far = dot(th, h[...]) + dot(tl, h[...]) + dot(th, l[...])
            f_re, f_im = far[:half], far[half:]
            m = [measured[slot, tile, pl.ds(parity, half, stride=2), :] for tile in range(2)]
            mh, ml = split(jnp.concatenate(m, axis=1))
            excess = f_re * f_re + f_im * f_im - (dot(mh, spread[...]) + dot(ml, spread[...]))
            h[:half, :], l[:half, :] = split(excess * f_re)
            h[half:, :], l[half:, :] = split(excess * f_im)
        th, tl = table(let)
        even = dot(th, uh[...]) + dot(tl, uh[...]) + dot(th, ul[...])
        th, tl = table(lot)
        odd = dot(th, vh[...]) + dot(tl, vh[...]) + dot(th, vl[...])
        for part in range(2):
            rows = slice(part * half, (part + 1) * half)
            lanes = slice(part * LANES, (part + 1) * LANES)
            for sign in range(2):
                out = slice(sign * half, (sign + 1) * half)
                t = even[rows] + odd[rows] if sign == 0 else even[rows] - odd[rows]
                uh[out, lanes], ul[out, lanes] = split(t[:, :LANES])
                vh[out, lanes], vl[out, lanes] = split(t[:, LANES:])
        even = dot3(uh[...], ul[...], *table(le))
        odd = dot3(vh[...], vl[...], *table(lo))
        for tile in range(2):
            chi = even + odd if tile == 0 else even - odd
            c_re, c_im = chi[:, :LANES], chi[:, LANES:]
            p_re, p_im = turned[0, tile], turned[1, tile]
            for part, g in enumerate((p_re * c_re + p_im * c_im, p_re * c_im - p_im * c_re)):
                if tile == 0:
                    places = (
                        (column, jnp.where(low_lanes, 0.0, g)),
                        (wrap_column, jnp.where(low_lanes, g, 0.0)),
                    )
                else:
                    places = ((column + 1, g),)
                for at, value in places:
                    top = value[:SUBLANES]
                    kept = jnp.where(low_rows, 0.0, top)
                    acc[part, at, body, :] += jnp.concatenate([kept, value[SUBLANES:]], axis=0)
                    acc[part, at, tail, :] += jnp.where(low_rows, top, 0.0)

    @pl.loop(0, height // size)
    def _(chunk):
        rows = pl.ds(chunk * size, size)
        for part in range(2):
            for column in range(tiles):
                grad_ref[part, 0, rows, column * LANES : (column + 1) * LANES] = acc[
                    part, column, rows, :
                ]
            spill_ref[part, rows, :] = acc[part, tiles, rows, :]


def probe_phase(used, positions, shift, tile_re, tile_im, edge_re, edge_im, probe_re, probe_im, intensity):
    height, width = tile_re.shape
    size = probe_re.shape[0]
    slots = intensity.shape[0]
    columns = width // LANES
    tables, spread = dft_tables(size)
    plane = pltpu.VMEM((size, size), SPLIT)
    passes = 26 * slots
    return pl.pallas_call(
        probe_kernel,
        out_shape=(
            jax.ShapeDtypeStruct((2, 1, height, width), jnp.float32),
            jax.ShapeDtypeStruct((2, height, LANES), jnp.float32),
            jax.ShapeDtypeStruct((SUBLANES, LANES), jnp.float32),
        ),
        in_specs=[SMEM, SMEM, SMEM, ANY, ANY, ANY, ANY, VMEM, VMEM, ANY, VMEM, VMEM],
        out_specs=(VMEM, VMEM, VMEM),
        scratch_shapes=[
            pltpu.VMEM((2, columns + 1, height, LANES), jnp.float32),
            pltpu.VMEM((2, columns + 1, height, LANES), jnp.float32),
            pltpu.VMEM((slots, 2, size, LANES), jnp.float32),
            pltpu.VMEM((2, 2, size, LANES), jnp.float32),
            plane, plane, plane, plane,
            pltpu.VMEM((SUBLANES, LANES), jnp.float32),
            pltpu.SemaphoreType.DMA((2 * (columns + 1),)),
            pltpu.SemaphoreType.DMA((slots, 2)),
        ],
        compiler_params=pltpu.CompilerParams(vmem_limit_bytes=VMEM_BYTES),
        cost_estimate=pl.CostEstimate(
            flops=passes * 2 * size**3, bytes_accessed=16 * height * width, transcendentals=0
        ),
        name="probes",
    )(used, positions, shift, tile_re, tile_im, edge_re, edge_im, probe_re, probe_im, intensity,
      jnp.asarray(tables), jnp.asarray(spread))


def moved(values, steps, weight, lead, amount, base, count):
    tile = jnp.floor_divide(amount, LANES)
    rest = amount - tile * LANES
    at = pl.ds(base + tile, count + 1)
    x = values[lead, at] + weight * steps[lead, at]
    x = x.reshape((count + 1) * SUBLANES, LANES)
    x = pltpu.roll(x, jnp.where(rest == 0, 0, LANES - rest), axis=1)
    keep = lanes_of((count * SUBLANES, LANES)) < LANES - rest
    return jnp.where(keep, x[: count * SUBLANES], x[SUBLANES:])


def volume_kernel(slope_ref, pieces, volume, fresh, parts, near, slope_near, cells, slope_cells):
    depth = volume.shape[0]
    columns = volume.shape[2]
    count = columns // LANES
    margin = (near.shape[1] - count) // 2
    tilts = near.shape[0]
    per_tile = pieces.shape[2] // LANES
    tiles = pieces.shape[0] // tilts
    last = lanes_of((SUBLANES, LANES)) == LANES - 1
    first = lanes_of((SUBLANES, LANES)) == 0

    def place(ref, lead, tile, value):
        ref[lead, margin + tile] = value
        if tile < margin:
            ref[lead, margin + tile + count] = value
        if tile >= count - margin:
            ref[lead, margin + tile - count] = value

    for tilt in range(tilts):
        row = []
        for tile in range(count):
            lanes = slice(tile % per_tile * LANES, (tile % per_tile + 1) * LANES)
            row.append(pieces[tilt * tiles + tile // per_tile, :, lanes])
        back = [pltpu.roll(x, LANES - 1, axis=1) for x in row]
        for tile in range(count):
            place(near, tilt, tile, row[tile])
            further = jnp.where(last, back[(tile + 1) % count], back[tile])
            place(slope_near, tilt, tile, further - row[tile])

    def weights(tilt, level):
        numer = level * slope_ref[tilt]
        whole = jnp.floor_divide(numer, depth)
        return whole, (numer - whole * depth).astype(jnp.float32) / depth

    @pl.loop(0, depth)
    def _(level):
        total = None
        for tilt in range(tilts):
            whole, frac = weights(tilt, level)
            term = moved(near, slope_near, frac, tilt, whole, margin, count)
            total = term if total is None else total + term
        total = total / tilts
        row = []
        for tile in range(count):
            lanes = slice(tile * LANES, (tile + 1) * LANES)
            value = volume[level, :, lanes] + total[tile * SUBLANES : (tile + 1) * SUBLANES]
            fresh[level, :, lanes] = value
            row.append(value)
        ahead = [pltpu.roll(x, 1, axis=1) for x in row]
        for tile in range(count):
            place(cells, level, tile, row[tile])
            further = jnp.where(first, ahead[tile - 1], ahead[tile])
            place(slope_cells, level, tile, further - row[tile])

    for tilt in range(tilts):
        def add_level(level, total):
            whole, frac = weights(tilt, level)
            return total + moved(cells, slope_cells, frac, level, -whole, margin, count)

        total = lax.fori_loop(
            0, depth, add_level, jnp.zeros((count * SUBLANES, LANES), jnp.float32)
        )
        for tile in range(count):
            lanes = slice(tile % per_tile * LANES, (tile % per_tile + 1) * LANES)
            parts[tilt * tiles + tile // per_tile, :, lanes] = total[
                tile * SUBLANES : (tile + 1) * SUBLANES
            ]


def volume_phase(slope, pieces, volume):
    depth, band, columns = volume.shape
    tilts = slope.shape[0]
    width = pieces.shape[2]
    margin = width // LANES + 1
    count = columns // LANES + 2 * margin
    near = pltpu.VMEM((tilts, count, SUBLANES, LANES), jnp.float32)
    cells = pltpu.VMEM((depth, count, SUBLANES, LANES), jnp.float32)

    def rows(shape):
        return pl.BlockSpec((shape[0], SUBLANES, shape[2]), lambda i: (0, i, 0))

    return pl.pallas_call(
        volume_kernel,
        grid=(band // SUBLANES,),
        out_shape=(
            jax.ShapeDtypeStruct(volume.shape, jnp.float32),
            jax.ShapeDtypeStruct(pieces.shape, jnp.float32),
        ),
        in_specs=[SMEM, rows(pieces.shape), rows(volume.shape)],
        out_specs=(rows(volume.shape), rows(pieces.shape)),
        scratch_shapes=[near, near, cells, cells],
        compiler_params=pltpu.CompilerParams(vmem_limit_bytes=VMEM_BYTES),
        cost_estimate=pl.CostEstimate(
            flops=8 * tilts * volume.size, bytes_accessed=8 * volume.size, transcendentals=0
        ),
        name="volume",
    )(slope, pieces, volume)


def local(
    obj_re, obj_im, probe_re, probe_im, intensity, positions, counts, row_shift, slope, volume
):
    tile_re = obj_re[0]
    tile_im = obj_im[0]
    height, width = tile_re.shape
    margin = LANES
    edge_re = passed_along(tile_re[:, :margin], "tile", -1)
    edge_im = passed_along(tile_im[:, :margin], "tile", -1)
    grad, spill, _ = probe_phase(
        counts, positions[0], row_shift, tile_re, tile_im, edge_re, edge_im,
        probe_re, probe_im, intensity[0],
    )
    spill = passed_along(spill, "tile", 1)
    grad = grad.at[:, 0, :, :margin].add(spill)
    residual = tile_re * grad[1, 0] - tile_im * grad[0, 0]
    routed = jnp.roll(residual, row_shift[0], axis=0)
    axes = ("tilt", "tile")
    devices = lax.axis_size("tilt") * lax.axis_size("tile")
    routed = routed.reshape(devices, height // devices, width)
    pieces = lax.all_to_all(routed, axes, split_axis=0, concat_axis=0, tiled=True)
    fresh, parts = volume_phase(slope, pieces, volume)
    returned = lax.all_to_all(parts, axes, split_axis=0, concat_axis=0, tiled=True)
    reprojection = jnp.roll(returned.reshape(height, width), -row_shift[0], axis=0)[None]
    return (fresh, reprojection, grad)


def solution(mesh):
    placed = (
        P("tilt", None, "tile"),
        P("tilt", None, "tile"),
        P(),
        P(),
        P("tilt", "tile", None, None),
        P("tilt", "tile", None),
        P("tilt", "tile"),
        P("tilt"),
        P(),
        P(None, ("tilt", "tile"), None),
    )
    return jax.shard_map(
        local,
        mesh=mesh,
        in_specs=placed,
        out_specs=(
            P(None, ("tilt", "tile"), None),
            P("tilt", None, "tile"),
            P(None, "tilt", None, "tile"),
        ),
        check_vma=False,
    )
```

profile of v0, /device:TPU:0, one launch (start us, length us, event | category | flops | bytes accessed | tf_op | source)
XLA Modules:
  0.0 220.3 jit_solution(6411845575406097486)
XLA Ops:
  0.6 0.0 copy-start.2
  0.6 1.1 slice.49
  1.7 1.3 collective-permute-start.1
  3.0 1.1 slice.48
  4.1 1.3 collective-permute-start
  6.7 0.0 copy-done.2
  6.7 0.7 copy.15.positions_ref
  7.4 12.0 %collective-permute-done.1.edge_im = f32[1024,128]{1,0:T(8,128)S(1)} collective-permute-done((f32[1024,128]{1,0:T(8,128)S(1)}, f32[1024,128]{1,0:T(8,128)S(1)}, u32[]{:S(2)}, u32[]{:S(2)}) %collective-permute-start.1) | collective-permute-done | bytes 524320 | tf_op jit(solution)/shard_map/ppermute | solution.py:25
  19.3 0.0 copy-start.3
  19.3 10.4 %collective-permute-done.edge_re = f32[1024,128]{1,0:T(8,128)S(1)} collective-permute-done((f32[1024,128]{1,0:T(8,128)S(1)}, f32[1024,128]{1,0:T(8,128)S(1)}, u32[]{:S(2)}, u32[]{:S(2)}) %collective-permute-start) | collective-permute-done | bytes 524320 | tf_op jit(solution)/shard_map/ppermute | solution.py:25
  29.8 0.0 copy-start.4
  29.8 0.0 copy-done.3
  29.8 0.8 copy-done.4
  30.5 8.2 %probes.1 = (f32[2,1,1024,384]{3,2,1,0:T(8,128)}, f32[2,1024,128]{2,1,0:T(8,128)}, f32[8,128]{1,0:T(8,128)}) custom-call(s32[1,1]{1,0:T(1,128)S(6)} %copy.17.used_ref, s32[8,2]{1,0:T(8,128)} %copy.15.positions_ref, s32[1]{0:T(128)} %copy.18.shift_ref, f32[1024,384]{1,0:T(8,128)} %bitcast.34, f32[1024,384]{1,0:T(8,128)} %bitcast.36, f32[1024,128]{1,0:T(8,128)} %copy-done.4, ...), custom_call_target="tpu_custom_call" | custom-call | flops 6979321856 | bytes 6291456 | tf_op jit(solution)/shard_map/probes/pallas_call | solution.py:254
  38.7 8.6 %collective-permute-start.2 = (f32[2,1024,128]{2,1,0:T(8,128)}, f32[2,1024,128]{2,1,0:T(8,128)S(1)}, u32[]{:S(2)}, u32[]{:S(2)}) collective-permute-start(f32[2,1024,128]{2,1,0:T(8,128)} %get-tuple-element.21), channel_id=1, source_target_pairs={{0,1},{1,2},{2,3},{3,4},{4,5},{5,6},{6,7},{8,9},{9,10},{10,11},{11... | collective-permute-start | bytes 3145736 | tf_op jit(solution)/shard_map/ppermute | solution.py:25
  47.4 21.7 %collective-permute-done.2 = f32[2,1024,128]{2,1,0:T(8,128)S(1)} collective-permute-done((f32[2,1024,128]{2,1,0:T(8,128)}, f32[2,1024,128]{2,1,0:T(8,128)S(1)}, u32[]{:S(2)}, u32[]{:S(2)}) %collective-permute-start.2) | collective-permute-done | bytes 1048608 | tf_op jit(solution)/shard_map/ppermute | solution.py:25
  69.1 0.0 copy-start
  69.1 0.0 copy-start.1
  69.1 2.4 %fusion.6 = f32[2,1,1024,384]{3,2,1,0:T(8,128)} fusion(f32[2,1,1024,384]{3,2,1,0:T(8,128)} %get-tuple-element.20, f32[2,1024,128]{2,1,0:T(8,128)S(1)} %collective-permute-done.2), kind=kLoop, calls=%fused_computation.13 | loop fusion | flops 262144 | bytes 3145728 | tf_op jit(solution)/shard_map/scatter-add | solution.py:406
  71.6 0.0 copy-done
  71.6 0.0 copy-done.1
  71.6 2.3 %fusion.4 = f32[1024,384]{1,0:T(8,128)S(1)} fusion(f32[2,1,1024,384]{3,2,1,0:T(8,128)} %fusion.6, f32[1,1024,384]{2,1,0:T(8,128)S(1)} %copy-done.1, f32[1,1024,384]{2,1,0:T(8,128)S(1)} %copy-done), kind=kLoop, calls=%fused_computation.9 | loop fusion | flops 1179648 | bytes 7864320 | tf_op jit(solution)/shard_map/sub | solution.py:407
  73.9 0.8 fusion.2
  74.8 53.5 %all_to_all.10.pieces = f32[32,32,384]{2,1,0:T(8,128)} all-to-all(f32[32,32,384]{2,1,0:T(8,128)S(1)} %bitcast.32), channel_id=1, replica_groups=mesh['tilt'=4,'tile'=8] {'tilt','tile'}, dimensions={0} | all-to-all | bytes 3145728 | tf_op jit(solution)/shard_map/all_to_all | solution.py:412
  128.3 48.6 %volume.2 = (f32[16,32,3072]{2,1,0:T(8,128)}, f32[32,32,384]{2,1,0:T(8,128)}) custom-call(s32[4]{0:T(128)} %slope_ref.1, f32[32,32,384]{2,1,0:T(8,128)} %all_to_all.10.pieces, f32[16,32,3072]{2,1,0:T(8,128)} %volume.3), custom_call_target="tpu_custom_call" | custom-call | flops 50331648 | bytes 12582912 | tf_op jit(solution)/shard_map/volume/pallas_call | solution.py:374
  176.8 2.7 %all-to-all-start.1 = ((f32[32,32,384]{2,1,0:T(8,128)}), f32[32,32,384]{2,1,0:T(8,128)S(1)}, u32[]{:S(2)}, u32[]{:S(2)}) async-start(f32[32,32,384]{2,1,0:T(8,128)} %get-tuple-element.23), calls=%async_computation.1 | async-start | bytes 3145728 | tf_op jit(solution)/shard_map/all_to_all | solution.py:414
  179.6 38.8 %all-to-all-done.1 = f32[32,32,384]{2,1,0:T(8,128)S(1)} async-done(((f32[32,32,384]{2,1,0:T(8,128)}), f32[32,32,384]{2,1,0:T(8,128)S(1)}, u32[]{:S(2)}, u32[]{:S(2)}) %all-to-all-start.1) | async-done | bytes 1572896 | tf_op jit(solution)/shard_map/all_to_all | solution.py:414
  218.4 2.0 fusion.1
Async XLA Ops:
  0.6 6.1 %copy-start.2 = (s32[1,8,2]{1,2,0:T(2,128)S(1)}, s32[1,8,2]{1,2,0:T(2,128)}, u32[]{:S(2)}) copy-start(s32[1,8,2]{1,2,0:T(2,128)} %param.21) | copy-start | bytes 196
  1.7 17.6 %collective-permute-start.1 = (f32[1024,128]{1,0:T(8,128)S(1)}, f32[1024,128]{1,0:T(8,128)S(1)}, u32[]{:S(2)}, u32[]{:S(2)}) collective-permute-start(f32[1024,128]{1,0:T(8,128)S(1)} %slice.49), channel_id=1, source_target_pairs={{1,0},{2,1},{3,2},{4,3},{5,4},{6,5},{7,6},{9,8},{10,9},{11,10},{12... | collective-permute-start | bytes 1572872 | tf_op jit(solution)/shard_map/ppermute | solution.py:25
  4.1 25.6 %collective-permute-start = (f32[1024,128]{1,0:T(8,128)S(1)}, f32[1024,128]{1,0:T(8,128)S(1)}, u32[]{:S(2)}, u32[]{:S(2)}) collective-permute-start(f32[1024,128]{1,0:T(8,128)S(1)} %slice.48), channel_id=1, source_target_pairs={{1,0},{2,1},{3,2},{4,3},{5,4},{6,5},{7,6},{9,8},{10,9},{11,10},{12... | collective-permute-start | bytes 1572872 | tf_op jit(solution)/shard_map/ppermute | solution.py:25
  19.3 10.4 %copy-start.3 = (f32[1024,128]{1,0:T(8,128)}, f32[1024,128]{1,0:T(8,128)S(1)}, u32[]{:S(2)}) copy-start(f32[1024,128]{1,0:T(8,128)S(1)} %collective-permute-done.1.edge_im) | copy-start | bytes 1572868
  29.8 0.8 copy-start.4
  38.7 30.4 %collective-permute-start.2 = (f32[2,1024,128]{2,1,0:T(8,128)}, f32[2,1024,128]{2,1,0:T(8,128)S(1)}, u32[]{:S(2)}, u32[]{:S(2)}) collective-permute-start(f32[2,1024,128]{2,1,0:T(8,128)} %get-tuple-element.21), channel_id=1, source_target_pairs={{0,1},{1,2},{2,3},{3,4},{4,5},{5,6},{6,7},{8,9},{9,10},{10,11},{11... | collective-permute-start | bytes 3145736 | tf_op jit(solution)/shard_map/ppermute | solution.py:25
  69.1 2.5 %copy-start = (f32[1,1024,384]{2,1,0:T(8,128)S(1)}, f32[1,1024,384]{2,1,0:T(8,128)}, u32[]{:S(2)}) copy-start(f32[1,1024,384]{2,1,0:T(8,128)} %param.16) | copy-start | bytes 4718596
  69.1 2.5 %copy-start.1 = (f32[1,1024,384]{2,1,0:T(8,128)S(1)}, f32[1,1024,384]{2,1,0:T(8,128)}, u32[]{:S(2)}) copy-start(f32[1,1024,384]{2,1,0:T(8,128)} %param.17) | copy-start | bytes 4718596
  176.8 41.5 %all-to-all-start.1 = ((f32[32,32,384]{2,1,0:T(8,128)}), f32[32,32,384]{2,1,0:T(8,128)S(1)}, u32[]{:S(2)}, u32[]{:S(2)}) async-start(f32[32,32,384]{2,1,0:T(8,128)} %get-tuple-element.23), calls=%async_computation.1 | async-start | bytes 3145728 | tf_op jit(solution)/shard_map/all_to_all | solution.py:414
where the time goes:
time: 217 us; the launch traced here: 220 us
  waiting for transfers between devices  82.9 us (38%)
  Pallas kernels  56.7 us (26%)
  blocking collectives  53.5 us (25%)
  starting transfers between devices  13.9 us (6%)
  other arithmetic  7.61 us (4%)
  local copies, waits for them, and re-layouts  3.64 us (2%)
    all_to_all x1, blocking collectives, local(): lax.all_to_all(routed, axes, split_axis=0, concat_axis=0, tiled=True)  53.5 us
    pallas_call x1, Pallas kernels, volume_phase(): pl.pallas_call(volume_kernel, grid=(band // SUBLANES,), out_shape=(jax.Sh...  48.6 us
    ppermute x3, waiting for transfers between devices, passed_along(): return lax.ppermute(block, axis, route)  44.1 us
    all_to_all x1, waiting for transfers between devices, local(): lax.all_to_all(parts, axes, split_axis=0, concat_axis=0, tiled=True)  38.8 us
    ppermute x3, starting transfers between devices, passed_along(): return lax.ppermute(block, axis, route)  11.2 us
    pallas_call x1, Pallas kernels, probe_phase(): pl.pallas_call(probe_kernel, out_shape=(jax.ShapeDtypeStruct((2, 1, heigh...  8.17 us
  transfers between devices with their start and end apart: 4, of which 4 were waited for; matrix products, arithmetic and copies ran while one was open for 1% of the time, Pallas kernels for 0%

commit v1 on v0

v1 whole, which is shorter than its diff:
```python
import functools
import math

import jax
import jax.numpy as jnp
import ml_dtypes
import numpy as np
from jax import lax
from jax.experimental import pallas as pl
from jax.experimental.pallas import tpu as pltpu
from jax.sharding import PartitionSpec as P

LANES = 128
SUBLANES = 8
VMEM_BYTES = 60 * 1024 * 1024
SPLIT = jnp.bfloat16
ANY = pl.BlockSpec(memory_space=pl.ANY)
HBM = pl.BlockSpec(memory_space=pltpu.HBM)
SMEM = pl.BlockSpec(memory_space=pltpu.SMEM)
VMEM = pl.BlockSpec(memory_space=pltpu.VMEM)


def passed_along(block, axis, distance):
    devices = range(lax.axis_size(axis))
    route = [(i - distance, i) for i in devices if i - distance in devices]
    return lax.ppermute(block, axis, route)


def halves(table):
    high = table.astype(ml_dtypes.bfloat16)
    low = (table - high.astype(np.float64)).astype(ml_dtypes.bfloat16)
    return high, low


def dft_tables(length):
    half = length // 2
    index = np.arange(length)
    angle = (index[:, None] * index[None, :] % length) * (-2.0 * math.pi / length)
    wave = (np.cos(angle) + 1j * np.sin(angle)) / math.sqrt(length)
    tables = []
    for parity in (0, 1):
        part = wave[parity::2, :half]
        pair = np.block([[part.real, -part.imag], [part.imag, part.real]])
        tables += [*halves(pair), *halves(pair.T)]
    order = np.concatenate([index[0::2], index[1::2]])
    spread = np.zeros((length, length))
    spread[order, index] = 1.0
    return np.stack(tables), spread.astype(ml_dtypes.bfloat16)


def split(x):
    high = x.astype(SPLIT)
    return high, (x - high.astype(jnp.float32)).astype(SPLIT)


def dot(a, b):
    return jnp.dot(a, b, preferred_element_type=jnp.float32)


def dot3(ah, al, bh, bl):
    return dot(ah, bh) + dot(ah, bl) + dot(al, bh)


def lanes_of(shape):
    return lax.broadcasted_iota(jnp.int32, shape, len(shape) - 1)


def rows_of(shape):
    return lax.broadcasted_iota(jnp.int32, shape, len(shape) - 2)


def rolled(x, row, lane):
    size = x.shape[0]
    tiles = x.shape[1] // LANES
    cut = []
    for tile in range(tiles):
        part = x[:, tile * LANES : (tile + 1) * LANES].reshape(-1, SUBLANES, LANES)
        turned = pltpu.roll(part, row, axis=1)
        before = jnp.concatenate([turned[-1:], turned[:-1]], axis=0)
        part = jnp.where(rows_of(part.shape) < row, before, turned).reshape(size, LANES)
        cut.append(pltpu.roll(part, lane, axis=1))
    keep = lanes_of(cut[0].shape) >= lane
    return [jnp.where(keep, cut[tile], cut[tile - 1]) for tile in range(tiles)]


def probe_kernel(
    used_ref, positions_ref, shift_ref,
    *refs, base, beyond,
):
    if beyond:
        (tile_re, tile_im, edge_re, edge_im, begun, routed_left, probe_re, probe_im, intensity,
         tables, spread, grad_ref, early_ref, late_ref, routed_ref, *scratch) = refs
    else:
        (tile_re, tile_im, probe_re, probe_im, intensity, tables, spread,
         grad_ref, begun_ref, routed_ref, *scratch) = refs
    ext, acc, measured, turned, uh, ul, vh, vl, residual, routed, sems, slot_sems = scratch
    height = ext.shape[2]
    tiles = ext.shape[1]
    size = probe_re.shape[0]
    half = size // 2
    used = used_ref[0, 0]
    copies, late = [], []
    for part, tile in enumerate((tile_re, tile_im)):
        for column in range(tiles):
            if beyond and column == tiles - 1:
                source = (edge_re, edge_im)[part]
            else:
                source = tile.at[:, pl.ds(base + column * LANES, LANES)]
            sem = sems.at[0, part * tiles + column]
            copies.append(pltpu.make_async_copy(source, ext.at[part, column], sem))
            if beyond and column < tiles - 1:
                sem = sems.at[1, part * tiles + column]
                late.append(pltpu.make_async_copy(begun.at[part, column], acc.at[part, column], sem))
    if beyond:
        late.append(
            pltpu.make_async_copy(routed_left, routed.at[:, pl.ds(0, LANES)], sems.at[1, tiles - 1])
        )
    for copy in copies + late:
        copy.start()

    def fetch(slot):
        return [
            pltpu.make_async_copy(
                intensity.at[slot, :, pl.ds(tile * LANES, LANES)],
                measured.at[slot, tile],
                slot_sems.at[slot, tile],
            )
            for tile in range(2)
        ]

    def mine(slot):
        past = positions_ref[slot, 1] + size > base + tiles * LANES
        return past if not beyond else positions_ref[slot, 1] + size > base + (tiles - 1) * LANES

    def live(slot):
        return mine(slot) if beyond else jnp.logical_not(mine(slot))

    slots = measured.shape[0]
    for slot in range(slots):
        @pl.when(jnp.logical_and(slot < used, live(slot)))
        def _():
            for copy in fetch(slot):
                copy.start()

    first_fresh = tiles - 1 if beyond else 0

    @pl.loop(0, height // size)
    def _(chunk):
        rows = pl.ds(chunk * size, size)
        for part in range(2):
            for column in range(first_fresh, tiles):
                acc[part, column, rows, :] = jnp.zeros((size, LANES), jnp.float32)

    for copy in copies + late:
        copy.wait()

    le, let, lo, lot = 0, 2, 4, 6

    def table(which):
        return tables[which], tables[which + 1]

    def visit(slot):
        row = positions_ref[slot, 0]
        col = positions_ref[slot, 1] - base
        first = pl.multiple_of(row // SUBLANES * SUBLANES, SUBLANES)
        row_rest = row - first
        wrap = pl.multiple_of(jnp.minimum(first + size, height - SUBLANES), SUBLANES)
        column = col // LANES
        lane_rest = col - column * LANES
        wrap_column = jnp.minimum(column + 2, tiles - 1)
        body = pl.ds(first, size)
        tail = pl.ds(wrap, SUBLANES)
        low_rows = rows_of((SUBLANES, LANES)) < row_rest
        low_lanes = lanes_of((size, LANES)) < lane_rest

        for part, probe in enumerate((probe_re, probe_im)):
            for tile, piece in enumerate(rolled(probe[...], row_rest, lane_rest)):
                turned[part, tile] = piece

        def window(part, at):
            block = ext[part, at, body, :]
            top = jnp.where(low_rows, ext[part, at, tail, :], block[:SUBLANES])
            return jnp.concatenate([top, block[SUBLANES:]], axis=0)

        psi = []
        for tile in range(2):
            if tile == 0:
                o_re, o_im = (
                    jnp.where(low_lanes, window(part, wrap_column), window(part, column))
                    for part in range(2)
                )
            else:
                o_re, o_im = (window(part, column + 1) for part in range(2))
            p_re, p_im = turned[0, tile], turned[1, tile]
            psi.append((p_re * o_re - p_im * o_im, p_re * o_im + p_im * o_re))
        for part in range(2):
            lanes = slice(part * LANES, (part + 1) * LANES)
            uh[:, lanes], ul[:, lanes] = split(psi[0][part] + psi[1][part])
            vh[:, lanes], vl[:, lanes] = split(psi[0][part] - psi[1][part])
        even = dot3(uh[...], ul[...], *table(let))
        odd = dot3(vh[...], vl[...], *table(lot))
        for part in range(2):
            rows = slice(part * half, (part + 1) * half)
            for tile, y in enumerate((even, odd)):
                lanes = slice(tile * LANES, (tile + 1) * LANES)
                y = y[:, part * LANES : (part + 1) * LANES]
                uh[rows, lanes], ul[rows, lanes] = split(y[:half] + y[half:])
                vh[rows, lanes], vl[rows, lanes] = split(y[:half] - y[half:])
        for copy in fetch(slot):
            copy.wait()
        for parity, (h, l, which) in enumerate(((uh, ul, le), (vh, vl, lo))):
            th, tl = table(which)
            far = dot(th, h[...]) + dot(tl, h[...]) + dot(th, l[...])
            f_re, f_im = far[:half], far[half:]
            m = [measured[slot, tile, pl.ds(parity, half, stride=2), :] for tile in range(2)]
            mh, ml = split(jnp.concatenate(m, axis=1))
            excess = f_re * f_re + f_im * f_im - (dot(mh, spread[...]) + dot(ml, spread[...]))
            h[:half, :], l[:half, :] = split(excess * f_re)
            h[half:, :], l[half:, :] = split(excess * f_im)
        th, tl = table(let)
        even = dot(th, uh[...]) + dot(tl, uh[...]) + dot(th, ul[...])
        th, tl = table(lot)
        odd = dot(th, vh[...]) + dot(tl, vh[...]) + dot(th, vl[...])
        for part in range(2):
            rows = slice(part * half, (part + 1) * half)
            lanes = slice(part * LANES, (part + 1) * LANES)
            for sign in range(2):
                out = slice(sign * half, (sign + 1) * half)
                t = even[rows] + odd[rows] if sign == 0 else even[rows] - odd[rows]
                uh[out, lanes], ul[out, lanes] = split(t[:, :LANES])
                vh[out, lanes], vl[out, lanes] = split(t[:, LANES:])
        even = dot3(uh[...], ul[...], *table(le))
        odd = dot3(vh[...], vl[...], *table(lo))
        for tile in range(2):
            chi = even + odd if tile == 0 else even - odd
            c_re, c_im = chi[:, :LANES], chi[:, LANES:]
            p_re, p_im = turned[0, tile], turned[1, tile]
            for part, g in enumerate((p_re * c_re + p_im * c_im, p_re * c_im - p_im * c_re)):
                if tile == 0:
                    places = (
                        (column, jnp.where(low_lanes, 0.0, g)),
                        (wrap_column, jnp.where(low_lanes, g, 0.0)),
                    )
                else:
                    places = ((column + 1, g),)
                for at, value in places:
                    top = value[:SUBLANES]
                    kept = jnp.where(low_rows, 0.0, top)
                    acc[part, at, body, :] += jnp.concatenate([kept, value[SUBLANES:]], axis=0)
                    acc[part, at, tail, :] += jnp.where(low_rows, top, 0.0)

    @pl.loop(0, used)
    def _(slot):
        @pl.when(live(slot))
        def _():
            visit(slot)

    outs = []
    if beyond:
        for part in range(2):
            for column in range(tiles - 1):
                target = grad_ref.at[part, :, pl.ds(column * LANES, LANES)]
                outs.append((acc.at[part, column], target))
            rows = early_ref.shape[1]
            outs.append((acc.at[part, tiles - 1, pl.ds(0, rows)], early_ref.at[part]))
            outs.append((acc.at[part, tiles - 1, pl.ds(rows, height - rows)], late_ref.at[part]))
        routing = range(tiles)
    else:
        for part in range(2):
            outs.append((acc.at[part, 0], grad_ref.at[part]))
            for column in range(1, tiles):
                outs.append((acc.at[part, column], begun_ref.at[part, column - 1]))
        routing = range(1)
    outs = [pltpu.make_async_copy(*pair, sems.at[0, n]) for n, pair in enumerate(outs)]
    for copy in outs:
        copy.start()

    @pl.loop(0, height // size)
    def _(chunk):
        rows = pl.ds(chunk * size, size)
        for column in routing:
            value = ext[0, column, rows, :] * acc[1, column, rows, :] - (
                ext[1, column, rows, :] * acc[0, column, rows, :]
            )
            residual[column, rows, :] = value
            residual[column, pl.ds(height + chunk * size, size), :] = value

    shift = shift_ref[0]

    ahead = 1 if beyond else 0
    for chunk in range(height // size):
        rows = pl.ds(chunk * size, size)
        for column in routing:
            lanes = slice((column + ahead) * LANES, (column + ahead + 1) * LANES)
            routed[rows, lanes] = residual[column, pl.ds(height - shift + chunk * size, size), :]
        copy = pltpu.make_async_copy(routed.at[rows], routed_ref.at[rows], slot_sems.at[chunk, 0])
        copy.start()
        outs.append(copy)
    for copy in outs:
        copy.wait()


def probe_phase(used, positions, shift, tile, edge, begun, probe, intensity):
    height, width = tile[0].shape
    size = probe[0].shape[0]
    slots = intensity.shape[0]
    columns = width // LANES
    beyond = edge is not None
    tables, spread = dft_tables(size)
    plane = pltpu.VMEM((size, size), SPLIT)
    planes = pltpu.VMEM((2, columns, height, LANES), jnp.float32)
    routing = columns if beyond else 1

    def out(*shape):
        return jax.ShapeDtypeStruct(shape, jnp.float32)

    if beyond:
        operands = (*tile, *edge, *begun)
        early = height * 5 // 8 // SUBLANES * SUBLANES
        spills = (out(2, early, LANES), out(2, height - early, LANES))
        outs = (out(2, height, width - LANES), *spills, out(height, width + LANES))
        base = LANES
    else:
        operands = tile
        outs = (out(2, height, LANES), out(2, columns - 1, height, LANES), out(height, LANES))
        base = 0
    return pl.pallas_call(
        functools.partial(probe_kernel, base=base, beyond=beyond),
        out_shape=outs,
        in_specs=[SMEM, SMEM, SMEM, *[ANY] * len(operands), VMEM, VMEM, ANY, VMEM, VMEM],
        out_specs=(HBM,) * len(outs),
        scratch_shapes=[
            planes, planes,
            pltpu.VMEM((slots, 2, size, LANES), jnp.float32),
            pltpu.VMEM((2, 2, size, LANES), jnp.float32),
            plane, plane, plane, plane,
            pltpu.VMEM((routing, 2 * height, LANES), jnp.float32),
            pltpu.VMEM((height, outs[-1].shape[1]), jnp.float32),
            pltpu.SemaphoreType.DMA((2, 2 * columns + 2)),
            pltpu.SemaphoreType.DMA((max(slots, height // size), 2)),
        ],
        compiler_params=pltpu.CompilerParams(
            vmem_limit_bytes=VMEM_BYTES * 3 // 4 if beyond else VMEM_BYTES
        ),
        cost_estimate=pl.CostEstimate(
            flops=26 * slots * size**3, bytes_accessed=16 * height * width, transcendentals=0
        ),
        name="probes_beyond" if beyond else "probes_within",
    )(used, positions, shift, *operands, *probe, intensity, jnp.asarray(tables), jnp.asarray(spread))


def shift_tables(slope, depth):
    numer = jnp.arange(depth, dtype=jnp.int32)[None, :] * slope[:, None]
    whole = jnp.floor_divide(numer, depth)
    return whole, (numer - whole * depth).astype(jnp.float32) / depth


class Turned:
    def __init__(self, band, columns, margin):
        self.band = band
        self.segments = LANES // band
        self.length = columns // self.segments
        self.blocks = self.length // LANES
        self.margin = margin
        self.rows = self.length + 2 * margin

    def scratch(self, count):
        return pltpu.VMEM((count, self.rows, LANES), jnp.float32)

    def store(self, ref, lead, at, value):
        rows = value.shape[0]
        ref[lead, pl.ds(self.margin + at, rows), :] = value
        if at < self.margin:
            ref[lead, pl.ds(self.margin + self.length + at, rows), :] = pltpu.roll(
                value, LANES - self.band, axis=1
            )
        if at >= self.length - self.margin:
            ref[lead, pl.ds(at - self.length + self.margin, rows), :] = pltpu.roll(
                value, self.band, axis=1
            )

    def project(self, whole, frac, ref, tilt, at, rows):
        depth = ref.shape[0]

        def add_level(level, total):
            start = self.margin + at - whole[tilt, level]
            far = frac[tilt, level]
            return (
                total
                + (1.0 - far) * ref[level, pl.ds(start, rows), :]
                + far * ref[level, pl.ds(start - 1, rows), :]
            )

        zero = jnp.zeros((rows, LANES), jnp.float32)
        return lax.fori_loop(0, depth, add_level, zero, unroll=4)


def old_kernel(turned, whole, frac, volume, old, cells):
    depth = volume.shape[0]

    @pl.loop(0, depth)
    def _(level):
        for block in range(turned.blocks):
            cut = []
            for segment in range(turned.segments):
                start = segment * turned.length + block * LANES
                cut.append(volume[level, :, start : start + LANES])
            turned.store(cells, level, block * LANES, jnp.concatenate(cut, axis=0).T)

    @pl.loop(0, whole.shape[0])
    def _(tilt):
        for block in range(turned.blocks):
            at = block * LANES
            old[tilt, at : at + LANES, :] = turned.project(whole, frac, cells, tilt, at, LANES)


def step_kernel(
    turned, whole, frac, pieces, old, parts, update, near, cells, before, after, sems
):
    old_copy = pltpu.make_async_copy(old, before, sems.at[0])
    old_copy.start()
    depth = cells.shape[0]
    tilts = near.shape[0]
    tiles = pieces.shape[0] // tilts
    own = pieces.shape[2] // LANES - 1
    band = turned.band

    def place(block, segment):
        return divmod(segment * turned.blocks + block, own)

    @pl.loop(0, tilts)
    def _(tilt):
        for block in range(turned.blocks):
            cut = []
            for segment in range(turned.segments):
                tile, column = place(block, segment)
                source = tilt * tiles + tile
                value = pieces[source, :, column * LANES : (column + 1) * LANES]
                if column == 0 and tile > 0:
                    value = value + pieces[source - 1, :, own * LANES :]
                cut.append(value)
            turned.store(near, tilt, block * LANES, jnp.concatenate(cut, axis=0).T)

    rows = LANES // 2

    @pl.loop(0, depth)
    def _(level):
        for at in range(0, turned.length, rows):
            total = None
            for tilt in range(tilts):
                start = turned.margin + at + whole[tilt, level]
                far = frac[tilt, level] / tilts
                term = (1.0 / tilts - far) * near[tilt, pl.ds(start, rows), :] + (
                    far * near[tilt, pl.ds(start + 1, rows), :]
                )
                total = term if total is None else total + term
            turned.store(cells, level, at, total)

    main = cells.at[:, pl.ds(turned.margin, turned.length), :]
    update_copy = pltpu.make_async_copy(main, update, sems.at[1])
    update_copy.start()
    old_copy.wait()

    def send(tilt):
        block = pl.ds(tilt * tiles, tiles)
        return pltpu.make_async_copy(after.at[block], parts.at[block], sems.at[2 + tilt])

    @pl.loop(0, tilts)
    def _(tilt):
        for block in range(turned.blocks):
            at = block * LANES
            total = turned.project(whole, frac, cells, tilt, at, LANES)
            total = (total + before[tilt, at : at + LANES, :]).T
            for segment in range(turned.segments):
                tile, column = place(block, segment)
                after[tilt * tiles + tile, :, column * LANES : (column + 1) * LANES] = total[
                    segment * band : (segment + 1) * band
                ]

        send(tilt).start()

    for tilt in range(tilts):
        send(tilt).wait()
    update_copy.wait()


def fresh_kernel(turned, volume, update, fresh):
    for block in range(turned.blocks):
        value = update[0, block * LANES : (block + 1) * LANES, :].T
        for segment in range(turned.segments):
            start = segment * turned.length + block * LANES
            lanes = slice(start, start + LANES)
            rows = slice(segment * turned.band, (segment + 1) * turned.band)
            fresh[0, :, lanes] = volume[0, :, lanes] + value[rows]


def kernel_options(flops, size, share=1):
    return dict(
        compiler_params=pltpu.CompilerParams(vmem_limit_bytes=int(VMEM_BYTES * share)),
        cost_estimate=pl.CostEstimate(flops=flops, bytes_accessed=size, transcendentals=0),
    )


def old_projection(turned, whole, frac, volume):
    tilts = whole.shape[0]
    return pl.pallas_call(
        functools.partial(old_kernel, turned),
        out_shape=jax.ShapeDtypeStruct((tilts, turned.length, LANES), jnp.float32),
        in_specs=[SMEM, SMEM, VMEM],
        out_specs=VMEM,
        scratch_shapes=[turned.scratch(volume.shape[0])],
        name="old_projection",
        **kernel_options(8 * tilts * volume.size, 4 * volume.size),
    )(whole, frac, volume)


def volume_step(turned, whole, frac, pieces, old):
    tilts, depth = whole.shape
    width = pieces.shape[2] - LANES
    return pl.pallas_call(
        functools.partial(step_kernel, turned),
        out_shape=(
            jax.ShapeDtypeStruct((*pieces.shape[:2], width), jnp.float32),
            jax.ShapeDtypeStruct((depth, turned.length, LANES), jnp.float32),
        ),
        in_specs=[SMEM, SMEM, VMEM, HBM],
        out_specs=(HBM, HBM),
        scratch_shapes=[
            turned.scratch(tilts), turned.scratch(depth),
            pltpu.VMEM(old.shape, jnp.float32),
            pltpu.VMEM((*pieces.shape[:2], width), jnp.float32),
            pltpu.SemaphoreType.DMA((2 + tilts,)),
        ],
        name="volume_step",
        **kernel_options(16 * depth * old.size, 4 * depth * turned.length * LANES, 9 / 10),
    )(whole, frac, pieces, old)


def fresh_volume(turned, volume, update):
    depth, band, columns = volume.shape
    cells = pl.BlockSpec((1, band, columns), lambda i: (i, 0, 0))
    flat = pl.BlockSpec((1, turned.length, LANES), lambda i: (i, 0, 0))
    return pl.pallas_call(
        functools.partial(fresh_kernel, turned),
        grid=(depth,),
        out_shape=jax.ShapeDtypeStruct(volume.shape, jnp.float32),
        in_specs=[cells, flat],
        out_specs=cells,
        name="fresh_volume",
        **kernel_options(volume.size, 12 * volume.size),
    )(volume, update)


def local(
    obj_re, obj_im, probe_re, probe_im, intensity, positions, counts, row_shift, slope, volume
):
    tile = (obj_re[0], obj_im[0])
    height, width = tile[0].shape
    depth, band, columns = volume.shape
    axes = ("tilt", "tile")
    devices = lax.axis_size("tilt") * lax.axis_size("tile")
    turned = Turned(band, columns, width)
    whole, frac = shift_tables(slope, depth)
    probe = (probe_re, probe_im)

    edge = [passed_along(part[:, :LANES], "tile", -1) for part in tile]
    within = (counts, positions[0], row_shift)
    grad_left, *begun = probe_phase(*within, tile, None, None, probe, intensity[0])
    grad_right, early, late, routed = probe_phase(*within, tile, edge, begun, probe, intensity[0])
    routed = routed.reshape(devices, band, width + LANES)
    pieces = lax.all_to_all(routed, axes, split_axis=0, concat_axis=0, tiled=True)
    old = old_projection(turned, whole, frac, volume)
    pieces, early = lax.optimization_barrier((pieces, early))
    early = passed_along(early, "tile", 1)
    parts, update = volume_step(turned, whole, frac, pieces, old)
    parts, early, late = lax.optimization_barrier((parts, early, late))
    late = passed_along(late, "tile", 1)
    returned = lax.all_to_all(parts, axes, split_axis=0, concat_axis=0, tiled=True)
    fresh = fresh_volume(turned, volume, update)
    spill = jnp.concatenate([early, late], axis=1)
    grad = jnp.concatenate([grad_left + spill, grad_right], axis=2)[:, None]
    reprojection = jnp.roll(returned.reshape(height, width), -row_shift[0], axis=0)[None]
    return (fresh, reprojection, grad)


def solution(mesh):
    placed = (
        P("tilt", None, "tile"),
        P("tilt", None, "tile"),
        P(),
        P(),
        P("tilt", "tile", None, None),
        P("tilt", "tile", None),
        P("tilt", "tile"),
        P("tilt"),
        P(),
        P(None, ("tilt", "tile"), None),
    )
    return jax.shard_map(
        local,
        mesh=mesh,
        in_specs=placed,
        out_specs=(
            P(None, ("tilt", "tile"), None),
            P("tilt", None, "tile"),
            P(None, "tilt", None, "tile"),
        ),
        check_vma=False,
    )
```

time: 217 us -> 192 us (0.88)
  the two profiles are of different devices: /device:TPU:0 before, /device:TPU:17 now
where the time goes in v1:
time: 192 us; the launch traced here: 193 us
  blocking collectives  61 us (32%)
  Pallas kernels  56 us (29%)
  waiting for transfers between devices  39 us (20%)
  starting transfers between devices  18.6 us (10%)
  local copies, waits for them, and re-layouts  10.4 us (5%)
  other arithmetic  6.34 us (3%)
  between operations  2.16 us (1%)
    all_to_all x1, blocking collectives, local(): lax.all_to_all(routed, axes, split_axis=0, concat_axis=0, tiled=True)  61 us
    ppermute x4, waiting for transfers between devices, passed_along(): return lax.ppermute(block, axis, route)  39 us
    pallas_call x1, Pallas kernels, volume_step(): pl.pallas_call(functools.partial(step_kernel, turned), out_shape=(jax.Sha...  16.5 us
    pallas_call x1, Pallas kernels, old_projection(): pl.pallas_call(functools.partial(old_kernel, turned), out_shape=jax.Shape...  13.6 us
    pallas_call x1, Pallas kernels, fresh_volume(): pl.pallas_call(functools.partial(fresh_kernel, turned), grid=(depth,), ou...  13.3 us
    pallas_call x2, Pallas kernels, probe_phase(): pl.pallas_call(functools.partial(probe_kernel, base=base, beyond=beyond),...  12.6 us
    ppermute x4, starting transfers between devices, passed_along(): return lax.ppermute(block, axis, route)  11.9 us
    all_to_all x1, starting transfers between devices, local(): lax.all_to_all(parts, axes, split_axis=0, concat_axis=0, tiled=True)  6.65 us
  transfers between devices with their start and end apart: 5, of which 3 were waited for; matrix products, arithmetic and copies ran while one was open for 4% of the time, Pallas kernels for 25%

profile of v1, /device:TPU:17, one launch (start us, length us, event | category | flops | bytes accessed | tf_op | source)
XLA Modules:
  0.0 193.4 jit_solution(13687142377961100932)
XLA Ops:
  0.6 0.0 copy-start.15
  0.6 1.9 slice.8
  2.5 3.0 %collective-permute-start = (f32[1024,128]{1,0:T(8,128)}, f32[1024,128]{1,0:T(8,128)S(1)}, u32[]{:S(2)}, u32[]{:S(2)}) collective-permute-start(f32[1024,128]{1,0:T(8,128)} %slice.8), channel_id=1, source_target_pairs={{1,0},{2,1},{3,2},{4,3},{5,4},{6,5},{7,6},{9,8},{10,9},{11,10},{12... | collective-permute-start | bytes 1572872 | tf_op jit(solution)/shard_map/ppermute | solution.py:26
  5.5 1.9 slice.9
  7.4 2.1 %collective-permute-start.1 = (f32[1024,128]{1,0:T(8,128)}, f32[1024,128]{1,0:T(8,128)}, u32[]{:S(2)}, u32[]{:S(2)}) collective-permute-start(f32[1024,128]{1,0:T(8,128)} %slice.9), channel_id=1, source_target_pairs={{1,0},{2,1},{3,2},{4,3},{5,4},{6,5},{7,6},{9,8},{10,9},{11,10},{12... | collective-permute-start | bytes 1572872 | tf_op jit(solution)/shard_map/ppermute | solution.py:26
  10.2 0.0 copy-done.15
  10.2 0.7 copy.18.positions_ref
  11.5 0.0 copy-start
  11.5 0.0 copy-start.1
  11.6 0.0 copy-start.2
  11.6 0.0 copy-start.7
  11.6 5.5 %probes_within.1 = (f32[2,1024,128]{2,1,0:T(8,128)}, f32[2,2,1024,128]{3,2,1,0:T(8,128)}, f32[1024,128]{1,0:T(8,128)}) custom-call(s32[1,1]{1,0:T(1,128)S(6)} %copy.20.used_ref, s32[8,2]{1,0:T(8,128)} %copy.18.positions_ref, s32[1]{0:T(128)} %copy.21.shift_ref, f32[1024,384]{1,0:T(8,128)} %bitcast.16, f32[1024,384]{1,0:T(8,128)} %bitcast.19, ...), custom_call_target="tpu_custom_call" | custom-call | flops 3489660928 | bytes 6291456 | tf_op jit(solution)/shard_map/probes_within/pallas_call | solution.py:327
  17.1 0.3 collective-permute-done.refs_2_
  17.4 0.8 copy-done.3
  18.2 10.5 %collective-permute-done.1.refs_3_ = f32[1024,128]{1,0:T(8,128)} collective-permute-done((f32[1024,128]{1,0:T(8,128)}, f32[1024,128]{1,0:T(8,128)}, u32[]{:S(2)}, u32[]{:S(2)}) %collective-permute-start.1) | collective-permute-done | bytes 524320 | tf_op jit(solution)/shard_map/ppermute | solution.py:26
  28.7 0.0 copy-done
  28.7 0.0 copy-done.1
  28.7 0.0 copy-done.2
  28.7 0.0 copy-done.7
  28.8 0.0 copy-start.4
  28.8 1.0 copy-done.4
  29.8 0.9 copy-done.8
  30.8 1.2 copy-done.9
  32.0 0.9 copy-done.10
  32.9 1.0 copy-done.11
  33.9 7.1 %probes_beyond.1 = (f32[2,1024,256]{2,1,0:T(8,128)}, f32[2,640,128]{2,1,0:T(8,128)S(1)}, f32[2,384,128]{2,1,0:T(8,128)S(1)}, f32[1024,512]{1,0:T(8,128)}) custom-call(s32[1,1]{1,0:T(1,128)S(6)} %copy.20.used_ref, s32[8,2]{1,0:T(8,128)S(1)} %copy-done.2, s32[1]{0:T(128)} %copy.21.shift_ref, f32[1024,384]{1,0:T(8,128)S(1)} %bitcast.17, ...), custom_call_target="tpu_custom_call" | custom-call | flops 3489660928 | bytes 6291456 | tf_op jit(solution)/shard_map/probes_beyond/pallas_call | solution.py:327
  41.0 0.0 copy-start.5
  41.0 0.0 copy-start.14
  41.0 61.0 %all_to_all.10.pieces = f32[32,32,512]{2,1,0:T(8,128)} all-to-all(f32[32,32,512]{2,1,0:T(8,128)} %bitcast.22), channel_id=1, replica_groups=mesh['tilt'=4,'tile'=8] {'tilt','tile'}, dimensions={0} | all-to-all | bytes 4194304 | tf_op jit(solution)/shard_map/all_to_all | solution.py:571
  102.0 0.0 copy-done.5
  102.0 3.6 %collective-permute-start.2 = (f32[2,640,128]{2,1,0:T(8,128)S(1)}, f32[2,640,128]{2,1,0:T(8,128)}, u32[]{:S(2)}, u32[]{:S(2)}) collective-permute-start(f32[2,640,128]{2,1,0:T(8,128)S(1)} %get-tuple-element.24), channel_id=1, source_target_pairs={{0,1},{1,2},{2,3},{3,4},{4,5},{5,6},{6,7},{8,9},{9,10},{10,11},{11... | collective-permute-start | bytes 1966088 | tf_op jit(solution)/shard_map/ppermute | solution.py:26
  105.7 0.0 copy-done.14
  105.7 0.7 add_select_fusion.whole
  106.3 0.7 convert_multiply_fusion.frac
  107.0 13.6 %old_projection.1.old = f32[4,768,128]{2,1,0:T(8,128)} custom-call(s32[4,16]{1,0:T(4,128)} %add_select_fusion.whole, f32[4,16]{1,0:T(4,128)} %convert_multiply_fusion.frac, f32[16,32,3072]{2,1,0:T(8,128)} %volume.3), custom_call_target="tpu_custom_call" | custom-call | flops 50331648 | bytes 6291456 | tf_op jit(solution)/shard_map/old_projection/pallas_call | solution.py:506
  120.6 16.5 %volume_step.1 = (f32[32,32,384]{2,1,0:T(8,128)}, f32[16,768,128]{2,1,0:T(8,128)}) custom-call(s32[4,16]{1,0:T(4,128)} %add_select_fusion.whole, f32[4,16]{1,0:T(4,128)} %convert_multiply_fusion.frac, f32[32,32,512]{2,1,0:T(8,128)} %all_to_all.10.pieces, f32[4,768,128]{2,1,0:T(8,128)} %old_projection.1.old), custom_call_target="tpu_custom_call" | custom-call | flops 100663296 | bytes 6291456 | tf_op jit(solution)/shard_map/volume_step/pallas_call | solution.py:520
  137.1 0.0 copy-start.6
  137.1 0.0 collective-permute-done.2
  137.1 6.7 %all-to-all-start.1 = ((f32[32,32,384]{2,1,0:T(8,128)}), f32[32,32,384]{2,1,0:T(8,128)S(1)}, u32[]{:S(2)}, u32[]{:S(2)}) async-start(f32[32,32,384]{2,1,0:T(8,128)} %get-tuple-element.26), calls=%async_computation.1 | async-start | bytes 3145728 | tf_op jit(solution)/shard_map/all_to_all | solution.py:578
  143.8 0.0 copy-done.6
  143.8 3.1 %collective-permute-start.3 = (f32[2,384,128]{2,1,0:T(8,128)S(1)}, f32[2,384,128]{2,1,0:T(8,128)S(1)}, u32[]{:S(2)}, u32[]{:S(2)}) collective-permute-start(f32[2,384,128]{2,1,0:T(8,128)S(1)} %copy-done.6), channel_id=1, source_target_pairs={{0,1},{1,2},{2,3},{3,4},{4,5},{5,6},{6,7},{8,9},{9,10},{10,11},{11... | collective-permute-start | bytes 1179656 | tf_op jit(solution)/shard_map/ppermute | solution.py:26
  147.0 13.3 %fresh_volume.1 = f32[16,32,3072]{2,1,0:T(8,128)} custom-call(f32[16,32,3072]{2,1,0:T(8,128)} %volume.3, f32[16,768,128]{2,1,0:T(8,128)} %get-tuple-element.22.update), custom_call_target="tpu_custom_call" | custom-call | flops 1572864 | bytes 18874368 | tf_op jit(solution)/shard_map/fresh_volume/pallas_call | solution.py:543
  160.2 28.1 %collective-permute-done.3 = f32[2,384,128]{2,1,0:T(8,128)S(1)} collective-permute-done((f32[2,384,128]{2,1,0:T(8,128)S(1)}, f32[2,384,128]{2,1,0:T(8,128)S(1)}, u32[]{:S(2)}, u32[]{:S(2)}) %collective-permute-start.3) | collective-permute-done | bytes 393248 | tf_op jit(solution)/shard_map/ppermute | solution.py:26
  188.4 0.0 copy-done.13
  188.4 1.2 maximum_add_fusion
  189.6 1.9 maximum_bitcast_fusion
  191.5 0.0 all-to-all-done.1
  191.5 2.0 %fusion.1 = f32[1,1024,384]{2,1,0:T(8,128)} fusion(s32[]{:T(128)S(6)} %select_n.20, f32[1024,384]{1,0:T(8,128)S(1)} %bitcast.21), kind=kLoop, calls=%fused_computation.4 | loop fusion | flops 393216 | bytes 3145732 | tf_op jit(solution)/shard_map/broadcast_in_dim | solution.py:582
  (8 shorter events, 0.0 us)
Async XLA Ops:
  0.6 9.6 %copy-start.15 = (s32[1,8,2]{1,2,0:T(2,128)S(1)}, s32[1,8,2]{1,2,0:T(2,128)}, u32[]{:S(2)}) copy-start(s32[1,8,2]{1,2,0:T(2,128)} %param.19) | copy-start | bytes 196
  2.5 14.9 %collective-permute-start = (f32[1024,128]{1,0:T(8,128)}, f32[1024,128]{1,0:T(8,128)S(1)}, u32[]{:S(2)}, u32[]{:S(2)}) collective-permute-start(f32[1024,128]{1,0:T(8,128)} %slice.8), channel_id=1, source_target_pairs={{1,0},{2,1},{3,2},{4,3},{5,4},{6,5},{7,6},{9,8},{10,9},{11,10},{12... | collective-permute-start | bytes 1572872 | tf_op jit(solution)/shard_map/ppermute | solution.py:26
  7.4 21.3 %collective-permute-start.1 = (f32[1024,128]{1,0:T(8,128)}, f32[1024,128]{1,0:T(8,128)}, u32[]{:S(2)}, u32[]{:S(2)}) collective-permute-start(f32[1024,128]{1,0:T(8,128)} %slice.9), channel_id=1, source_target_pairs={{1,0},{2,1},{3,2},{4,3},{5,4},{6,5},{7,6},{9,8},{10,9},{11,10},{12... | collective-permute-start | bytes 1572872 | tf_op jit(solution)/shard_map/ppermute | solution.py:26
  11.5 17.2 %copy-start = (f32[1,1024,384]{2,1,0:T(8,128)S(1)}, f32[1,1024,384]{2,1,0:T(8,128)}, u32[]{:S(2)}) copy-start(f32[1,1024,384]{2,1,0:T(8,128)} %param.14) | copy-start | bytes 4718596
  11.5 17.2 %copy-start.1 = (f32[1,1024,384]{2,1,0:T(8,128)S(1)}, f32[1,1024,384]{2,1,0:T(8,128)}, u32[]{:S(2)}) copy-start(f32[1,1024,384]{2,1,0:T(8,128)} %param.15) | copy-start | bytes 4718596
  11.6 17.2 %copy-start.2 = (s32[8,2]{1,0:T(8,128)S(1)}, s32[8,2]{1,0:T(8,128)}, u32[]{:S(2)}) copy-start(s32[8,2]{1,0:T(8,128)} %copy.18.positions_ref) | copy-start | bytes 196
  11.6 17.2 %copy-start.7 = (f32[256,256]{1,0:T(8,128)S(1)}, f32[256,256]{1,0:T(8,128)}, u32[]{:S(2)}) copy-start(f32[256,256]{1,0:T(8,128)} %refs_6_.2) | copy-start | bytes 786436
  17.4 0.8 copy-start.3
  28.8 1.0 copy-start.4
  29.8 0.9 copy-start.8
  30.8 1.2 copy-start.9
  32.0 0.9 copy-start.10
  32.9 1.0 copy-start.11
  41.0 61.0 %copy-start.5 = (f32[2,384,128]{2,1,0:T(8,128)}, f32[2,384,128]{2,1,0:T(8,128)S(1)}, u32[]{:S(2)}) copy-start(f32[2,384,128]{2,1,0:T(8,128)S(1)} %get-tuple-element.29) | copy-start | bytes 1179652
  41.0 64.7 %copy-start.14 = (s32[4]{0:T(128)S(1)}, s32[4]{0:T(128)}, u32[]{:S(2)}) copy-start(s32[4]{0:T(128)} %param.22) | copy-start | bytes 52
  102.0 35.1 %collective-permute-start.2 = (f32[2,640,128]{2,1,0:T(8,128)S(1)}, f32[2,640,128]{2,1,0:T(8,128)}, u32[]{:S(2)}, u32[]{:S(2)}) collective-permute-start(f32[2,640,128]{2,1,0:T(8,128)S(1)} %get-tuple-element.24), channel_id=1, source_target_pairs={{0,1},{1,2},{2,3},{3,4},{4,5},{5,6},{6,7},{8,9},{9,10},{10,11},{11... | collective-permute-start | bytes 1966088 | tf_op jit(solution)/shard_map/ppermute | solution.py:26
  137.1 6.7 %copy-start.6 = (f32[2,384,128]{2,1,0:T(8,128)S(1)}, f32[2,384,128]{2,1,0:T(8,128)}, u32[]{:S(2)}) copy-start(f32[2,384,128]{2,1,0:T(8,128)} %copy-done.5) | copy-start | bytes 1179652
  137.1 54.3 %all-to-all-start.1 = ((f32[32,32,384]{2,1,0:T(8,128)}), f32[32,32,384]{2,1,0:T(8,128)S(1)}, u32[]{:S(2)}, u32[]{:S(2)}) async-start(f32[32,32,384]{2,1,0:T(8,128)} %get-tuple-element.26), calls=%async_computation.1 | async-start | bytes 3145728 | tf_op jit(solution)/shard_map/all_to_all | solution.py:578
  143.8 44.6 %collective-permute-start.3 = (f32[2,384,128]{2,1,0:T(8,128)S(1)}, f32[2,384,128]{2,1,0:T(8,128)S(1)}, u32[]{:S(2)}, u32[]{:S(2)}) collective-permute-start(f32[2,384,128]{2,1,0:T(8,128)S(1)} %copy-done.6), channel_id=1, source_target_pairs={{0,1},{1,2},{2,3},{3,4},{4,5},{5,6},{6,7},{8,9},{9,10},{10,11},{11... | collective-permute-start | bytes 1179656 | tf_op jit(solution)/shard_map/ppermute | solution.py:26
  147.0 41.4 %copy-start.13 = (f32[2,1024,128]{2,1,0:T(8,128)S(1)}, f32[2,1024,128]{2,1,0:T(8,128)}, u32[]{:S(2)}) copy-start(f32[2,1024,128]{2,1,0:T(8,128)} %get-tuple-element.27) | copy-start | bytes 3145732
  160.2 29.4 %copy-start.12 = (f32[2,1024,256]{2,1,0:T(8,128)S(1)}, f32[2,1024,256]{2,1,0:T(8,128)}, u32[]{:S(2)}) copy-start(f32[2,1024,256]{2,1,0:T(8,128)} %get-tuple-element.30) | copy-start | bytes 6291460

commit v2 on v1

--- a/solution.py
+++ b/solution.py
@@ -88,34 +88,33 @@
     *refs, base, beyond,
 ):
     if beyond:
-        (tile_re, tile_im, edge_re, edge_im, begun, routed_left, probe_re, probe_im, intensity,
-         tables, spread, grad_ref, early_ref, late_ref, routed_ref, *scratch) = refs
+        (tile_re, tile_im, edge, begun, probe_re, probe_im, intensity, tables_from, spread_from,
+         grad_ref, early_ref, late_ref, routed_ref, *scratch) = refs
     else:
-        (tile_re, tile_im, probe_re, probe_im, intensity, tables, spread,
+        (tile_re, tile_im, probe_re, probe_im, intensity, tables_from, spread_from,
          grad_ref, begun_ref, routed_ref, *scratch) = refs
-    ext, acc, measured, turned, uh, ul, vh, vl, residual, routed, sems, slot_sems = scratch
+    (ext, acc, measured, probes, tables, spread, turned, uh, ul, vh, vl, residual, routed,
+     prior, sems, slot_sems) = scratch
     height = ext.shape[2]
     tiles = ext.shape[1]
-    size = probe_re.shape[0]
+    size = probes.shape[1]
     half = size // 2
     used = used_ref[0, 0]
-    copies, late = [], []
+    copies = [
+        pltpu.make_async_copy(probe_re, probes.at[0], sems.at[0, 2 * tiles]),
+        pltpu.make_async_copy(probe_im, probes.at[1], sems.at[0, 2 * tiles + 1]),
+        pltpu.make_async_copy(tables_from, tables, sems.at[1, 0]),
+        pltpu.make_async_copy(spread_from, spread, sems.at[1, 1]),
+    ]
     for part, tile in enumerate((tile_re, tile_im)):
         for column in range(tiles):
             if beyond and column == tiles - 1:
-                source = (edge_re, edge_im)[part]
+                source = edge.at[part]
             else:
                 source = tile.at[:, pl.ds(base + column * LANES, LANES)]
             sem = sems.at[0, part * tiles + column]
             copies.append(pltpu.make_async_copy(source, ext.at[part, column], sem))
-            if beyond and column < tiles - 1:
-                sem = sems.at[1, part * tiles + column]
-                late.append(pltpu.make_async_copy(begun.at[part, column], acc.at[part, column], sem))
-    if beyond:
-        late.append(
-            pltpu.make_async_copy(routed_left, routed.at[:, pl.ds(0, LANES)], sems.at[1, tiles - 1])
-        )
-    for copy in copies + late:
+    for copy in copies:
         copy.start()
 
     def fetch(slot):
@@ -142,17 +141,18 @@
             for copy in fetch(slot):
                 copy.start()
 
-    first_fresh = tiles - 1 if beyond else 0
-
     @pl.loop(0, height // size)
     def _(chunk):
         rows = pl.ds(chunk * size, size)
         for part in range(2):
-            for column in range(first_fresh, tiles):
+            for column in range(tiles):
                 acc[part, column, rows, :] = jnp.zeros((size, LANES), jnp.float32)
 
-    for copy in copies + late:
+    for copy in copies:
         copy.wait()
+    if beyond:
+        earlier = pltpu.make_async_copy(begun, prior, sems.at[1, 2])
+        earlier.start()
 
     le, let, lo, lot = 0, 2, 4, 6
 
@@ -173,8 +173,8 @@
         low_rows = rows_of((SUBLANES, LANES)) < row_rest
         low_lanes = lanes_of((size, LANES)) < lane_rest
 
-        for part, probe in enumerate((probe_re, probe_im)):
-            for tile, piece in enumerate(rolled(probe[...], row_rest, lane_rest)):
+        for part in range(2):
+            for tile, piece in enumerate(rolled(probes[part], row_rest, lane_rest)):
                 turned[part, tile] = piece
 
         def window(part, at):
@@ -255,49 +255,72 @@
         def _():
             visit(slot)
 
+    if beyond:
+        earlier.wait()
+    routing = tiles if beyond else 1
+
+    @pl.loop(0, height // size)
+    def _(chunk):
+        rows = pl.ds(chunk * size, size)
+        for column in range(routing):
+            g_re, g_im = acc[0, column, rows, :], acc[1, column, rows, :]
+            if beyond and column < tiles - 1:
+                g_re = g_re + prior[0, column, rows, :]
+                g_im = g_im + prior[1, column, rows, :]
+                acc[0, column, rows, :] = g_re
+                acc[1, column, rows, :] = g_im
+            value = ext[0, column, rows, :] * g_im - ext[1, column, rows, :] * g_re
+            residual[column, rows, :] = value
+            residual[column, pl.ds(height + chunk * size, size), :] = value
+
+    shift = shift_ref[0]
     outs = []
-    if beyond:
-        for part in range(2):
+    for chunk in range(height // size):
+        rows = pl.ds(chunk * size, size)
+        for column in range(routing):
+            lanes = slice(column * LANES, (column + 1) * LANES)
+            routed[rows, lanes] = residual[column, pl.ds(height - shift + chunk * size, size), :]
+        outs.append((routed.at[rows], routed_ref.at[rows]))
+    for part in range(2):
+        if beyond:
+            rows = early_ref.shape[1]
             for column in range(tiles - 1):
                 target = grad_ref.at[part, :, pl.ds(column * LANES, LANES)]
                 outs.append((acc.at[part, column], target))
-            rows = early_ref.shape[1]
             outs.append((acc.at[part, tiles - 1, pl.ds(0, rows)], early_ref.at[part]))
             outs.append((acc.at[part, tiles - 1, pl.ds(rows, height - rows)], late_ref.at[part]))
-        routing = range(tiles)
-    else:
-        for part in range(2):
+        else:
             outs.append((acc.at[part, 0], grad_ref.at[part]))
             for column in range(1, tiles):
                 outs.append((acc.at[part, column], begun_ref.at[part, column - 1]))
-        routing = range(1)
-    outs = [pltpu.make_async_copy(*pair, sems.at[0, n]) for n, pair in enumerate(outs)]
+    outs = [pltpu.make_async_copy(*pair, sems.at[2, n]) for n, pair in enumerate(outs)]
     for copy in outs:
         copy.start()
-
-    @pl.loop(0, height // size)
-    def _(chunk):
-        rows = pl.ds(chunk * size, size)
-        for column in routing:
-            value = ext[0, column, rows, :] * acc[1, column, rows, :] - (
-                ext[1, column, rows, :] * acc[0, column, rows, :]
-            )
-            residual[column, rows, :] = value
-            residual[column, pl.ds(height + chunk * size, size), :] = value
-
-    shift = shift_ref[0]
-
-    ahead = 1 if beyond else 0
-    for chunk in range(height // size):
-        rows = pl.ds(chunk * size, size)
-        for column in routing:
-            lanes = slice((column + ahead) * LANES, (column + ahead + 1) * LANES)
-            routed[rows, lanes] = residual[column, pl.ds(height - shift + chunk * size, size), :]
-        copy = pltpu.make_async_copy(routed.at[rows], routed_ref.at[rows], slot_sems.at[chunk, 0])
-        copy.start()
-        outs.append(copy)
     for copy in outs:
         copy.wait()
+
+
+def margin_kernel(tile_re, tile_im, out, sems):
+    copies = [
+        pltpu.make_async_copy(tile.at[:, pl.ds(0, LANES)], out.at[part], sems.at[part])
+        for part, tile in enumerate((tile_re, tile_im))
+    ]
+    for copy in copies:
+        copy.start()
+    for copy in copies:
+        copy.wait()
+
+
+def margins(tile_re, tile_im):
+    return pl.pallas_call(
+        margin_kernel,
+        out_shape=jax.ShapeDtypeStruct((2, tile_re.shape[0], LANES), jnp.float32),
+        in_specs=[HBM, HBM],
+        out_specs=HBM,
+        scratch_shapes=[pltpu.SemaphoreType.DMA((2,))],
+        compiler_params=pltpu.CompilerParams(vmem_limit_bytes=VMEM_BYTES),
+        name="margins",
+    )(tile_re, tile_im)
 
 
 def probe_phase(used, positions, shift, tile, edge, begun, probe, intensity):
@@ -315,10 +338,10 @@
         return jax.ShapeDtypeStruct(shape, jnp.float32)
 
     if beyond:
-        operands = (*tile, *edge, *begun)
+        operands = (*tile, edge, begun)
         early = height * 5 // 8 // SUBLANES * SUBLANES
         spills = (out(2, early, LANES), out(2, height - early, LANES))
-        outs = (out(2, height, width - LANES), *spills, out(height, width + LANES))
+        outs = (out(2, height, width - LANES), *spills, out(height, width))
         base = LANES
     else:
         operands = tile
@@ -327,21 +350,23 @@
     return pl.pallas_call(
         functools.partial(probe_kernel, base=base, beyond=beyond),
         out_shape=outs,
-        in_specs=[SMEM, SMEM, SMEM, *[ANY] * len(operands), VMEM, VMEM, ANY, VMEM, VMEM],
+        in_specs=[SMEM, SMEM, SMEM, *[HBM] * (len(operands) + 5)],
         out_specs=(HBM,) * len(outs),
         scratch_shapes=[
             planes, planes,
             pltpu.VMEM((slots, 2, size, LANES), jnp.float32),
+            pltpu.VMEM((2, size, size), jnp.float32),
+            pltpu.VMEM(tables.shape, SPLIT),
+            plane,
             pltpu.VMEM((2, 2, size, LANES), jnp.float32),
             plane, plane, plane, plane,
             pltpu.VMEM((routing, 2 * height, LANES), jnp.float32),
             pltpu.VMEM((height, outs[-1].shape[1]), jnp.float32),
-            pltpu.SemaphoreType.DMA((2, 2 * columns + 2)),
-            pltpu.SemaphoreType.DMA((max(slots, height // size), 2)),
+            pltpu.VMEM((2, columns - 1, height, LANES), jnp.float32),
+            pltpu.SemaphoreType.DMA((3, 2 * columns + 2 + height // size)),
+            pltpu.SemaphoreType.DMA((slots, 2)),
         ],
-        compiler_params=pltpu.CompilerParams(
-            vmem_limit_bytes=VMEM_BYTES * 3 // 4 if beyond else VMEM_BYTES
-        ),
+        compiler_params=pltpu.CompilerParams(vmem_limit_bytes=VMEM_BYTES),
         cost_estimate=pl.CostEstimate(
             flops=26 * slots * size**3, bytes_accessed=16 * height * width, transcendentals=0
         ),
@@ -415,14 +440,14 @@
 
 
 def step_kernel(
-    turned, whole, frac, pieces, old, parts, update, near, cells, before, after, sems
+    turned, whole, frac, left, right, old, parts, update, near, cells, before, after, sems
 ):
     old_copy = pltpu.make_async_copy(old, before, sems.at[0])
     old_copy.start()
     depth = cells.shape[0]
     tilts = near.shape[0]
-    tiles = pieces.shape[0] // tilts
-    own = pieces.shape[2] // LANES - 1
+    tiles = right.shape[0] // tilts
+    own = right.shape[2] // LANES
     band = turned.band
 
     def place(block, segment):
@@ -435,9 +460,12 @@
             for segment in range(turned.segments):
                 tile, column = place(block, segment)
                 source = tilt * tiles + tile
-                value = pieces[source, :, column * LANES : (column + 1) * LANES]
-                if column == 0 and tile > 0:
-                    value = value + pieces[source - 1, :, own * LANES :]
+                if column > 0:
+                    value = right[source, :, (column - 1) * LANES : column * LANES]
+                elif tile > 0:
+                    value = left[source] + right[source - 1, :, (own - 1) * LANES :]
+                else:
+                    value = left[source]
                 cut.append(value)
             turned.store(near, tilt, block * LANES, jnp.concatenate(cut, axis=0).T)
 
@@ -514,26 +542,25 @@
     )(whole, frac, volume)
 
 
-def volume_step(turned, whole, frac, pieces, old):
+def volume_step(turned, whole, frac, left, right, old):
     tilts, depth = whole.shape
-    width = pieces.shape[2] - LANES
     return pl.pallas_call(
         functools.partial(step_kernel, turned),
         out_shape=(
-            jax.ShapeDtypeStruct((*pieces.shape[:2], width), jnp.float32),
+            jax.ShapeDtypeStruct(right.shape, jnp.float32),
             jax.ShapeDtypeStruct((depth, turned.length, LANES), jnp.float32),
         ),
-        in_specs=[SMEM, SMEM, VMEM, HBM],
+        in_specs=[SMEM, SMEM, VMEM, VMEM, HBM],
         out_specs=(HBM, HBM),
         scratch_shapes=[
             turned.scratch(tilts), turned.scratch(depth),
             pltpu.VMEM(old.shape, jnp.float32),
-            pltpu.VMEM((*pieces.shape[:2], width), jnp.float32),
+            pltpu.VMEM(right.shape, jnp.float32),
             pltpu.SemaphoreType.DMA((2 + tilts,)),
         ],
         name="volume_step",
         **kernel_options(16 * depth * old.size, 4 * depth * turned.length * LANES, 9 / 10),
-    )(whole, frac, pieces, old)
+    )(whole, frac, left, right, old)
 
 
 def fresh_volume(turned, volume, update):
@@ -563,19 +590,25 @@
     whole, frac = shift_tables(slope, depth)
     probe = (probe_re, probe_im)
 
-    edge = [passed_along(part[:, :LANES], "tile", -1) for part in tile]
     within = (counts, positions[0], row_shift)
-    grad_left, *begun = probe_phase(*within, tile, None, None, probe, intensity[0])
-    grad_right, early, late, routed = probe_phase(*within, tile, edge, begun, probe, intensity[0])
-    routed = routed.reshape(devices, band, width + LANES)
-    pieces = lax.all_to_all(routed, axes, split_axis=0, concat_axis=0, tiled=True)
+
+    def exchanged(blocks):
+        return lax.all_to_all(blocks, axes, split_axis=0, concat_axis=0, tiled=True)
+
+    edge = passed_along(margins(*tile), "tile", -1)
+    grad_left, begun, left = probe_phase(*within, tile, None, None, probe, intensity[0])
+    left, edge = lax.optimization_barrier((left, edge))
+    left = exchanged(left.reshape(devices, band, LANES))
+    grad_right, early, late, right = probe_phase(*within, tile, edge, begun, probe, intensity[0])
+    right, whole = lax.optimization_barrier((right, whole))
+    right = exchanged(right.reshape(devices, band, width))
     old = old_projection(turned, whole, frac, volume)
-    pieces, early = lax.optimization_barrier((pieces, early))
+    right, early, old = lax.optimization_barrier((right, early, old))
     early = passed_along(early, "tile", 1)
-    parts, update = volume_step(turned, whole, frac, pieces, old)
+    parts, update = volume_step(turned, whole, frac, left, right, old)
     parts, early, late = lax.optimization_barrier((parts, early, late))
     late = passed_along(late, "tile", 1)
-    returned = lax.all_to_all(parts, axes, split_axis=0, concat_axis=0, tiled=True)
+    returned = exchanged(parts)
     fresh = fresh_volume(turned, volume, update)
     spill = jnp.concatenate([early, late], axis=1)
     grad = jnp.concatenate([grad_left + spill, grad_right], axis=2)[:, None]

time: 192 us -> 213 us (1.11)
  Pallas kernels: 56 us -> 94.2 us
  blocking collectives: 61 us -> 46.6 us
  local copies, waits for them, and re-layouts: 10.4 us -> 2.45 us
  waiting for transfers between devices: 39 us -> 41.3 us
    pallas_call x0 -> x1, Pallas kernels: none -> 32.9 us  [margins(): pl.pallas_call(margin_kernel, out_shape=jax.ShapeDtypeStruct((2, tile_re....]
    all_to_all x1, blocking collectives: 61 us -> 46.6 us  [exchanged(): return lax.all_to_all(blocks, axes, split_axis=0, concat_axis=0, tiled=True)]
    pallas_call x2, Pallas kernels: 12.6 us -> 18 us  [probe_phase(): pl.pallas_call(functools.partial(probe_kernel, base=base, beyond=beyond),...]
    all_to_all x1 -> x2, starting transfers between devices: 6.65 us -> 11.2 us  [exchanged(): return lax.all_to_all(blocks, axes, split_axis=0, concat_axis=0, tiled=True)]
    unnamed x32 -> x14, local copies, waits for them, and re-layouts: 6 us -> 1.78 us
    slice x2 -> x0, local copies, waits for them, and re-layouts: 3.74 us -> none  [local(): edge = [passed_along(part[:, :LANES], 'tile', -1) for part in tile]]
    ppermute x4 -> x3, starting transfers between devices: 11.9 us -> 9.25 us  [passed_along(): return lax.ppermute(block, axis, route)]
    ppermute x4 -> x3, waiting for transfers between devices: 39 us -> 41.3 us  [passed_along(): return lax.ppermute(block, axis, route)]
  transfers between devices with their start and end apart: 5 -> 5, of which waited for: 3 -> 2; matrix products, arithmetic and copies ran while one was open for 4% -> 2% of each run, Pallas kernels for 25% -> 24%
where the time goes in v2:
time: 213 us
  Pallas kernels  94.2 us (44%)
  blocking collectives  46.6 us (22%)
  waiting for transfers between devices  41.3 us (19%)
  starting transfers between devices  20.5 us (10%)
  other arithmetic  6.21 us (3%)
  local copies, waits for them, and re-layouts  2.45 us (1%)
    all_to_all x1, blocking collectives, exchanged(): return lax.all_to_all(blocks, axes, split_axis=0, concat_axis=0, tiled=True)  46.6 us
    ppermute x3, waiting for transfers between devices, passed_along(): return lax.ppermute(block, axis, route)  41.3 us
    pallas_call x1, Pallas kernels, margins(): pl.pallas_call(margin_kernel, out_shape=jax.ShapeDtypeStruct((2, tile_re....  32.9 us
    pallas_call x2, Pallas kernels, probe_phase(): pl.pallas_call(functools.partial(probe_kernel, base=base, beyond=beyond),...  18 us
    pallas_call x1, Pallas kernels, volume_step(): pl.pallas_call(functools.partial(step_kernel, turned), out_shape=(jax.Sha...  16.3 us
    pallas_call x1, Pallas kernels, old_projection(): pl.pallas_call(functools.partial(old_kernel, turned), out_shape=jax.Shape...  13.6 us
    pallas_call x1, Pallas kernels, fresh_volume(): pl.pallas_call(functools.partial(fresh_kernel, turned), grid=(depth,), ou...  13.3 us
    all_to_all x2, starting transfers between devices, exchanged(): return lax.all_to_all(blocks, axes, split_axis=0, concat_axis=0, tiled=True)  11.2 us
  transfers between devices with their start and end apart: 5, of which 2 were waited for; matrix products, arithmetic and copies ran while one was open for 2% of the time, Pallas kernels for 24%

profile of v2, /device:TPU:17, one launch (start us, length us, event | category | flops | bytes accessed | tf_op | source)
XLA Modules:
  0.0 213.2 jit_solution(2555960604471677928)
XLA Ops:
  0.6 0.0 copy-start.4
  0.6 0.0 copy-start.3
  0.7 32.9 %margins.1 = f32[2,1024,128]{2,1,0:T(8,128)} custom-call(f32[1024,384]{1,0:T(8,128)} %bitcast.18, f32[1024,384]{1,0:T(8,128)} %bitcast.21), custom_call_target="tpu_custom_call" | custom-call | tf_op jit(solution)/shard_map/margins/pallas_call | solution.py:315
  33.5 3.0 %collective-permute-start = (f32[2,1024,128]{2,1,0:T(8,128)}, f32[2,1024,128]{2,1,0:T(8,128)S(1)}, u32[]{:S(2)}, u32[]{:S(2)}) collective-permute-start(f32[2,1024,128]{2,1,0:T(8,128)} %margins.1), channel_id=1, source_target_pairs={{1,0},{2,1},{3,2},{4,3},{5,4},{6,5},{7,6},{9,8},{10,9},{11,10},{12... | collective-permute-start | bytes 3145736 | tf_op jit(solution)/shard_map/ppermute | solution.py:26
  37.2 0.0 copy-done.4
  37.2 0.7 copy.18.positions_ref
  38.6 0.0 copy-done.3
  38.6 0.6 add_select_fusion.whole
  39.2 7.6 %probes_within.1 = (f32[2,1024,128]{2,1,0:T(8,128)}, f32[2,2,1024,128]{3,2,1,0:T(8,128)}, f32[1024,128]{1,0:T(8,128)}) custom-call(s32[1,1]{1,0:T(1,128)S(6)} %copy.20.used_ref, s32[8,2]{1,0:T(8,128)} %copy.18.positions_ref, s32[1]{0:T(128)} %copy.21.shift_ref, f32[1024,384]{1,0:T(8,128)} %bitcast.19, f32[1024,384]{1,0:T(8,128)} %bitcast.22, ...), custom_call_target="tpu_custom_call" | custom-call | flops 3489660928 | bytes 6291456 | tf_op jit(solution)/shard_map/probes_within/pallas_call | solution.py:350
  46.8 12.8 %collective-permute-done.refs_2_ = f32[2,1024,128]{2,1,0:T(8,128)S(1)} collective-permute-done((f32[2,1024,128]{2,1,0:T(8,128)}, f32[2,1024,128]{2,1,0:T(8,128)S(1)}, u32[]{:S(2)}, u32[]{:S(2)}) %collective-permute-start) | collective-permute-done | bytes 1048608 | tf_op jit(solution)/shard_map/ppermute | solution.py:26
  59.7 0.0 copy-start.5
  59.7 1.0 copy-done.5
  60.6 10.4 %probes_beyond.1 = (f32[2,1024,256]{2,1,0:T(8,128)}, f32[2,640,128]{2,1,0:T(8,128)}, f32[2,384,128]{2,1,0:T(8,128)}, f32[1024,384]{1,0:T(8,128)}) custom-call(s32[1,1]{1,0:T(1,128)S(6)} %copy.20.used_ref, s32[8,2]{1,0:T(8,128)} %copy.18.positions_ref, s32[1]{0:T(128)} %copy.21.shift_ref, f32[1024,384]{1,0:T(8,128)} %bitcast.20, f32[1024,384]{1,0:T(8,128)} %bitcast.23, ...), custom_call_target="tpu_custom_call" | custom-call | flops 3489660928 | bytes 6291456 | tf_op jit(solution)/shard_map/probes_beyond/pallas_call | solution.py:350
  71.1 46.6 %all_to_all.15.right = f32[32,32,384]{2,1,0:T(8,128)} all-to-all(f32[32,32,384]{2,1,0:T(8,128)} %bitcast.17), channel_id=1, replica_groups=mesh['tilt'=4,'tile'=8] {'tilt','tile'}, dimensions={0} | all-to-all | bytes 3145728 | tf_op jit(solution)/shard_map/all_to_all | solution.py:596
  117.6 6.0 %all-to-all-start = ((f32[32,32,128]{2,1,0:T(8,128)}), f32[32,32,128]{2,1,0:T(8,128)S(1)}, u32[]{:S(2)}, u32[]{:S(2)}) async-start(f32[32,32,128]{2,1,0:T(8,128)} %bitcast.4), calls=%async_computation | async-start | bytes 1048576 | tf_op jit(solution)/shard_map/all_to_all | solution.py:596
  123.6 0.7 convert_multiply_fusion.frac
  124.3 0.0 copy-start.6
  124.3 13.6 %old_projection.1.old = f32[4,768,128]{2,1,0:T(8,128)} custom-call(s32[4,16]{1,0:T(4,128)} %add_select_fusion.whole, f32[4,16]{1,0:T(4,128)} %convert_multiply_fusion.frac, f32[16,32,3072]{2,1,0:T(8,128)} %volume.3), custom_call_target="tpu_custom_call" | custom-call | flops 50331648 | bytes 6291456 | tf_op jit(solution)/shard_map/old_projection/pallas_call | solution.py:534
  137.9 0.0 copy-done.6
  137.9 3.1 %collective-permute-start.1 = (f32[2,640,128]{2,1,0:T(8,128)S(1)}, f32[2,640,128]{2,1,0:T(8,128)S(1)}, u32[]{:S(2)}, u32[]{:S(2)}) collective-permute-start(f32[2,640,128]{2,1,0:T(8,128)S(1)} %copy-done.6), channel_id=1, source_target_pairs={{0,1},{1,2},{2,3},{3,4},{4,5},{5,6},{6,7},{8,9},{9,10},{10,11},{11... | collective-permute-start | bytes 1966088 | tf_op jit(solution)/shard_map/ppermute | solution.py:26
  141.1 0.0 all-to-all-done.left
  141.1 0.0 copy-start.1
  141.1 0.8 copy-done.1
  141.9 16.3 %volume_step.1 = (f32[32,32,384]{2,1,0:T(8,128)}, f32[16,768,128]{2,1,0:T(8,128)}) custom-call(s32[4,16]{1,0:T(4,128)} %add_select_fusion.whole, f32[4,16]{1,0:T(4,128)} %convert_multiply_fusion.frac, f32[32,32,128]{2,1,0:T(8,128)} %copy-done.1, f32[32,32,384]{2,1,0:T(8,128)} %all_to_all.15.right, f32[4,768,128]{2,1,0:T(8,128)} %old_projection.1.old), custom_call_target="tpu_custom_call" | custom-call | flops 100663296 | bytes 6291456 | tf_op jit(solution)/shard_map/volume_step/pallas_call | solution.py:547
  158.2 0.0 collective-permute-done.1
  158.2 5.2 %all-to-all-start.2 = ((f32[32,32,384]{2,1,0:T(8,128)}), f32[32,32,384]{2,1,0:T(8,128)S(1)}, u32[]{:S(2)}, u32[]{:S(2)}) async-start(f32[32,32,384]{2,1,0:T(8,128)} %get-tuple-element.36), calls=%async_computation.2 | async-start | bytes 3145728 | tf_op jit(solution)/shard_map/all_to_all | solution.py:596
  163.4 3.1 %collective-permute-start.2 = (f32[2,384,128]{2,1,0:T(8,128)}, f32[2,384,128]{2,1,0:T(8,128)}, u32[]{:S(2)}, u32[]{:S(2)}) collective-permute-start(f32[2,384,128]{2,1,0:T(8,128)} %get-tuple-element.39), channel_id=1, source_target_pairs={{0,1},{1,2},{2,3},{3,4},{4,5},{5,6},{6,7},{8,9},{9,10},{10,11},{11... | collective-permute-start | bytes 1179656 | tf_op jit(solution)/shard_map/ppermute | solution.py:26
  166.6 0.0 copy-start.2
  166.6 13.3 %fresh_volume.1 = f32[16,32,3072]{2,1,0:T(8,128)} custom-call(f32[16,32,3072]{2,1,0:T(8,128)} %volume.3, f32[16,768,128]{2,1,0:T(8,128)} %get-tuple-element.32.update), custom_call_target="tpu_custom_call" | custom-call | flops 1572864 | bytes 18874368 | tf_op jit(solution)/shard_map/fresh_volume/pallas_call | solution.py:570
  179.8 0.0 copy-start
  179.8 28.4 %collective-permute-done.2 = f32[2,384,128]{2,1,0:T(8,128)} collective-permute-done((f32[2,384,128]{2,1,0:T(8,128)}, f32[2,384,128]{2,1,0:T(8,128)}, u32[]{:S(2)}, u32[]{:S(2)}) %collective-permute-start.2) | collective-permute-done | bytes 393248 | tf_op jit(solution)/shard_map/ppermute | solution.py:26
  208.2 0.0 copy-done.2
  208.2 1.1 maximum_add_fusion
  209.4 0.0 copy-done
  209.4 1.9 maximum_bitcast_fusion
  211.2 0.0 all-to-all-done.2
  211.2 2.0 fusion.1
Async XLA Ops:
  0.6 36.6 %copy-start.4 = (s32[1,8,2]{1,2,0:T(2,128)S(1)}, s32[1,8,2]{1,2,0:T(2,128)}, u32[]{:S(2)}) copy-start(s32[1,8,2]{1,2,0:T(2,128)} %param.19) | copy-start | bytes 196
  0.6 37.9 %copy-start.3 = (s32[4]{0:T(128)S(1)}, s32[4]{0:T(128)}, u32[]{:S(2)}) copy-start(s32[4]{0:T(128)} %param.22) | copy-start | bytes 52
  33.5 26.1 %collective-permute-start = (f32[2,1024,128]{2,1,0:T(8,128)}, f32[2,1024,128]{2,1,0:T(8,128)S(1)}, u32[]{:S(2)}, u32[]{:S(2)}) collective-permute-start(f32[2,1024,128]{2,1,0:T(8,128)} %margins.1), channel_id=1, source_target_pairs={{1,0},{2,1},{3,2},{4,3},{5,4},{6,5},{7,6},{9,8},{10,9},{11,10},{12... | collective-permute-start | bytes 3145736 | tf_op jit(solution)/shard_map/ppermute | solution.py:26
  59.7 1.0 copy-start.5
  117.6 23.4 %all-to-all-start = ((f32[32,32,128]{2,1,0:T(8,128)}), f32[32,32,128]{2,1,0:T(8,128)S(1)}, u32[]{:S(2)}, u32[]{:S(2)}) async-start(f32[32,32,128]{2,1,0:T(8,128)} %bitcast.4), calls=%async_computation | async-start | bytes 1048576 | tf_op jit(solution)/shard_map/all_to_all | solution.py:596
  124.3 13.6 %copy-start.6 = (f32[2,640,128]{2,1,0:T(8,128)S(1)}, f32[2,640,128]{2,1,0:T(8,128)}, u32[]{:S(2)}) copy-start(f32[2,640,128]{2,1,0:T(8,128)} %get-tuple-element.34) | copy-start | bytes 1966084
  137.9 20.3 %collective-permute-start.1 = (f32[2,640,128]{2,1,0:T(8,128)S(1)}, f32[2,640,128]{2,1,0:T(8,128)S(1)}, u32[]{:S(2)}, u32[]{:S(2)}) collective-permute-start(f32[2,640,128]{2,1,0:T(8,128)S(1)} %copy-done.6), channel_id=1, source_target_pairs={{0,1},{1,2},{2,3},{3,4},{4,5},{5,6},{6,7},{8,9},{9,10},{10,11},{11... | collective-permute-start | bytes 1966088 | tf_op jit(solution)/shard_map/ppermute | solution.py:26
  141.1 0.8 copy-start.1
  158.2 53.0 %all-to-all-start.2 = ((f32[32,32,384]{2,1,0:T(8,128)}), f32[32,32,384]{2,1,0:T(8,128)S(1)}, u32[]{:S(2)}, u32[]{:S(2)}) async-start(f32[32,32,384]{2,1,0:T(8,128)} %get-tuple-element.36), calls=%async_computation.2 | async-start | bytes 3145728 | tf_op jit(solution)/shard_map/all_to_all | solution.py:596
  163.4 44.8 %collective-permute-start.2 = (f32[2,384,128]{2,1,0:T(8,128)}, f32[2,384,128]{2,1,0:T(8,128)}, u32[]{:S(2)}, u32[]{:S(2)}) collective-permute-start(f32[2,384,128]{2,1,0:T(8,128)} %get-tuple-element.39), channel_id=1, source_target_pairs={{0,1},{1,2},{2,3},{3,4},{4,5},{5,6},{6,7},{8,9},{9,10},{10,11},{11... | collective-permute-start | bytes 1179656 | tf_op jit(solution)/shard_map/ppermute | solution.py:26
  166.6 41.7 %copy-start.2 = (f32[2,1024,128]{2,1,0:T(8,128)S(1)}, f32[2,1024,128]{2,1,0:T(8,128)}, u32[]{:S(2)}) copy-start(f32[2,1024,128]{2,1,0:T(8,128)} %get-tuple-element.37) | copy-start | bytes 3145732
  179.8 29.5 %copy-start = (f32[2,1024,256]{2,1,0:T(8,128)S(1)}, f32[2,1024,256]{2,1,0:T(8,128)}, u32[]{:S(2)}) copy-start(f32[2,1024,256]{2,1,0:T(8,128)} %get-tuple-element.40) | copy-start | bytes 6291460

commit v3 on v2

--- a/solution.py
+++ b/solution.py
@@ -13,6 +13,7 @@
 LANES = 128
 SUBLANES = 8
 VMEM_BYTES = 60 * 1024 * 1024
+PROBE_SCRATCH = 15
 SPLIT = jnp.bfloat16
 ANY = pl.BlockSpec(memory_space=pl.ANY)
 HBM = pl.BlockSpec(memory_space=pltpu.HBM)
@@ -23,6 +24,12 @@
 def passed_along(block, axis, distance):
     devices = range(lax.axis_size(axis))
     route = [(i - distance, i) for i in devices if i - distance in devices]
+    return lax.ppermute(block, axis, route)
+
+
+def passed_by(block, axis, first, step):
+    count = lax.axis_size(axis)
+    route = [(i, i + step) for i in range(first, count, 2) if 0 <= i + step < count]
     return lax.ppermute(block, axis, route)
 
 
@@ -89,12 +96,12 @@
 ):
     if beyond:
         (tile_re, tile_im, edge, begun, probe_re, probe_im, intensity, tables_from, spread_from,
-         grad_ref, early_ref, late_ref, routed_ref, *scratch) = refs
+         grad_ref, *spill_refs, routed_ref) = refs[: len(refs) - PROBE_SCRATCH]
     else:
         (tile_re, tile_im, probe_re, probe_im, intensity, tables_from, spread_from,
-         grad_ref, begun_ref, routed_ref, *scratch) = refs
-    (ext, acc, measured, probes, tables, spread, turned, uh, ul, vh, vl, residual, routed,
-     prior, sems, slot_sems) = scratch
+         grad_ref, begun_ref, routed_ref) = refs[: len(refs) - PROBE_SCRATCH]
+    (ext, acc, measured, probes, tables, spread, turned, planes, residual, routed,
+     prior, listed, sems, slot_sems, out_sems) = refs[len(refs) - PROBE_SCRATCH :]
     height = ext.shape[2]
     tiles = ext.shape[1]
     size = probes.shape[1]
@@ -159,7 +166,7 @@
     def table(which):
         return tables[which], tables[which + 1]
 
-    def visit(slot):
+    def visit(slot, turned, uh, ul, vh, vl):
         row = positions_ref[slot, 0]
         col = positions_ref[slot, 1] - base
         first = pl.multiple_of(row // SUBLANES * SUBLANES, SUBLANES)
@@ -197,6 +204,7 @@
             lanes = slice(part * LANES, (part + 1) * LANES)
             uh[:, lanes], ul[:, lanes] = split(psi[0][part] + psi[1][part])
             vh[:, lanes], vl[:, lanes] = split(psi[0][part] - psi[1][part])
+        yield
         even = dot3(uh[...], ul[...], *table(let))
         odd = dot3(vh[...], vl[...], *table(lot))
         for part in range(2):
@@ -206,6 +214,7 @@
                 y = y[:, part * LANES : (part + 1) * LANES]
                 uh[rows, lanes], ul[rows, lanes] = split(y[:half] + y[half:])
                 vh[rows, lanes], vl[rows, lanes] = split(y[:half] - y[half:])
+        yield
         for copy in fetch(slot):
             copy.wait()
         for parity, (h, l, which) in enumerate(((uh, ul, le), (vh, vl, lo))):
@@ -217,6 +226,7 @@
             excess = f_re * f_re + f_im * f_im - (dot(mh, spread[...]) + dot(ml, spread[...]))
             h[:half, :], l[:half, :] = split(excess * f_re)
             h[half:, :], l[half:, :] = split(excess * f_im)
+        yield
         th, tl = table(let)
         even = dot(th, uh[...]) + dot(tl, uh[...]) + dot(th, ul[...])
         th, tl = table(lot)
@@ -229,6 +239,7 @@
                 t = even[rows] + odd[rows] if sign == 0 else even[rows] - odd[rows]
                 uh[out, lanes], ul[out, lanes] = split(t[:, :LANES])
                 vh[out, lanes], vl[out, lanes] = split(t[:, LANES:])
+        yield
         even = dot3(uh[...], ul[...], *table(le))
         odd = dot3(vh[...], vl[...], *table(lo))
         for tile in range(2):
@@ -248,55 +259,77 @@
                     kept = jnp.where(low_rows, 0.0, top)
                     acc[part, at, body, :] += jnp.concatenate([kept, value[SUBLANES:]], axis=0)
                     acc[part, at, tail, :] += jnp.where(low_rows, top, 0.0)
-
-    @pl.loop(0, used)
-    def _(slot):
+        yield
+
+    def buffers(which):
+        return (turned.at[which], *(planes.at[which, n] for n in range(4)))
+
+    def together(*slots):
+        for _ in zip(*(visit(slot, *buffers(which)) for which, slot in enumerate(slots))):
+            pass
+
+    def enlist(slot, count):
         @pl.when(live(slot))
         def _():
-            visit(slot)
-
+            listed[count] = slot
+
+        return count + live(slot).astype(jnp.int32)
+
+    count = lax.fori_loop(0, used, enlist, 0)
+
+    @pl.loop(0, count // 2)
+    def _(pair):
+        together(listed[2 * pair], listed[2 * pair + 1])
+
+    @pl.when(count % 2 == 1)
+    def _():
+        together(listed[count - 1])
+
+    sent = []
+
+    def send(source, target):
+        sent.append(pltpu.make_async_copy(source, target, out_sems.at[len(sent)]))
+        sent[-1].start()
+
+    last = tiles - 1
+    for part in range(2):
+        if beyond:
+            first_row = 0
+            for spill_ref in spill_refs:
+                rows = pl.ds(first_row, spill_ref.shape[1])
+                send(acc.at[part, last, rows], spill_ref.at[part])
+                first_row += spill_ref.shape[1]
+        else:
+            send(acc.at[part, 0], grad_ref.at[part])
+            for column in range(1, tiles):
+                send(acc.at[part, column], begun_ref.at[part, column - 1])
     if beyond:
         earlier.wait()
     routing = tiles if beyond else 1
 
-    @pl.loop(0, height // size)
-    def _(chunk):
+    for chunk in range(height // size):
         rows = pl.ds(chunk * size, size)
         for column in range(routing):
             g_re, g_im = acc[0, column, rows, :], acc[1, column, rows, :]
-            if beyond and column < tiles - 1:
+            if beyond and column < last:
                 g_re = g_re + prior[0, column, rows, :]
                 g_im = g_im + prior[1, column, rows, :]
-                acc[0, column, rows, :] = g_re
-                acc[1, column, rows, :] = g_im
+                lanes = pl.ds(column * LANES, LANES)
+                for part, g in enumerate((g_re, g_im)):
+                    acc[part, column, rows, :] = g
+                    send(acc.at[part, column, rows], grad_ref.at[part, rows, lanes])
             value = ext[0, column, rows, :] * g_im - ext[1, column, rows, :] * g_re
             residual[column, rows, :] = value
             residual[column, pl.ds(height + chunk * size, size), :] = value
 
     shift = shift_ref[0]
-    outs = []
     for chunk in range(height // size):
         rows = pl.ds(chunk * size, size)
         for column in range(routing):
             lanes = slice(column * LANES, (column + 1) * LANES)
             routed[rows, lanes] = residual[column, pl.ds(height - shift + chunk * size, size), :]
-        outs.append((routed.at[rows], routed_ref.at[rows]))
-    for part in range(2):
-        if beyond:
-            rows = early_ref.shape[1]
-            for column in range(tiles - 1):
-                target = grad_ref.at[part, :, pl.ds(column * LANES, LANES)]
-                outs.append((acc.at[part, column], target))
-            outs.append((acc.at[part, tiles - 1, pl.ds(0, rows)], early_ref.at[part]))
-            outs.append((acc.at[part, tiles - 1, pl.ds(rows, height - rows)], late_ref.at[part]))
-        else:
-            outs.append((acc.at[part, 0], grad_ref.at[part]))
-            for column in range(1, tiles):
-                outs.append((acc.at[part, column], begun_ref.at[part, column - 1]))
-    outs = [pltpu.make_async_copy(*pair, sems.at[2, n]) for n, pair in enumerate(outs)]
-    for copy in outs:
-        copy.start()
-    for copy in outs:
+        send(routed.at[rows], routed_ref.at[rows])
+    for copy in sent:
         copy.wait()
 
 
@@ -312,13 +345,14 @@
 
 
 def margins(tile_re, tile_im):
+    shape = (2, tile_re.shape[0], LANES)
     return pl.pallas_call(
         margin_kernel,
-        out_shape=jax.ShapeDtypeStruct((2, tile_re.shape[0], LANES), jnp.float32),
+        out_shape=jax.ShapeDtypeStruct(shape, jnp.float32),
         in_specs=[HBM, HBM],
-        out_specs=HBM,
+        out_specs=VMEM,
         scratch_shapes=[pltpu.SemaphoreType.DMA((2,))],
-        compiler_params=pltpu.CompilerParams(vmem_limit_bytes=VMEM_BYTES),
+        compiler_params=pltpu.CompilerParams(vmem_limit_bytes=VMEM_BYTES // 4),
         name="margins",
     )(tile_re, tile_im)
 
@@ -339,8 +373,9 @@
 
     if beyond:
         operands = (*tile, edge, begun)
-        early = height * 5 // 8 // SUBLANES * SUBLANES
-        spills = (out(2, early, LANES), out(2, height - early, LANES))
+        early = height * 9 // 16 // SUBLANES * SUBLANES
+        late = (height - early) // 2 // SUBLANES * SUBLANES
+        spills = [out(2, rows, LANES) for rows in (early, late, height - early - late)]
         outs = (out(2, height, width - LANES), *spills, out(height, width))
         base = LANES
     else:
@@ -350,7 +385,7 @@
     return pl.pallas_call(
         functools.partial(probe_kernel, base=base, beyond=beyond),
         out_shape=outs,
-        in_specs=[SMEM, SMEM, SMEM, *[HBM] * (len(operands) + 5)],
+        in_specs=[SMEM, SMEM, SMEM, *[HBM if x is not edge else ANY for x in operands], *[HBM] * 5],
         out_specs=(HBM,) * len(outs),
         scratch_shapes=[
             planes, planes,
@@ -358,13 +393,15 @@
             pltpu.VMEM((2, size, size), jnp.float32),
             pltpu.VMEM(tables.shape, SPLIT),
             plane,
-            pltpu.VMEM((2, 2, size, LANES), jnp.float32),
-            plane, plane, plane, plane,
+            pltpu.VMEM((2, 2, 2, size, LANES), jnp.float32),
+            pltpu.VMEM((2, 4, size, size), SPLIT),
             pltpu.VMEM((routing, 2 * height, LANES), jnp.float32),
             pltpu.VMEM((height, outs[-1].shape[1]), jnp.float32),
             pltpu.VMEM((2, columns - 1, height, LANES), jnp.float32),
-            pltpu.SemaphoreType.DMA((3, 2 * columns + 2 + height // size)),
+            pltpu.SMEM((slots,), jnp.int32),
+            pltpu.SemaphoreType.DMA((2, 2 * columns + 2)),
             pltpu.SemaphoreType.DMA((slots, 2)),
+            pltpu.SemaphoreType.DMA((3 * columns + (2 * columns + 1) * (height // size),)),
         ],
         compiler_params=pltpu.CompilerParams(vmem_limit_bytes=VMEM_BYTES),
         cost_estimate=pl.CostEstimate(
@@ -407,17 +444,17 @@
     def project(self, whole, frac, ref, tilt, at, rows):
         depth = ref.shape[0]
 
-        def add_level(level, total):
-            start = self.margin + at - whole[tilt, level]
-            far = frac[tilt, level]
-            return (
-                total
-                + (1.0 - far) * ref[level, pl.ds(start, rows), :]
-                + far * ref[level, pl.ds(start - 1, rows), :]
-            )
-
-        zero = jnp.zeros((rows, LANES), jnp.float32)
-        return lax.fori_loop(0, depth, add_level, zero, unroll=4)
+        def add_level(level, totals):
+            plain, weighted = totals
+            start = self.margin + at - whole[tilt, level] - SUBLANES
+            x = ref[level, pl.ds(start, rows + SUBLANES), :]
+            return plain + x[SUBLANES:], weighted + frac[tilt, level] * x
+
+        zero = jnp.zeros((rows + SUBLANES, LANES), jnp.float32)
+        plain, weighted = lax.fori_loop(
+            0, depth, add_level, (zero[SUBLANES:], zero), unroll=8
+        )
+        return plain - weighted[SUBLANES:] + weighted[SUBLANES - 1 : SUBLANES - 1 + rows]
 
 
 def old_kernel(turned, whole, frac, volume, old, cells):
@@ -440,21 +477,35 @@
 
 
 def step_kernel(
-    turned, whole, frac, left, right, old, parts, update, near, cells, before, after, sems
+    turned, whole, frac, left_from, right_from, old, parts, update,
+    near, cells, left, right, before, after, sems, level_sems,
 ):
-    old_copy = pltpu.make_async_copy(old, before, sems.at[0])
-    old_copy.start()
+    old_copy = pltpu.make_async_copy(old, before, sems.at[0, 0])
     depth = cells.shape[0]
     tilts = near.shape[0]
-    tiles = right.shape[0] // tilts
-    own = right.shape[2] // LANES
+    tiles = right_from.shape[0] // tilts
+    own = right_from.shape[2] // LANES
     band = turned.band
+
+    def fetch(tilt):
+        block = pl.ds(tilt * tiles, tiles)
+        return [
+            pltpu.make_async_copy(source.at[block], target.at[block], sems.at[2 + n, tilt])
+            for n, (source, target) in enumerate(((left_from, left), (right_from, right)))
+        ]
+
+    for tilt in range(tilts):
+        for copy in fetch(tilt):
+            copy.start()
+    old_copy.start()
 
     def place(block, segment):
         return divmod(segment * turned.blocks + block, own)
 
     @pl.loop(0, tilts)
     def _(tilt):
+        for copy in fetch(tilt):
+            copy.wait()
         for block in range(turned.blocks):
             cut = []
             for segment in range(turned.segments):
@@ -467,38 +518,42 @@
                 else:
                     value = left[source]
                 cut.append(value)
-            turned.store(near, tilt, block * LANES, jnp.concatenate(cut, axis=0).T)
+            value = jnp.concatenate(cut, axis=0).T * (1.0 / tilts)
+            turned.store(near, tilt, block * LANES, value)
 
     rows = LANES // 2
+
+    def keep(level):
+        main = cells.at[level, pl.ds(turned.margin, turned.length), :]
+        return pltpu.make_async_copy(main, update.at[level], level_sems.at[level])
 
     @pl.loop(0, depth)
     def _(level):
         for at in range(0, turned.length, rows):
-            total = None
+            plain = weighted = None
             for tilt in range(tilts):
                 start = turned.margin + at + whole[tilt, level]
-                far = frac[tilt, level] / tilts
-                term = (1.0 / tilts - far) * near[tilt, pl.ds(start, rows), :] + (
-                    far * near[tilt, pl.ds(start + 1, rows), :]
-                )
-                total = term if total is None else total + term
-            turned.store(cells, level, at, total)
-
-    main = cells.at[:, pl.ds(turned.margin, turned.length), :]
-    update_copy = pltpu.make_async_copy(main, update, sems.at[1])
-    update_copy.start()
+                x = near[tilt, pl.ds(start, rows + SUBLANES), :]
+                y = frac[tilt, level] * x
+                plain = x[:rows] if plain is None else plain + x[:rows]
+                weighted = y if weighted is None else weighted + y
+            value = plain - weighted[:rows] + weighted[1 : 1 + rows]
+            turned.store(cells, level, at, value)
+        keep(level).start()
+
     old_copy.wait()
 
     def send(tilt):
         block = pl.ds(tilt * tiles, tiles)
-        return pltpu.make_async_copy(after.at[block], parts.at[block], sems.at[2 + tilt])
+        return pltpu.make_async_copy(after.at[block], parts.at[block], sems.at[1, tilt])
 
     @pl.loop(0, tilts)
     def _(tilt):
         for block in range(turned.blocks):
             at = block * LANES
-            total = turned.project(whole, frac, cells, tilt, at, LANES)
-            total = (total + before[tilt, at : at + LANES, :]).T
+            before[tilt, at : at + LANES, :] += turned.project(whole, frac, cells, tilt, at, LANES)
+        for block in range(turned.blocks):
+            total = before[tilt, block * LANES : (block + 1) * LANES, :].T
             for segment in range(turned.segments):
                 tile, column = place(block, segment)
                 after[tilt * tiles + tile, :, column * LANES : (column + 1) * LANES] = total[
@@ -509,17 +564,19 @@
 
     for tilt in range(tilts):
         send(tilt).wait()
-    update_copy.wait()
+    for level in range(depth):
+        keep(level).wait()
 
 
 def fresh_kernel(turned, volume, update, fresh):
-    for block in range(turned.blocks):
-        value = update[0, block * LANES : (block + 1) * LANES, :].T
-        for segment in range(turned.segments):
-            start = segment * turned.length + block * LANES
-            lanes = slice(start, start + LANES)
-            rows = slice(segment * turned.band, (segment + 1) * turned.band)
-            fresh[0, :, lanes] = volume[0, :, lanes] + value[rows]
+    for level in range(volume.shape[0]):
+        for block in range(turned.blocks):
+            value = update[level, block * LANES : (block + 1) * LANES, :].T
+            for segment in range(turned.segments):
+                start = segment * turned.length + block * LANES
+                lanes = slice(start, start + LANES)
+                rows = slice(segment * turned.band, (segment + 1) * turned.band)
+                fresh[level, :, lanes] = volume[level, :, lanes] + value[rows]
 
 
 def kernel_options(flops, size, share=1):
@@ -550,13 +607,16 @@
             jax.ShapeDtypeStruct(right.shape, jnp.float32),
             jax.ShapeDtypeStruct((depth, turned.length, LANES), jnp.float32),
         ),
-        in_specs=[SMEM, SMEM, VMEM, VMEM, HBM],
+        in_specs=[SMEM, SMEM, ANY, ANY, HBM],
         out_specs=(HBM, HBM),
         scratch_shapes=[
             turned.scratch(tilts), turned.scratch(depth),
+            pltpu.VMEM(left.shape, jnp.float32),
+            pltpu.VMEM(right.shape, jnp.float32),
             pltpu.VMEM(old.shape, jnp.float32),
             pltpu.VMEM(right.shape, jnp.float32),
-            pltpu.SemaphoreType.DMA((2 + tilts,)),
+            pltpu.SemaphoreType.DMA((4, tilts)),
+            pltpu.SemaphoreType.DMA((depth,)),
         ],
         name="volume_step",
         **kernel_options(16 * depth * old.size, 4 * depth * turned.length * LANES, 9 / 10),
@@ -565,11 +625,12 @@
 
 def fresh_volume(turned, volume, update):
     depth, band, columns = volume.shape
-    cells = pl.BlockSpec((1, band, columns), lambda i: (i, 0, 0))
-    flat = pl.BlockSpec((1, turned.length, LANES), lambda i: (i, 0, 0))
+    levels = math.gcd(depth, 4)
+    cells = pl.BlockSpec((levels, band, columns), lambda i: (i, 0, 0))
+    flat = pl.BlockSpec((levels, turned.length, LANES), lambda i: (i, 0, 0))
     return pl.pallas_call(
         functools.partial(fresh_kernel, turned),
-        grid=(depth,),
+        grid=(depth // levels,),
         out_shape=jax.ShapeDtypeStruct(volume.shape, jnp.float32),
         in_specs=[cells, flat],
         out_specs=cells,
@@ -597,20 +658,24 @@
 
     edge = passed_along(margins(*tile), "tile", -1)
     grad_left, begun, left = probe_phase(*within, tile, None, None, probe, intensity[0])
-    left, edge = lax.optimization_barrier((left, edge))
+    left, whole, frac = lax.optimization_barrier((left, whole, frac))
     left = exchanged(left.reshape(devices, band, LANES))
-    grad_right, early, late, right = probe_phase(*within, tile, edge, begun, probe, intensity[0])
-    right, whole = lax.optimization_barrier((right, whole))
+    grad_right, early, late, relayed, right = probe_phase(*within, tile, edge, begun, probe, intensity[0])
+    right, left, whole = lax.optimization_barrier((right, left, whole))
     right = exchanged(right.reshape(devices, band, width))
     old = old_projection(turned, whole, frac, volume)
     right, early, old = lax.optimization_barrier((right, early, old))
     early = passed_along(early, "tile", 1)
     parts, update = volume_step(turned, whole, frac, left, right, old)
-    parts, early, late = lax.optimization_barrier((parts, early, late))
+    parts, early, late, relayed = lax.optimization_barrier((parts, early, late, relayed))
     late = passed_along(late, "tile", 1)
+    straight = passed_by(relayed, "tile", 0, 1)
+    relayed = passed_by(relayed, "tile", 1, -1)
     returned = exchanged(parts)
     fresh = fresh_volume(turned, volume, update)
-    spill = jnp.concatenate([early, late], axis=1)
+    relayed, fresh = lax.optimization_barrier((relayed, fresh))
+    relayed = straight + passed_by(relayed, "tile", 0, 2)
+    spill = jnp.concatenate([early, late, relayed], axis=1)
     grad = jnp.concatenate([grad_left + spill, grad_right], axis=2)[:, None]
     reprojection = jnp.roll(returned.reshape(height, width), -row_shift[0], axis=0)[None]
     return (fresh, reprojection, grad)

time: 213 us -> 161 us (0.76); the launches traced: 213 us -> 159 us
  blocking collectives: 46.6 us -> 0 us
  Pallas kernels: 94.2 us -> 58 us
  starting transfers between devices: 20.5 us -> 48.3 us
    all_to_all x1 -> x0, blocking collectives: 46.6 us -> none  [exchanged(): return lax.all_to_all(blocks, axes, split_axis=0, concat_axis=0, tiled=True)]
    ppermute x3, waiting for transfers between devices: 41.3 us -> 1.29 us  [passed_along(): return lax.ppermute(block, axis, route)]
    pallas_call x2, Pallas kernels: 46.1 us -> 8.2 us  [the longest x1 8.11 us: fresh_volume(): pl.pallas_call(functools.partial(fresh_kernel, turned), grid=(depth // le...]
    all_to_all x2 -> x3, waiting for transfers between devices: 0.01 us -> 20.9 us  [exchanged(): return lax.all_to_all(blocks, axes, split_axis=0, concat_axis=0, tiled=True)]
    ppermute x0 -> x3, waiting for transfers between devices: none -> 17.6 us  [passed_by(): return lax.ppermute(block, axis, route)]
    all_to_all x2 -> x3, starting transfers between devices: 11.2 us -> 26.3 us  [exchanged(): return lax.all_to_all(blocks, axes, split_axis=0, concat_axis=0, tiled=True)]
    ppermute x0 -> x3, starting transfers between devices: none -> 12.5 us  [passed_by(): return lax.ppermute(block, axis, route)]
    pallas_call x2, Pallas kernels: 18 us -> 23.6 us  [probe_phase(): pl.pallas_call(functools.partial(probe_kernel, base=base, beyond=beyond),...]
  transfers between devices with their start and end apart: 5 -> 9, of which waited for: 2 -> 5; matrix products, arithmetic and copies ran while one was open for 2% -> 3% of each run, Pallas kernels for 24% -> 36%
where the time goes in v3:
time: 161 us; the launch traced here: 159 us
  Pallas kernels  58 us (36%)
  starting transfers between devices  48.3 us (30%)
  waiting for transfers between devices  39.8 us (25%)
  other arithmetic  6.25 us (4%)
  local copies, waits for them, and re-layouts  4.48 us (3%)
  between operations  2.19 us (1%)
    all_to_all x3, starting transfers between devices, exchanged(): return lax.all_to_all(blocks, axes, split_axis=0, concat_axis=0, tiled=True)  26.3 us
    pallas_call x2, Pallas kernels, probe_phase(): pl.pallas_call(functools.partial(probe_kernel, base=base, beyond=beyond),...  23.6 us
    all_to_all x3, waiting for transfers between devices, exchanged(): return lax.all_to_all(blocks, axes, split_axis=0, concat_axis=0, tiled=True)  20.9 us
    ppermute x3, waiting for transfers between devices, passed_by(): return lax.ppermute(block, axis, route)  17.6 us
    pallas_call x1, Pallas kernels, volume_step(): pl.pallas_call(functools.partial(step_kernel, turned), out_shape=(jax.Sha...  13.3 us
    pallas_call x1, Pallas kernels, old_projection(): pl.pallas_call(functools.partial(old_kernel, turned), out_shape=jax.Shape...  13 us
    ppermute x3, starting transfers between devices, passed_by(): return lax.ppermute(block, axis, route)  12.5 us
    ppermute x3, starting transfers between devices, passed_along(): return lax.ppermute(block, axis, route)  9.48 us
  transfers between devices with their start and end apart: 9, of which 5 were waited for; matrix products, arithmetic and copies ran while one was open for 3% of the time, Pallas kernels for 36%

profile of v3, /device:TPU:17, one launch (start us, length us, event | category | flops | bytes accessed | tf_op | source)
XLA Modules:
  0.0 159.1 jit_solution(13629848564324739109)
XLA Ops:
  0.6 0.0 copy-start
  0.6 1.4 copy-done
  2.0 0.0 copy-start.1
  2.0 1.4 copy-done.1
  3.5 0.1 margins.1
  3.6 3.0 %collective-permute-start = (f32[2,1024,128]{2,1,0:T(8,128)S(1)}, f32[2,1024,128]{2,1,0:T(8,128)S(1)}, u32[]{:S(2)}, u32[]{:S(2)}) collective-permute-start(f32[2,1024,128]{2,1,0:T(8,128)S(1)} %margins.1), channel_id=1, source_target_pairs={{1,0},{2,1},{3,2},{4,3},{5,4},{6,5},{7,6},{9,8},{10,9},{11,10},{12... | collective-permute-start | bytes 3145736 | tf_op jit(solution)/shard_map/ppermute | solution.py:27
  6.6 0.0 copy-done.6
  6.6 0.6 add_select_fusion.whole
  7.2 0.6 convert_multiply_fusion.frac
  8.5 0.0 copy-done.7
  8.5 0.7 copy.18.positions_ref
  9.8 11.6 %probes_within.1 = (f32[2,1024,128]{2,1,0:T(8,128)}, f32[2,2,1024,128]{3,2,1,0:T(8,128)}, f32[1024,128]{1,0:T(8,128)}) custom-call(s32[1,1]{1,0:T(1,128)S(6)} %copy.20.used_ref, s32[8,2]{1,0:T(8,128)} %copy.18.positions_ref, s32[1]{0:T(128)} %copy.21.shift_ref, f32[1024,384]{1,0:T(8,128)} %bitcast.16, f32[1024,384]{1,0:T(8,128)} %bitcast.19, ...), custom_call_target="tpu_custom_call" | custom-call | flops 3489660928 | bytes 6291456 | tf_op jit(solution)/shard_map/probes_within/pallas_call | solution.py:385
  21.4 7.7 %all-to-all-start = ((f32[32,32,128]{2,1,0:T(8,128)}), f32[32,32,128]{2,1,0:T(8,128)S(1)}, u32[]{:S(2)}, u32[]{:S(2)}) async-start(f32[32,32,128]{2,1,0:T(8,128)} %bitcast.24), calls=%async_computation | async-start | bytes 1048576 | tf_op jit(solution)/shard_map/all_to_all | solution.py:657
  29.1 0.3 collective-permute-done.refs_2_
  29.5 1.0 copy-done.8
  30.4 12.0 %probes_beyond.1 = (f32[2,1024,256]{2,1,0:T(8,128)}, f32[2,576,128]{2,1,0:T(8,128)}, f32[2,224,128]{2,1,0:T(8,128)}, f32[2,224,128]{2,1,0:T(8,128)}, f32[1024,384]{1,0:T(8,128)}) custom-call(s32[1,1]{1,0:T(1,128)S(6)} %copy.20.used_ref, s32[8,2]{1,0:T(8,128)} %copy.18.positions_ref, s32[1]{0:T(128)} %copy.21.shift_ref, f32[1024,384]{1,0:T(8,128)} %bitcast.17, ...), custom_call_target="tpu_custom_call" | custom-call | flops 3489660928 | bytes 6291456 | tf_op jit(solution)/shard_map/probes_beyond/pallas_call | solution.py:385
  42.4 0.0 all-to-all-done.left_from
  42.5 0.0 copy-start.4
  42.5 11.1 %all-to-all-start.1 = ((f32[32,32,384]{2,1,0:T(8,128)}), f32[32,32,384]{2,1,0:T(8,128)S(1)}, u32[]{:S(2)}, u32[]{:S(2)}) async-start(f32[32,32,384]{2,1,0:T(8,128)} %bitcast.23), calls=%async_computation.1 | async-start | bytes 3145728 | tf_op jit(solution)/shard_map/all_to_all | solution.py:657
  53.6 0.0 copy-start.9
  53.6 13.0 %old_projection.1.old = f32[4,768,128]{2,1,0:T(8,128)} custom-call(s32[4,16]{1,0:T(4,128)} %add_select_fusion.whole, f32[4,16]{1,0:T(4,128)} %convert_multiply_fusion.frac, f32[16,32,3072]{2,1,0:T(8,128)} %volume.3), custom_call_target="tpu_custom_call" | custom-call | flops 50331648 | bytes 6291456 | tf_op jit(solution)/shard_map/old_projection/pallas_call | solution.py:591
  66.6 0.0 copy-done.4
  66.6 20.9 %all-to-all-done.1.right_from = f32[32,32,384]{2,1,0:T(8,128)S(1)} async-done(((f32[32,32,384]{2,1,0:T(8,128)}), f32[32,32,384]{2,1,0:T(8,128)S(1)}, u32[]{:S(2)}, u32[]{:S(2)}) %all-to-all-start.1) | async-done | bytes 1572896 | tf_op jit(solution)/shard_map/all_to_all | solution.py:657
  87.5 0.0 copy-done.9
  87.5 4.5 %collective-permute-start.1 = (f32[2,576,128]{2,1,0:T(8,128)S(1)}, f32[2,576,128]{2,1,0:T(8,128)}, u32[]{:S(2)}, u32[]{:S(2)}) collective-permute-start(f32[2,576,128]{2,1,0:T(8,128)S(1)} %copy-done.9), channel_id=1, source_target_pairs={{0,1},{1,2},{2,3},{3,4},{4,5},{5,6},{6,7},{8,9},{9,10},{10,11},{11... | collective-permute-start | bytes 1769480 | tf_op jit(solution)/shard_map/ppermute | solution.py:27
  92.1 0.0 copy-done.2
  92.1 13.3 %volume_step.1 = (f32[32,32,384]{2,1,0:T(8,128)}, f32[16,768,128]{2,1,0:T(8,128)}) custom-call(s32[4,16]{1,0:T(4,128)} %add_select_fusion.whole, f32[4,16]{1,0:T(4,128)} %convert_multiply_fusion.frac, f32[32,32,128]{2,1,0:T(8,128)} %copy-done.4, f32[32,32,384]{2,1,0:T(8,128)} %copy-done.2, f32[4,768,128]{2,1,0:T(8,128)} %old_projection.1.old), custom_call_target="tpu_custom_call" | custom-call | flops 100663296 | bytes 6291456 | tf_op jit(solution)/shard_map/volume_step/pallas_call | solution.py:604
  105.3 0.0 collective-permute-done.1
  105.4 7.5 %all-to-all-start.2 = ((f32[32,32,384]{2,1,0:T(8,128)}), f32[32,32,384]{2,1,0:T(8,128)S(1)}, u32[]{:S(2)}, u32[]{:S(2)}) async-start(f32[32,32,384]{2,1,0:T(8,128)} %get-tuple-element.47), calls=%async_computation.2 | async-start | bytes 3145728 | tf_op jit(solution)/shard_map/all_to_all | solution.py:657
  112.9 1.3 collective-permute-start.2
  114.2 0.0 copy-start.10
  114.2 0.0 copy-start.5
  114.2 8.1 %fresh_volume.1 = f32[16,32,3072]{2,1,0:T(8,128)} custom-call(f32[16,32,3072]{2,1,0:T(8,128)} %volume.3, f32[16,768,128]{2,1,0:T(8,128)} %get-tuple-element.45.update), custom_call_target="tpu_custom_call" | custom-call | flops 1572864 | bytes 18874368 | tf_op jit(solution)/shard_map/fresh_volume/pallas_call | solution.py:631
  122.3 4.7 %collective-permute-start.4 = (f32[2,224,128]{2,1,0:T(8,128)}, f32[2,224,128]{2,1,0:T(8,128)S(1)}, u32[]{:S(2)}, u32[]{:S(2)}) collective-permute-start(f32[2,224,128]{2,1,0:T(8,128)} %get-tuple-element.44), channel_id=1, source_target_pairs={{0,1},{2,3},{4,5},{6,7},{8,9},{10,11},{12,13},{14,15},{16,17},{18,... | collective-permute-start | bytes 688136 | tf_op jit(solution)/shard_map/ppermute | solution.py:33
  127.0 2.5 %collective-permute-done.2 = f32[2,224,128]{2,1,0:T(8,128)} collective-permute-done((f32[2,224,128]{2,1,0:T(8,128)}, f32[2,224,128]{2,1,0:T(8,128)}, u32[]{:S(2)}, u32[]{:S(2)}) %collective-permute-start.2) | collective-permute-done | bytes 229408 | tf_op jit(solution)/shard_map/ppermute | solution.py:33
  129.5 6.5 %collective-permute-start.5 = (f32[2,224,128]{2,1,0:T(8,128)}, f32[2,224,128]{2,1,0:T(8,128)S(1)}, u32[]{:S(2)}, u32[]{:S(2)}) collective-permute-start(f32[2,224,128]{2,1,0:T(8,128)} %collective-permute-done.2), channel_id=1, source_target_pairs={{0,2},{2,4},{4,6},{8,10},{10,12},{12,14},{16,18},{18,20},{20,22},{... | collective-permute-start | bytes 688136 | tf_op jit(solution)/shard_map/ppermute | solution.py:33
  136.0 0.0 copy-done.10
  136.1 1.9 %collective-permute-start.3 = (f32[2,224,128]{2,1,0:T(8,128)S(1)}, f32[2,224,128]{2,1,0:T(8,128)S(1)}, u32[]{:S(2)}, u32[]{:S(2)}) collective-permute-start(f32[2,224,128]{2,1,0:T(8,128)S(1)} %copy-done.10), channel_id=1, source_target_pairs={{0,1},{1,2},{2,3},{3,4},{4,5},{5,6},{6,7},{8,9},{9,10},{10,11},{11... | collective-permute-start | bytes 688136 | tf_op jit(solution)/shard_map/ppermute | solution.py:27
  138.0 0.0 copy-start.3
  138.0 0.0 collective-permute-done.4
  138.0 15.0 %collective-permute-done.5 = f32[2,224,128]{2,1,0:T(8,128)S(1)} collective-permute-done((f32[2,224,128]{2,1,0:T(8,128)}, f32[2,224,128]{2,1,0:T(8,128)S(1)}, u32[]{:S(2)}, u32[]{:S(2)}) %collective-permute-start.5) | collective-permute-done | bytes 229408 | tf_op jit(solution)/shard_map/ppermute | solution.py:33
  153.1 0.9 collective-permute-done.3
  154.0 0.0 copy-done.5
  154.0 1.2 maximum_add_fusion
  155.2 0.0 copy-done.3
  155.2 1.9 %maximum_bitcast_fusion = f32[2,1,1024,384]{3,2,1,0:T(8,128)} fusion(f32[2,1024,256]{2,1,0:T(8,128)S(1)} %copy-done.3, f32[2,1024,128]{2,1,0:T(8,128)S(1)} %maximum_add_fusion), kind=kLoop, calls=%fused_computation.2 | loop fusion | flops 786432 | bytes 6291456
  157.1 0.0 all-to-all-done.2
  157.1 2.0 %fusion.1 = f32[1,1024,384]{2,1,0:T(8,128)} fusion(s32[]{:T(128)S(6)} %select_n.20, f32[1024,384]{1,0:T(8,128)S(1)} %bitcast.22), kind=kLoop, calls=%fused_computation.4 | loop fusion | flops 393216 | bytes 3145732 | tf_op jit(solution)/shard_map/broadcast_in_dim | solution.py:680
  (5 shorter events, 0.0 us)
Async XLA Ops:
  0.6 1.4 copy-start
  2.0 1.4 copy-start.1
  3.5 3.1 %copy-start.6 = (s32[4]{0:T(128)S(1)}, s32[4]{0:T(128)}, u32[]{:S(2)}) copy-start(s32[4]{0:T(128)} %param.22) | copy-start | bytes 52
  3.5 5.0 %copy-start.7 = (s32[1,8,2]{1,2,0:T(2,128)S(1)}, s32[1,8,2]{1,2,0:T(2,128)}, u32[]{:S(2)}) copy-start(s32[1,8,2]{1,2,0:T(2,128)} %param.19) | copy-start | bytes 196
  3.6 25.9 %collective-permute-start = (f32[2,1024,128]{2,1,0:T(8,128)S(1)}, f32[2,1024,128]{2,1,0:T(8,128)S(1)}, u32[]{:S(2)}, u32[]{:S(2)}) collective-permute-start(f32[2,1024,128]{2,1,0:T(8,128)S(1)} %margins.1), channel_id=1, source_target_pairs={{1,0},{2,1},{3,2},{4,3},{5,4},{6,5},{7,6},{9,8},{10,9},{11,10},{12... | collective-permute-start | bytes 3145736 | tf_op jit(solution)/shard_map/ppermute | solution.py:27
  21.4 21.1 %all-to-all-start = ((f32[32,32,128]{2,1,0:T(8,128)}), f32[32,32,128]{2,1,0:T(8,128)S(1)}, u32[]{:S(2)}, u32[]{:S(2)}) async-start(f32[32,32,128]{2,1,0:T(8,128)} %bitcast.24), calls=%async_computation | async-start | bytes 1048576 | tf_op jit(solution)/shard_map/all_to_all | solution.py:657
  29.5 1.0 copy-start.8
  42.5 24.1 %copy-start.4 = (f32[32,32,128]{2,1,0:T(8,128)}, f32[32,32,128]{2,1,0:T(8,128)S(1)}, u32[]{:S(2)}) copy-start(f32[32,32,128]{2,1,0:T(8,128)S(1)} %all-to-all-done.left_from) | copy-start | bytes 1572868
  42.5 45.1 %all-to-all-start.1 = ((f32[32,32,384]{2,1,0:T(8,128)}), f32[32,32,384]{2,1,0:T(8,128)S(1)}, u32[]{:S(2)}, u32[]{:S(2)}) async-start(f32[32,32,384]{2,1,0:T(8,128)} %bitcast.23), calls=%async_computation.1 | async-start | bytes 3145728 | tf_op jit(solution)/shard_map/all_to_all | solution.py:657
  53.6 33.9 %copy-start.9 = (f32[2,576,128]{2,1,0:T(8,128)S(1)}, f32[2,576,128]{2,1,0:T(8,128)}, u32[]{:S(2)}) copy-start(f32[2,576,128]{2,1,0:T(8,128)} %get-tuple-element.41) | copy-start | bytes 1769476
  87.5 4.5 %copy-start.2 = (f32[32,32,384]{2,1,0:T(8,128)}, f32[32,32,384]{2,1,0:T(8,128)S(1)}, u32[]{:S(2)}) copy-start(f32[32,32,384]{2,1,0:T(8,128)S(1)} %all-to-all-done.1.right_from) | copy-start | bytes 4718596
  87.5 17.8 %collective-permute-start.1 = (f32[2,576,128]{2,1,0:T(8,128)S(1)}, f32[2,576,128]{2,1,0:T(8,128)}, u32[]{:S(2)}, u32[]{:S(2)}) collective-permute-start(f32[2,576,128]{2,1,0:T(8,128)S(1)} %copy-done.9), channel_id=1, source_target_pairs={{0,1},{1,2},{2,3},{3,4},{4,5},{5,6},{6,7},{8,9},{9,10},{10,11},{11... | collective-permute-start | bytes 1769480 | tf_op jit(solution)/shard_map/ppermute | solution.py:27
  105.4 51.7 %all-to-all-start.2 = ((f32[32,32,384]{2,1,0:T(8,128)}), f32[32,32,384]{2,1,0:T(8,128)S(1)}, u32[]{:S(2)}, u32[]{:S(2)}) async-start(f32[32,32,384]{2,1,0:T(8,128)} %get-tuple-element.47), calls=%async_computation.2 | async-start | bytes 3145728 | tf_op jit(solution)/shard_map/all_to_all | solution.py:657
  112.9 16.6 %collective-permute-start.2 = (f32[2,224,128]{2,1,0:T(8,128)}, f32[2,224,128]{2,1,0:T(8,128)}, u32[]{:S(2)}, u32[]{:S(2)}) collective-permute-start(f32[2,224,128]{2,1,0:T(8,128)} %get-tuple-element.44), channel_id=1, source_target_pairs={{1,0},{3,2},{5,4},{7,6},{9,8},{11,10},{13,12},{15,14},{17,16},{19,... | collective-permute-start | bytes 688136 | tf_op jit(solution)/shard_map/ppermute | solution.py:33
  114.2 21.9 %copy-start.10 = (f32[2,224,128]{2,1,0:T(8,128)S(1)}, f32[2,224,128]{2,1,0:T(8,128)}, u32[]{:S(2)}) copy-start(f32[2,224,128]{2,1,0:T(8,128)} %get-tuple-element.50) | copy-start | bytes 688132
  114.2 39.8 %copy-start.5 = (f32[2,1024,128]{2,1,0:T(8,128)S(1)}, f32[2,1024,128]{2,1,0:T(8,128)}, u32[]{:S(2)}) copy-start(f32[2,1024,128]{2,1,0:T(8,128)} %get-tuple-element.48) | copy-start | bytes 3145732
  122.3 15.7 %collective-permute-start.4 = (f32[2,224,128]{2,1,0:T(8,128)}, f32[2,224,128]{2,1,0:T(8,128)S(1)}, u32[]{:S(2)}, u32[]{:S(2)}) collective-permute-start(f32[2,224,128]{2,1,0:T(8,128)} %get-tuple-element.44), channel_id=1, source_target_pairs={{0,1},{2,3},{4,5},{6,7},{8,9},{10,11},{12,13},{14,15},{16,17},{18,... | collective-permute-start | bytes 688136 | tf_op jit(solution)/shard_map/ppermute | solution.py:33
  129.5 23.6 %collective-permute-start.5 = (f32[2,224,128]{2,1,0:T(8,128)}, f32[2,224,128]{2,1,0:T(8,128)S(1)}, u32[]{:S(2)}, u32[]{:S(2)}) collective-permute-start(f32[2,224,128]{2,1,0:T(8,128)} %collective-permute-done.2), channel_id=1, source_target_pairs={{0,2},{2,4},{4,6},{8,10},{10,12},{12,14},{16,18},{18,20},{20,22},{... | collective-permute-start | bytes 688136 | tf_op jit(solution)/shard_map/ppermute | solution.py:33
  136.1 18.0 %collective-permute-start.3 = (f32[2,224,128]{2,1,0:T(8,128)S(1)}, f32[2,224,128]{2,1,0:T(8,128)S(1)}, u32[]{:S(2)}, u32[]{:S(2)}) collective-permute-start(f32[2,224,128]{2,1,0:T(8,128)S(1)} %copy-done.10), channel_id=1, source_target_pairs={{0,1},{1,2},{2,3},{3,4},{4,5},{5,6},{6,7},{8,9},{9,10},{10,11},{11... | collective-permute-start | bytes 688136 | tf_op jit(solution)/shard_map/ppermute | solution.py:27
  138.0 17.2 %copy-start.3 = (f32[2,1024,256]{2,1,0:T(8,128)S(1)}, f32[2,1024,256]{2,1,0:T(8,128)}, u32[]{:S(2)}) copy-start(f32[2,1024,256]{2,1,0:T(8,128)} %get-tuple-element.52) | copy-start | bytes 6291460

commit v4 on v3

--- a/solution.py
+++ b/solution.py
@@ -333,14 +333,22 @@
         copy.wait()
 
 
-def margin_kernel(tile_re, tile_im, out, sems):
-    copies = [
-        pltpu.make_async_copy(tile.at[:, pl.ds(0, LANES)], out.at[part], sems.at[part])
-        for part, tile in enumerate((tile_re, tile_im))
-    ]
-    for copy in copies:
+def margin_kernel(tile_re, tile_im, out, held, sems):
+    height = tile_re.shape[0]
+    first, second = [], []
+    for n, tile in enumerate((tile_re, tile_im)):
+        for part in range(2):
+            rows = pl.ds(part * height // 2, height // 2)
+            source = tile.at[rows, pl.ds(0, LANES)]
+            sem = sems.at[2 * n + part]
+            first.append(pltpu.make_async_copy(source, held.at[n, rows], sem))
+            second.append(pltpu.make_async_copy(held.at[n, rows], out.at[n, rows], sem))
+    for copy in first:
         copy.start()
-    for copy in copies:
+    for before, after in zip(first, second):
+        before.wait()
+        after.start()
+    for copy in second:
         copy.wait()
 
 
@@ -350,9 +358,9 @@
         margin_kernel,
         out_shape=jax.ShapeDtypeStruct(shape, jnp.float32),
         in_specs=[HBM, HBM],
-        out_specs=VMEM,
-        scratch_shapes=[pltpu.SemaphoreType.DMA((2,))],
-        compiler_params=pltpu.CompilerParams(vmem_limit_bytes=VMEM_BYTES // 4),
+        out_specs=HBM,
+        scratch_shapes=[pltpu.VMEM(shape, jnp.float32), pltpu.SemaphoreType.DMA((4,))],
+        compiler_params=pltpu.CompilerParams(vmem_limit_bytes=VMEM_BYTES),
         name="margins",
     )(tile_re, tile_im)
 
@@ -673,10 +681,13 @@
     relayed = passed_by(relayed, "tile", 1, -1)
     returned = exchanged(parts)
     fresh = fresh_volume(turned, volume, update)
-    relayed, fresh = lax.optimization_barrier((relayed, fresh))
+    rows = early.shape[1]
+    early = jnp.pad(early, ((0, 0), (0, height - rows), (0, 0)))
+    grad = jnp.concatenate([grad_left + early, grad_right], axis=2)[:, None]
+    relayed, fresh, grad = lax.optimization_barrier((relayed, fresh, grad))
     relayed = straight + passed_by(relayed, "tile", 0, 2)
-    spill = jnp.concatenate([early, late, relayed], axis=1)
-    grad = jnp.concatenate([grad_left + spill, grad_right], axis=2)[:, None]
+    late = jnp.concatenate([late, relayed], axis=1)
+    grad = grad.at[:, 0, rows:, :LANES].add(late)
     reprojection = jnp.roll(returned.reshape(height, width), -row_shift[0], axis=0)[None]
     return (fresh, reprojection, grad)
 

time: 161 us -> 155 us (0.963); the launches traced: 159 us -> 155 us
  waiting for transfers between devices: 39.8 us -> 43.9 us
  Pallas kernels: 58 us -> 54.5 us
  local copies, waits for them, and re-layouts: 4.48 us -> 1.66 us
  starting transfers between devices: 48.3 us -> 45.7 us
    pallas_call x2, Pallas kernels: 23.6 us -> 18.2 us  [probe_phase(): pl.pallas_call(functools.partial(probe_kernel, base=base, beyond=beyond),...]
    all_to_all x3, waiting for transfers between devices: 20.9 us -> 23.9 us  [exchanged(): return lax.all_to_all(blocks, axes, split_axis=0, concat_axis=0, tiled=True)]
    unnamed x22 -> x16, local copies, waits for them, and re-layouts: 3.81 us -> 1 us
    ppermute x3, starting transfers between devices: 12.5 us -> 10.6 us  [passed_by(): return lax.ppermute(block, axis, route)]
    broadcast_in_dim x0 -> x1, other arithmetic: none -> 1.87 us  [local(): grad = jnp.concatenate([grad_left + early, grad_right], axis=2)[:, None]]
    unnamed x1 -> x0, other arithmetic: 1.87 us -> none
    pallas_call x1, Pallas kernels: 0.09 us -> 1.96 us  [margins(): pl.pallas_call(margin_kernel, out_shape=jax.ShapeDtypeStruct(shape, jnp.f...]
    scatter-add x0 -> x1, other arithmetic: none -> 1.85 us  [local(): grad = grad.at[:, 0, rows:, :LANES].add(late)]
  transfers between devices with their start and end apart: 9 -> 9, of which waited for: 5 -> 6; matrix products, arithmetic and copies ran while one was open for 3% -> 4% of each run, Pallas kernels for 36% -> 34%
where the time goes in v4:
time: 155 us
  Pallas kernels  54.5 us (35%)
  starting transfers between devices  45.7 us (29%)
  waiting for transfers between devices  43.9 us (28%)
  other arithmetic  7.04 us (5%)
  between operations  2.18 us (1%)
  local copies, waits for them, and re-layouts  1.66 us (1%)
    all_to_all x3, starting transfers between devices, exchanged(): return lax.all_to_all(blocks, axes, split_axis=0, concat_axis=0, tiled=True)  25.7 us
    all_to_all x3, waiting for transfers between devices, exchanged(): return lax.all_to_all(blocks, axes, split_axis=0, concat_axis=0, tiled=True)  23.9 us
    pallas_call x2, Pallas kernels, probe_phase(): pl.pallas_call(functools.partial(probe_kernel, base=base, beyond=beyond),...  18.2 us
    ppermute x3, waiting for transfers between devices, passed_by(): return lax.ppermute(block, axis, route)  17.5 us
    pallas_call x1, Pallas kernels, volume_step(): pl.pallas_call(functools.partial(step_kernel, turned), out_shape=(jax.Sha...  13.3 us
    pallas_call x1, Pallas kernels, old_projection(): pl.pallas_call(functools.partial(old_kernel, turned), out_shape=jax.Shape...  12.9 us
    ppermute x3, starting transfers between devices, passed_by(): return lax.ppermute(block, axis, route)  10.6 us
    ppermute x3, starting transfers between devices, passed_along(): return lax.ppermute(block, axis, route)  9.48 us
  transfers between devices with their start and end apart: 9, of which 6 were waited for; matrix products, arithmetic and copies ran while one was open for 4% of the time, Pallas kernels for 34%

profile of v4, /device:TPU:17, one launch (start us, length us, event | category | flops | bytes accessed | tf_op | source)
XLA Modules:
  0.0 155.0 jit_solution(9771634852732647226)
XLA Ops:
  0.6 0.0 copy-start.4
  0.6 0.0 copy-start.5
  0.7 2.0 %margins.1 = f32[2,1024,128]{2,1,0:T(8,128)} custom-call(f32[1024,384]{1,0:T(8,128)} %bitcast.24, f32[1024,384]{1,0:T(8,128)} %bitcast.27), custom_call_target="tpu_custom_call" | custom-call | tf_op jit(solution)/shard_map/margins/pallas_call | solution.py:357
  2.6 3.0 %collective-permute-start = (f32[2,1024,128]{2,1,0:T(8,128)}, f32[2,1024,128]{2,1,0:T(8,128)S(1)}, u32[]{:S(2)}, u32[]{:S(2)}) collective-permute-start(f32[2,1024,128]{2,1,0:T(8,128)} %margins.1), channel_id=1, source_target_pairs={{1,0},{2,1},{3,2},{4,3},{5,4},{6,5},{7,6},{9,8},{10,9},{11,10},{12... | collective-permute-start | bytes 3145736 | tf_op jit(solution)/shard_map/ppermute | solution.py:27
  5.7 0.0 copy-done.4
  5.7 0.6 add_select_fusion.whole
  6.3 0.6 convert_multiply_fusion.frac
  7.5 0.0 copy-done.5
  7.5 0.7 copy.18.positions_ref
  8.9 10.7 %probes_within.1 = (f32[2,1024,128]{2,1,0:T(8,128)}, f32[2,2,1024,128]{3,2,1,0:T(8,128)}, f32[1024,128]{1,0:T(8,128)}) custom-call(s32[1,1]{1,0:T(1,128)S(6)} %copy.21.used_ref, s32[8,2]{1,0:T(8,128)} %copy.18.positions_ref, s32[1]{0:T(128)} %copy.22.shift_ref, f32[1024,384]{1,0:T(8,128)} %bitcast.25, f32[1024,384]{1,0:T(8,128)} %bitcast.28, ...), custom_call_target="tpu_custom_call" | custom-call | flops 3489660928 | bytes 6291456 | tf_op jit(solution)/shard_map/probes_within/pallas_call | solution.py:393
  19.6 7.6 %all-to-all-start = ((f32[32,32,128]{2,1,0:T(8,128)}), f32[32,32,128]{2,1,0:T(8,128)S(1)}, u32[]{:S(2)}, u32[]{:S(2)}) async-start(f32[32,32,128]{2,1,0:T(8,128)} %bitcast.30), calls=%async_computation | async-start | bytes 1048576 | tf_op jit(solution)/shard_map/all_to_all | solution.py:665
  27.2 1.6 %collective-permute-done.refs_2_ = f32[2,1024,128]{2,1,0:T(8,128)S(1)} collective-permute-done((f32[2,1024,128]{2,1,0:T(8,128)}, f32[2,1024,128]{2,1,0:T(8,128)S(1)}, u32[]{:S(2)}, u32[]{:S(2)}) %collective-permute-start) | collective-permute-done | bytes 1048608 | tf_op jit(solution)/shard_map/ppermute | solution.py:27
  28.7 0.0 copy-start.6
  28.7 1.0 copy-done.6
  29.7 7.5 %probes_beyond.1 = (f32[2,1024,256]{2,1,0:T(8,128)}, f32[2,576,128]{2,1,0:T(8,128)}, f32[2,224,128]{2,1,0:T(8,128)}, f32[2,224,128]{2,1,0:T(8,128)}, f32[1024,384]{1,0:T(8,128)}) custom-call(s32[1,1]{1,0:T(1,128)S(6)} %copy.21.used_ref, s32[8,2]{1,0:T(8,128)} %copy.18.positions_ref, s32[1]{0:T(128)} %copy.22.shift_ref, f32[1024,384]{1,0:T(8,128)} %bitcast.26, ...), custom_call_target="tpu_custom_call" | custom-call | flops 3489660928 | bytes 6291456 | tf_op jit(solution)/shard_map/probes_beyond/pallas_call | solution.py:393
  37.3 2.9 %all-to-all-done.left_from = f32[32,32,128]{2,1,0:T(8,128)S(1)} async-done(((f32[32,32,128]{2,1,0:T(8,128)}), f32[32,32,128]{2,1,0:T(8,128)S(1)}, u32[]{:S(2)}, u32[]{:S(2)}) %all-to-all-start) | async-done | bytes 524320 | tf_op jit(solution)/shard_map/all_to_all | solution.py:665
  40.1 0.0 copy-start.2
  40.1 10.5 %all-to-all-start.1 = ((f32[32,32,384]{2,1,0:T(8,128)}), f32[32,32,384]{2,1,0:T(8,128)S(1)}, u32[]{:S(2)}, u32[]{:S(2)}) async-start(f32[32,32,384]{2,1,0:T(8,128)} %bitcast.23), calls=%async_computation.1 | async-start | bytes 3145728 | tf_op jit(solution)/shard_map/all_to_all | solution.py:665
  50.6 12.9 %old_projection.1.old = f32[4,768,128]{2,1,0:T(8,128)} custom-call(s32[4,16]{1,0:T(4,128)} %add_select_fusion.whole, f32[4,16]{1,0:T(4,128)} %convert_multiply_fusion.frac, f32[16,32,3072]{2,1,0:T(8,128)} %volume.3), custom_call_target="tpu_custom_call" | custom-call | flops 50331648 | bytes 6291456 | tf_op jit(solution)/shard_map/old_projection/pallas_call | solution.py:599
  63.5 0.0 copy-done.2
  63.5 21.0 %all-to-all-done.1.right_from = f32[32,32,384]{2,1,0:T(8,128)S(1)} async-done(((f32[32,32,384]{2,1,0:T(8,128)}), f32[32,32,384]{2,1,0:T(8,128)S(1)}, u32[]{:S(2)}, u32[]{:S(2)}) %all-to-all-start.1) | async-done | bytes 1572896 | tf_op jit(solution)/shard_map/all_to_all | solution.py:665
  84.5 0.0 copy-start
  84.5 4.5 %collective-permute-start.1 = (f32[2,576,128]{2,1,0:T(8,128)}, f32[2,576,128]{2,1,0:T(8,128)S(1)}, u32[]{:S(2)}, u32[]{:S(2)}) collective-permute-start(f32[2,576,128]{2,1,0:T(8,128)} %get-tuple-element.54), channel_id=1, source_target_pairs={{0,1},{1,2},{2,3},{3,4},{4,5},{5,6},{6,7},{8,9},{9,10},{10,11},{11... | collective-permute-start | bytes 1769480 | tf_op jit(solution)/shard_map/ppermute | solution.py:27
  89.1 0.0 copy-done
  89.1 13.3 %volume_step.1 = (f32[32,32,384]{2,1,0:T(8,128)}, f32[16,768,128]{2,1,0:T(8,128)}) custom-call(s32[4,16]{1,0:T(4,128)} %add_select_fusion.whole, f32[4,16]{1,0:T(4,128)} %convert_multiply_fusion.frac, f32[32,32,128]{2,1,0:T(8,128)} %copy-done.2, f32[32,32,384]{2,1,0:T(8,128)} %copy-done, f32[4,768,128]{2,1,0:T(8,128)} %old_projection.1.old), custom_call_target="tpu_custom_call" | custom-call | flops 100663296 | bytes 6291456 | tf_op jit(solution)/shard_map/volume_step/pallas_call | solution.py:612
  102.3 0.0 collective-permute-done.1
  102.3 7.6 %all-to-all-start.2 = ((f32[32,32,384]{2,1,0:T(8,128)}), f32[32,32,384]{2,1,0:T(8,128)S(1)}, u32[]{:S(2)}, u32[]{:S(2)}) async-start(f32[32,32,384]{2,1,0:T(8,128)} %get-tuple-element.63), calls=%async_computation.2 | async-start | bytes 3145728 | tf_op jit(solution)/shard_map/all_to_all | solution.py:665
  110.0 0.0 copy-start.3
  110.0 8.1 %fresh_volume.1 = f32[16,32,3072]{2,1,0:T(8,128)} custom-call(f32[16,32,3072]{2,1,0:T(8,128)} %volume.3, f32[16,768,128]{2,1,0:T(8,128)} %get-tuple-element.58.update), custom_call_target="tpu_custom_call" | custom-call | flops 1572864 | bytes 18874368 | tf_op jit(solution)/shard_map/fresh_volume/pallas_call | solution.py:639
  118.1 0.0 copy-start.1
  118.1 1.4 collective-permute-start.2
  119.5 4.7 %collective-permute-start.4 = (f32[2,224,128]{2,1,0:T(8,128)}, f32[2,224,128]{2,1,0:T(8,128)S(1)}, u32[]{:S(2)}, u32[]{:S(2)}) collective-permute-start(f32[2,224,128]{2,1,0:T(8,128)} %get-tuple-element.57), channel_id=1, source_target_pairs={{0,1},{2,3},{4,5},{6,7},{8,9},{10,11},{12,13},{14,15},{16,17},{18,... | collective-permute-start | bytes 688136 | tf_op jit(solution)/shard_map/ppermute | solution.py:33
  124.2 0.0 copy-done.3
  124.2 0.1 pad_add_fusion
  124.3 0.0 copy-done.1
  124.3 0.0 copy-start.7
  124.3 1.9 %maximum_bitcast_fusion = f32[2,1,1024,384]{3,2,0,1:T(8,128)} fusion(f32[2,1024,256]{2,1,0:T(8,128)S(1)} %copy-done.1, f32[2,1024,128]{2,1,0:T(8,128)S(1)} %pad_add_fusion), kind=kLoop, calls=%fused_computation | loop fusion | flops 786432 | bytes 6291456 | tf_op jit(solution)/shard_map/broadcast_in_dim | solution.py:686
  126.2 2.5 %collective-permute-done.2 = f32[2,224,128]{2,1,0:T(8,128)} collective-permute-done((f32[2,224,128]{2,1,0:T(8,128)}, f32[2,224,128]{2,1,0:T(8,128)}, u32[]{:S(2)}, u32[]{:S(2)}) %collective-permute-start.2) | collective-permute-done | bytes 229408 | tf_op jit(solution)/shard_map/ppermute | solution.py:33
  128.7 4.5 %collective-permute-start.5 = (f32[2,224,128]{2,1,0:T(8,128)}, f32[2,224,128]{2,1,0:T(8,128)S(1)}, u32[]{:S(2)}, u32[]{:S(2)}) collective-permute-start(f32[2,224,128]{2,1,0:T(8,128)} %collective-permute-done.2), channel_id=1, source_target_pairs={{0,2},{2,4},{4,6},{8,10},{10,12},{12,14},{16,18},{18,20},{20,22},{... | collective-permute-start | bytes 688136 | tf_op jit(solution)/shard_map/ppermute | solution.py:33
  133.1 0.0 copy-done.7
  133.2 1.9 %collective-permute-start.3 = (f32[2,224,128]{2,1,0:T(8,128)S(1)}, f32[2,224,128]{2,1,0:T(8,128)S(1)}, u32[]{:S(2)}, u32[]{:S(2)}) collective-permute-start(f32[2,224,128]{2,1,0:T(8,128)S(1)} %copy-done.7), channel_id=1, source_target_pairs={{0,1},{1,2},{2,3},{3,4},{4,5},{5,6},{6,7},{8,9},{9,10},{10,11},{11... | collective-permute-start | bytes 688136 | tf_op jit(solution)/shard_map/ppermute | solution.py:27
  135.1 0.0 collective-permute-done.4
  135.1 15.0 %collective-permute-done.5 = f32[2,224,128]{2,1,0:T(8,128)S(1)} collective-permute-done((f32[2,224,128]{2,1,0:T(8,128)}, f32[2,224,128]{2,1,0:T(8,128)S(1)}, u32[]{:S(2)}, u32[]{:S(2)}) %collective-permute-start.5) | collective-permute-done | bytes 229408 | tf_op jit(solution)/shard_map/ppermute | solution.py:33
  150.2 0.9 collective-permute-done.3
  151.1 1.8 %fusion.3 = f32[2,1,1024,384]{3,2,0,1:T(8,128)} fusion(f32[2,1,1024,384]{3,2,0,1:T(8,128)} %maximum_bitcast_fusion, f32[2,224,128]{2,1,0:T(8,128)S(1)} %add.29, f32[2,224,128]{2,1,0:T(8,128)S(1)} %collective-permute-done.3), kind=kLoop, calls=%fused_computation.8 | loop fusion | flops 229376 | bytes 1376256 | tf_op jit(solution)/shard_map/scatter-add | solution.py:690
  153.0 0.0 all-to-all-done.2
  153.0 2.0 %fusion.1 = f32[1,1024,384]{2,1,0:T(8,128)} fusion(s32[]{:T(128)S(6)} %select_n.20, f32[1024,384]{1,0:T(8,128)S(1)} %bitcast.21), kind=kLoop, calls=%fused_computation.4 | loop fusion | flops 393216 | bytes 3145732 | tf_op jit(solution)/shard_map/broadcast_in_dim | solution.py:691
  (1 shorter events, 0.0 us)
Async XLA Ops:
  0.6 5.0 %copy-start.4 = (s32[4]{0:T(128)S(1)}, s32[4]{0:T(128)}, u32[]{:S(2)}) copy-start(s32[4]{0:T(128)} %param.24) | copy-start | bytes 52
  0.6 6.9 %copy-start.5 = (s32[1,8,2]{1,2,0:T(2,128)S(1)}, s32[1,8,2]{1,2,0:T(2,128)}, u32[]{:S(2)}) copy-start(s32[1,8,2]{1,2,0:T(2,128)} %param.21) | copy-start | bytes 196
  2.6 26.1 %collective-permute-start = (f32[2,1024,128]{2,1,0:T(8,128)}, f32[2,1024,128]{2,1,0:T(8,128)S(1)}, u32[]{:S(2)}, u32[]{:S(2)}) collective-permute-start(f32[2,1024,128]{2,1,0:T(8,128)} %margins.1), channel_id=1, source_target_pairs={{1,0},{2,1},{3,2},{4,3},{5,4},{6,5},{7,6},{9,8},{10,9},{11,10},{12... | collective-permute-start | bytes 3145736 | tf_op jit(solution)/shard_map/ppermute | solution.py:27
  19.6 20.5 %all-to-all-start = ((f32[32,32,128]{2,1,0:T(8,128)}), f32[32,32,128]{2,1,0:T(8,128)S(1)}, u32[]{:S(2)}, u32[]{:S(2)}) async-start(f32[32,32,128]{2,1,0:T(8,128)} %bitcast.30), calls=%async_computation | async-start | bytes 1048576 | tf_op jit(solution)/shard_map/all_to_all | solution.py:665
  28.7 1.0 copy-start.6
  40.1 23.4 %copy-start.2 = (f32[32,32,128]{2,1,0:T(8,128)}, f32[32,32,128]{2,1,0:T(8,128)S(1)}, u32[]{:S(2)}) copy-start(f32[32,32,128]{2,1,0:T(8,128)S(1)} %all-to-all-done.left_from) | copy-start | bytes 1572868
  40.1 44.4 %all-to-all-start.1 = ((f32[32,32,384]{2,1,0:T(8,128)}), f32[32,32,384]{2,1,0:T(8,128)S(1)}, u32[]{:S(2)}, u32[]{:S(2)}) async-start(f32[32,32,384]{2,1,0:T(8,128)} %bitcast.23), calls=%async_computation.1 | async-start | bytes 3145728 | tf_op jit(solution)/shard_map/all_to_all | solution.py:665
  84.5 4.5 %copy-start = (f32[32,32,384]{2,1,0:T(8,128)}, f32[32,32,384]{2,1,0:T(8,128)S(1)}, u32[]{:S(2)}) copy-start(f32[32,32,384]{2,1,0:T(8,128)S(1)} %all-to-all-done.1.right_from) | copy-start | bytes 4718596
  84.5 17.8 %collective-permute-start.1 = (f32[2,576,128]{2,1,0:T(8,128)}, f32[2,576,128]{2,1,0:T(8,128)S(1)}, u32[]{:S(2)}, u32[]{:S(2)}) collective-permute-start(f32[2,576,128]{2,1,0:T(8,128)} %get-tuple-element.54), channel_id=1, source_target_pairs={{0,1},{1,2},{2,3},{3,4},{4,5},{5,6},{6,7},{8,9},{9,10},{10,11},{11... | collective-permute-start | bytes 1769480 | tf_op jit(solution)/shard_map/ppermute | solution.py:27
  102.3 50.6 %all-to-all-start.2 = ((f32[32,32,384]{2,1,0:T(8,128)}), f32[32,32,384]{2,1,0:T(8,128)S(1)}, u32[]{:S(2)}, u32[]{:S(2)}) async-start(f32[32,32,384]{2,1,0:T(8,128)} %get-tuple-element.63), calls=%async_computation.2 | async-start | bytes 3145728 | tf_op jit(solution)/shard_map/all_to_all | solution.py:665
  110.0 14.2 %copy-start.3 = (f32[2,1024,128]{2,1,0:T(8,128)S(1)}, f32[2,1024,128]{2,1,0:T(8,128)}, u32[]{:S(2)}) copy-start(f32[2,1024,128]{2,1,0:T(8,128)} %get-tuple-element.59) | copy-start | bytes 3145732
  118.1 6.2 %copy-start.1 = (f32[2,1024,256]{2,1,0:T(8,128)S(1)}, f32[2,1024,256]{2,1,0:T(8,128)}, u32[]{:S(2)}) copy-start(f32[2,1024,256]{2,1,0:T(8,128)} %get-tuple-element.61) | copy-start | bytes 6291460
  118.1 10.6 %collective-permute-start.2 = (f32[2,224,128]{2,1,0:T(8,128)}, f32[2,224,128]{2,1,0:T(8,128)}, u32[]{:S(2)}, u32[]{:S(2)}) collective-permute-start(f32[2,224,128]{2,1,0:T(8,128)} %get-tuple-element.57), channel_id=1, source_target_pairs={{1,0},{3,2},{5,4},{7,6},{9,8},{11,10},{13,12},{15,14},{17,16},{19,... | collective-permute-start | bytes 688136 | tf_op jit(solution)/shard_map/ppermute | solution.py:33
  119.5 15.6 %collective-permute-start.4 = (f32[2,224,128]{2,1,0:T(8,128)}, f32[2,224,128]{2,1,0:T(8,128)S(1)}, u32[]{:S(2)}, u32[]{:S(2)}) collective-permute-start(f32[2,224,128]{2,1,0:T(8,128)} %get-tuple-element.57), channel_id=1, source_target_pairs={{0,1},{2,3},{4,5},{6,7},{8,9},{10,11},{12,13},{14,15},{16,17},{18,... | collective-permute-start | bytes 688136 | tf_op jit(solution)/shard_map/ppermute | solution.py:33
  124.3 8.8 %copy-start.7 = (f32[2,224,128]{2,1,0:T(8,128)S(1)}, f32[2,224,128]{2,1,0:T(8,128)}, u32[]{:S(2)}) copy-start(f32[2,224,128]{2,1,0:T(8,128)} %get-tuple-element.65) | copy-start | bytes 688132
  128.7 21.5 %collective-permute-start.5 = (f32[2,224,128]{2,1,0:T(8,128)}, f32[2,224,128]{2,1,0:T(8,128)S(1)}, u32[]{:S(2)}, u32[]{:S(2)}) collective-permute-start(f32[2,224,128]{2,1,0:T(8,128)} %collective-permute-done.2), channel_id=1, source_target_pairs={{0,2},{2,4},{4,6},{8,10},{10,12},{12,14},{16,18},{18,20},{20,22},{... | collective-permute-start | bytes 688136 | tf_op jit(solution)/shard_map/ppermute | solution.py:33
  133.2 18.0 %collective-permute-start.3 = (f32[2,224,128]{2,1,0:T(8,128)S(1)}, f32[2,224,128]{2,1,0:T(8,128)S(1)}, u32[]{:S(2)}, u32[]{:S(2)}) collective-permute-start(f32[2,224,128]{2,1,0:T(8,128)S(1)} %copy-done.7), channel_id=1, source_target_pairs={{0,1},{1,2},{2,3},{3,4},{4,5},{5,6},{6,7},{8,9},{9,10},{10,11},{11... | collective-permute-start | bytes 688136 | tf_op jit(solution)/shard_map/ppermute | solution.py:27

commit v5 on v4

--- a/solution.py
+++ b/solution.py
@@ -411,7 +411,7 @@
             pltpu.SemaphoreType.DMA((slots, 2)),
             pltpu.SemaphoreType.DMA((3 * columns + (2 * columns + 1) * (height // size),)),
         ],
-        compiler_params=pltpu.CompilerParams(vmem_limit_bytes=VMEM_BYTES),
+        compiler_params=pltpu.CompilerParams(vmem_limit_bytes=VMEM_BYTES * 21 // 20),
         cost_estimate=pl.CostEstimate(
             flops=26 * slots * size**3, bytes_accessed=16 * height * width, transcendentals=0
         ),

time: 155 us -> 155 us (level); the launches traced: 155 us -> 153 us
  Pallas kernels: 54.5 us -> 52.6 us
    all_to_all x3, waiting for transfers between devices: 23.9 us -> 26.3 us  [exchanged(): return lax.all_to_all(blocks, axes, split_axis=0, concat_axis=0, tiled=True)]
    pallas_call x2, Pallas kernels: 18.2 us -> 16.2 us  [probe_phase(): pl.pallas_call(functools.partial(probe_kernel, base=base, beyond=beyond),...]
    ppermute x3, waiting for transfers between devices: 2.51 us -> 0.94 us  [passed_along(): return lax.ppermute(block, axis, route)]
  transfers between devices with their start and end apart: 9 -> 9, of which waited for: 6 -> 5; matrix products, arithmetic and copies ran while one was open for 4% -> 4% of each run, Pallas kernels for 34% -> 33%
where the time goes in v5:
time: 155 us; the launch traced here: 153 us
  Pallas kernels  52.6 us (34%)
  starting transfers between devices  45.9 us (30%)
  waiting for transfers between devices  44.8 us (29%)
  other arithmetic  7.06 us (5%)
  between operations  2.19 us (1%)
    all_to_all x3, waiting for transfers between devices, exchanged(): return lax.all_to_all(blocks, axes, split_axis=0, concat_axis=0, tiled=True)  26.3 us
    all_to_all x3, starting transfers between devices, exchanged(): return lax.all_to_all(blocks, axes, split_axis=0, concat_axis=0, tiled=True)  25.9 us
    ppermute x3, waiting for transfers between devices, passed_by(): return lax.ppermute(block, axis, route)  17.5 us
    pallas_call x2, Pallas kernels, probe_phase(): pl.pallas_call(functools.partial(probe_kernel, base=base, beyond=beyond),...  16.2 us
    pallas_call x1, Pallas kernels, volume_step(): pl.pallas_call(functools.partial(step_kernel, turned), out_shape=(jax.Sha...  13.3 us
    pallas_call x1, Pallas kernels, old_projection(): pl.pallas_call(functools.partial(old_kernel, turned), out_shape=jax.Shape...  13 us
    ppermute x3, starting transfers between devices, passed_by(): return lax.ppermute(block, axis, route)  10.6 us
    ppermute x3, starting transfers between devices, passed_along(): return lax.ppermute(block, axis, route)  9.48 us
  transfers between devices with their start and end apart: 9, of which 5 were waited for; matrix products, arithmetic and copies ran while one was open for 4% of the time, Pallas kernels for 33%

profile of v5, /device:TPU:17, one launch (start us, length us, event | category | flops | bytes accessed | tf_op | source)
XLA Modules:
  0.0 153.2 jit_solution(490178353761918690)
XLA Ops:
  0.6 0.0 copy-start.4
  0.6 0.0 copy-start.5
  0.7 2.0 %margins.1 = f32[2,1024,128]{2,1,0:T(8,128)} custom-call(f32[1024,384]{1,0:T(8,128)} %bitcast.24, f32[1024,384]{1,0:T(8,128)} %bitcast.27), custom_call_target="tpu_custom_call" | custom-call | tf_op jit(solution)/shard_map/margins/pallas_call | solution.py:357
  2.6 3.0 %collective-permute-start = (f32[2,1024,128]{2,1,0:T(8,128)}, f32[2,1024,128]{2,1,0:T(8,128)}, u32[]{:S(2)}, u32[]{:S(2)}) collective-permute-start(f32[2,1024,128]{2,1,0:T(8,128)} %margins.1), channel_id=1, source_target_pairs={{1,0},{2,1},{3,2},{4,3},{5,4},{6,5},{7,6},{9,8},{10,9},{11,10},{12... | collective-permute-start | bytes 3145736 | tf_op jit(solution)/shard_map/ppermute | solution.py:27
  5.7 0.0 copy-done.4
  5.7 0.6 add_select_fusion.whole
  6.3 0.7 convert_multiply_fusion.frac
  7.6 0.0 copy-done.5
  7.6 0.7 copy.18.positions_ref
  8.9 8.7 %probes_within.1 = (f32[2,1024,128]{2,1,0:T(8,128)}, f32[2,2,1024,128]{3,2,1,0:T(8,128)}, f32[1024,128]{1,0:T(8,128)}) custom-call(s32[1,1]{1,0:T(1,128)S(6)} %copy.21.used_ref, s32[8,2]{1,0:T(8,128)} %copy.18.positions_ref, s32[1]{0:T(128)} %copy.22.shift_ref, f32[1024,384]{1,0:T(8,128)} %bitcast.25, f32[1024,384]{1,0:T(8,128)} %bitcast.28, ...), custom_call_target="tpu_custom_call" | custom-call | flops 3489660928 | bytes 6291456 | tf_op jit(solution)/shard_map/probes_within/pallas_call | solution.py:393
  17.6 11.6 %all-to-all-start = ((f32[32,32,128]{2,1,0:T(8,128)}), f32[32,32,128]{2,1,0:T(8,128)S(1)}, u32[]{:S(2)}, u32[]{:S(2)}) async-start(f32[32,32,128]{2,1,0:T(8,128)} %bitcast.30), calls=%async_computation | async-start | bytes 1048576 | tf_op jit(solution)/shard_map/all_to_all | solution.py:665
  29.2 0.0 collective-permute-done.refs_2_
  29.2 7.5 %probes_beyond.1 = (f32[2,1024,256]{2,1,0:T(8,128)}, f32[2,576,128]{2,1,0:T(8,128)}, f32[2,224,128]{2,1,0:T(8,128)}, f32[2,224,128]{2,1,0:T(8,128)}, f32[1024,384]{1,0:T(8,128)}) custom-call(s32[1,1]{1,0:T(1,128)S(6)} %copy.21.used_ref, s32[8,2]{1,0:T(8,128)} %copy.18.positions_ref, s32[1]{0:T(128)} %copy.22.shift_ref, f32[1024,384]{1,0:T(8,128)} %bitcast.26, ...), custom_call_target="tpu_custom_call" | custom-call | flops 3489660928 | bytes 6291456 | tf_op jit(solution)/shard_map/probes_beyond/pallas_call | solution.py:393
  36.8 5.4 %all-to-all-done.left_from = f32[32,32,128]{2,1,0:T(8,128)S(1)} async-done(((f32[32,32,128]{2,1,0:T(8,128)}), f32[32,32,128]{2,1,0:T(8,128)S(1)}, u32[]{:S(2)}, u32[]{:S(2)}) %all-to-all-start) | async-done | bytes 524320 | tf_op jit(solution)/shard_map/all_to_all | solution.py:665
  42.1 0.0 copy-start.2
  42.1 6.9 %all-to-all-start.1 = ((f32[32,32,384]{2,1,0:T(8,128)}), f32[32,32,384]{2,1,0:T(8,128)S(1)}, u32[]{:S(2)}, u32[]{:S(2)}) async-start(f32[32,32,384]{2,1,0:T(8,128)} %bitcast.23), calls=%async_computation.1 | async-start | bytes 3145728 | tf_op jit(solution)/shard_map/all_to_all | solution.py:665
  49.1 0.0 copy-start.6
  49.1 13.0 %old_projection.1.old = f32[4,768,128]{2,1,0:T(8,128)} custom-call(s32[4,16]{1,0:T(4,128)} %add_select_fusion.whole, f32[4,16]{1,0:T(4,128)} %convert_multiply_fusion.frac, f32[16,32,3072]{2,1,0:T(8,128)} %volume.3), custom_call_target="tpu_custom_call" | custom-call | flops 50331648 | bytes 6291456 | tf_op jit(solution)/shard_map/old_projection/pallas_call | solution.py:599
  62.1 0.0 copy-done.2
  62.1 20.9 %all-to-all-done.1.right_from = f32[32,32,384]{2,1,0:T(8,128)S(1)} async-done(((f32[32,32,384]{2,1,0:T(8,128)}), f32[32,32,384]{2,1,0:T(8,128)S(1)}, u32[]{:S(2)}, u32[]{:S(2)}) %all-to-all-start.1) | async-done | bytes 1572896 | tf_op jit(solution)/shard_map/all_to_all | solution.py:665
  83.0 0.0 copy-start
  83.0 0.0 copy-done.6
  83.0 4.5 %collective-permute-start.1 = (f32[2,576,128]{2,1,0:T(8,128)S(1)}, f32[2,576,128]{2,1,0:T(8,128)S(1)}, u32[]{:S(2)}, u32[]{:S(2)}) collective-permute-start(f32[2,576,128]{2,1,0:T(8,128)S(1)} %copy-done.6), channel_id=1, source_target_pairs={{0,1},{1,2},{2,3},{3,4},{4,5},{5,6},{6,7},{8,9},{9,10},{10,11},{11... | collective-permute-start | bytes 1769480 | tf_op jit(solution)/shard_map/ppermute | solution.py:27
  87.5 0.0 copy-done
  87.6 13.3 %volume_step.1 = (f32[32,32,384]{2,1,0:T(8,128)}, f32[16,768,128]{2,1,0:T(8,128)}) custom-call(s32[4,16]{1,0:T(4,128)} %add_select_fusion.whole, f32[4,16]{1,0:T(4,128)} %convert_multiply_fusion.frac, f32[32,32,128]{2,1,0:T(8,128)} %copy-done.2, f32[32,32,384]{2,1,0:T(8,128)} %copy-done, f32[4,768,128]{2,1,0:T(8,128)} %old_projection.1.old), custom_call_target="tpu_custom_call" | custom-call | flops 100663296 | bytes 6291456 | tf_op jit(solution)/shard_map/volume_step/pallas_call | solution.py:612
  100.9 0.0 collective-permute-done.1
  100.9 7.4 %all-to-all-start.2 = ((f32[32,32,384]{2,1,0:T(8,128)}), f32[32,32,384]{2,1,0:T(8,128)S(1)}, u32[]{:S(2)}, u32[]{:S(2)}) async-start(f32[32,32,384]{2,1,0:T(8,128)} %get-tuple-element.63), calls=%async_computation.2 | async-start | bytes 3145728 | tf_op jit(solution)/shard_map/all_to_all | solution.py:665
  108.3 0.0 copy-start.3
  108.3 8.1 %fresh_volume.1 = f32[16,32,3072]{2,1,0:T(8,128)} custom-call(f32[16,32,3072]{2,1,0:T(8,128)} %volume.3, f32[16,768,128]{2,1,0:T(8,128)} %get-tuple-element.58.update), custom_call_target="tpu_custom_call" | custom-call | flops 1572864 | bytes 18874368 | tf_op jit(solution)/shard_map/fresh_volume/pallas_call | solution.py:639
  116.4 0.0 copy-start.1
  116.4 1.4 collective-permute-start.2
  117.8 4.7 %collective-permute-start.4 = (f32[2,224,128]{2,1,0:T(8,128)}, f32[2,224,128]{2,1,0:T(8,128)S(1)}, u32[]{:S(2)}, u32[]{:S(2)}) collective-permute-start(f32[2,224,128]{2,1,0:T(8,128)} %get-tuple-element.57), channel_id=1, source_target_pairs={{0,1},{2,3},{4,5},{6,7},{8,9},{10,11},{12,13},{14,15},{16,17},{18,... | collective-permute-start | bytes 688136 | tf_op jit(solution)/shard_map/ppermute | solution.py:33
  122.5 0.0 copy-done.3
  122.5 0.1 pad_add_fusion
  122.6 0.0 copy-done.1
  122.6 0.0 copy-start.7
  122.6 1.9 %maximum_bitcast_fusion = f32[2,1,1024,384]{3,2,0,1:T(8,128)} fusion(f32[2,1024,256]{2,1,0:T(8,128)S(1)} %copy-done.1, f32[2,1024,128]{2,1,0:T(8,128)S(1)} %pad_add_fusion), kind=kLoop, calls=%fused_computation | loop fusion | flops 786432 | bytes 6291456 | tf_op jit(solution)/shard_map/broadcast_in_dim | solution.py:686
  124.5 2.5 %collective-permute-done.2 = f32[2,224,128]{2,1,0:T(8,128)} collective-permute-done((f32[2,224,128]{2,1,0:T(8,128)}, f32[2,224,128]{2,1,0:T(8,128)}, u32[]{:S(2)}, u32[]{:S(2)}) %collective-permute-start.2) | collective-permute-done | bytes 229408 | tf_op jit(solution)/shard_map/ppermute | solution.py:33
  126.9 4.5 %collective-permute-start.5 = (f32[2,224,128]{2,1,0:T(8,128)}, f32[2,224,128]{2,1,0:T(8,128)S(1)}, u32[]{:S(2)}, u32[]{:S(2)}) collective-permute-start(f32[2,224,128]{2,1,0:T(8,128)} %collective-permute-done.2), channel_id=1, source_target_pairs={{0,2},{2,4},{4,6},{8,10},{10,12},{12,14},{16,18},{18,20},{20,22},{... | collective-permute-start | bytes 688136 | tf_op jit(solution)/shard_map/ppermute | solution.py:33
  131.4 0.0 copy-done.7
  131.4 1.9 %collective-permute-start.3 = (f32[2,224,128]{2,1,0:T(8,128)S(1)}, f32[2,224,128]{2,1,0:T(8,128)S(1)}, u32[]{:S(2)}, u32[]{:S(2)}) collective-permute-start(f32[2,224,128]{2,1,0:T(8,128)S(1)} %copy-done.7), channel_id=1, source_target_pairs={{0,1},{1,2},{2,3},{3,4},{4,5},{5,6},{6,7},{8,9},{9,10},{10,11},{11... | collective-permute-start | bytes 688136 | tf_op jit(solution)/shard_map/ppermute | solution.py:27
  133.4 0.0 collective-permute-done.4
  133.4 15.0 %collective-permute-done.5 = f32[2,224,128]{2,1,0:T(8,128)S(1)} collective-permute-done((f32[2,224,128]{2,1,0:T(8,128)}, f32[2,224,128]{2,1,0:T(8,128)S(1)}, u32[]{:S(2)}, u32[]{:S(2)}) %collective-permute-start.5) | collective-permute-done | bytes 229408 | tf_op jit(solution)/shard_map/ppermute | solution.py:33
  148.5 0.9 collective-permute-done.3
  149.4 1.8 %fusion.3 = f32[2,1,1024,384]{3,2,0,1:T(8,128)} fusion(f32[2,1,1024,384]{3,2,0,1:T(8,128)} %maximum_bitcast_fusion, f32[2,224,128]{2,1,0:T(8,128)S(1)} %add.29, f32[2,224,128]{2,1,0:T(8,128)S(1)} %collective-permute-done.3), kind=kLoop, calls=%fused_computation.8 | loop fusion | flops 229376 | bytes 1376256 | tf_op jit(solution)/shard_map/scatter-add | solution.py:690
  151.3 0.0 all-to-all-done.2
  151.3 2.0 %fusion.1 = f32[1,1024,384]{2,1,0:T(8,128)} fusion(s32[]{:T(128)S(6)} %select_n.20, f32[1024,384]{1,0:T(8,128)S(1)} %bitcast.21), kind=kLoop, calls=%fused_computation.4 | loop fusion | flops 393216 | bytes 3145732 | tf_op jit(solution)/shard_map/broadcast_in_dim | solution.py:691
  (1 shorter events, 0.0 us)
Async XLA Ops:
  0.6 5.0 %copy-start.4 = (s32[4]{0:T(128)S(1)}, s32[4]{0:T(128)}, u32[]{:S(2)}) copy-start(s32[4]{0:T(128)} %param.24) | copy-start | bytes 52
  0.6 6.9 %copy-start.5 = (s32[1,8,2]{1,2,0:T(2,128)S(1)}, s32[1,8,2]{1,2,0:T(2,128)}, u32[]{:S(2)}) copy-start(s32[1,8,2]{1,2,0:T(2,128)} %param.21) | copy-start | bytes 196
  2.6 26.6 %collective-permute-start = (f32[2,1024,128]{2,1,0:T(8,128)}, f32[2,1024,128]{2,1,0:T(8,128)}, u32[]{:S(2)}, u32[]{:S(2)}) collective-permute-start(f32[2,1024,128]{2,1,0:T(8,128)} %margins.1), channel_id=1, source_target_pairs={{1,0},{2,1},{3,2},{4,3},{5,4},{6,5},{7,6},{9,8},{10,9},{11,10},{12... | collective-permute-start | bytes 3145736 | tf_op jit(solution)/shard_map/ppermute | solution.py:27
  17.6 24.5 %all-to-all-start = ((f32[32,32,128]{2,1,0:T(8,128)}), f32[32,32,128]{2,1,0:T(8,128)S(1)}, u32[]{:S(2)}, u32[]{:S(2)}) async-start(f32[32,32,128]{2,1,0:T(8,128)} %bitcast.30), calls=%async_computation | async-start | bytes 1048576 | tf_op jit(solution)/shard_map/all_to_all | solution.py:665
  42.1 19.9 %copy-start.2 = (f32[32,32,128]{2,1,0:T(8,128)}, f32[32,32,128]{2,1,0:T(8,128)S(1)}, u32[]{:S(2)}) copy-start(f32[32,32,128]{2,1,0:T(8,128)S(1)} %all-to-all-done.left_from) | copy-start | bytes 1572868
  42.1 40.9 %all-to-all-start.1 = ((f32[32,32,384]{2,1,0:T(8,128)}), f32[32,32,384]{2,1,0:T(8,128)S(1)}, u32[]{:S(2)}, u32[]{:S(2)}) async-start(f32[32,32,384]{2,1,0:T(8,128)} %bitcast.23), calls=%async_computation.1 | async-start | bytes 3145728 | tf_op jit(solution)/shard_map/all_to_all | solution.py:665
  49.1 33.9 %copy-start.6 = (f32[2,576,128]{2,1,0:T(8,128)S(1)}, f32[2,576,128]{2,1,0:T(8,128)}, u32[]{:S(2)}) copy-start(f32[2,576,128]{2,1,0:T(8,128)} %get-tuple-element.54) | copy-start | bytes 1769476
  83.0 4.5 %copy-start = (f32[32,32,384]{2,1,0:T(8,128)}, f32[32,32,384]{2,1,0:T(8,128)S(1)}, u32[]{:S(2)}) copy-start(f32[32,32,384]{2,1,0:T(8,128)S(1)} %all-to-all-done.1.right_from) | copy-start | bytes 4718596
  83.0 17.9 %collective-permute-start.1 = (f32[2,576,128]{2,1,0:T(8,128)S(1)}, f32[2,576,128]{2,1,0:T(8,128)S(1)}, u32[]{:S(2)}, u32[]{:S(2)}) collective-permute-start(f32[2,576,128]{2,1,0:T(8,128)S(1)} %copy-done.6), channel_id=1, source_target_pairs={{0,1},{1,2},{2,3},{3,4},{4,5},{5,6},{6,7},{8,9},{9,10},{10,11},{11... | collective-permute-start | bytes 1769480 | tf_op jit(solution)/shard_map/ppermute | solution.py:27
  100.9 50.4 %all-to-all-start.2 = ((f32[32,32,384]{2,1,0:T(8,128)}), f32[32,32,384]{2,1,0:T(8,128)S(1)}, u32[]{:S(2)}, u32[]{:S(2)}) async-start(f32[32,32,384]{2,1,0:T(8,128)} %get-tuple-element.63), calls=%async_computation.2 | async-start | bytes 3145728 | tf_op jit(solution)/shard_map/all_to_all | solution.py:665
  108.3 14.2 %copy-start.3 = (f32[2,1024,128]{2,1,0:T(8,128)S(1)}, f32[2,1024,128]{2,1,0:T(8,128)}, u32[]{:S(2)}) copy-start(f32[2,1024,128]{2,1,0:T(8,128)} %get-tuple-element.59) | copy-start | bytes 3145732
  116.4 6.2 %copy-start.1 = (f32[2,1024,256]{2,1,0:T(8,128)S(1)}, f32[2,1024,256]{2,1,0:T(8,128)}, u32[]{:S(2)}) copy-start(f32[2,1024,256]{2,1,0:T(8,128)} %get-tuple-element.61) | copy-start | bytes 6291460
  116.4 10.6 %collective-permute-start.2 = (f32[2,224,128]{2,1,0:T(8,128)}, f32[2,224,128]{2,1,0:T(8,128)}, u32[]{:S(2)}, u32[]{:S(2)}) collective-permute-start(f32[2,224,128]{2,1,0:T(8,128)} %get-tuple-element.57), channel_id=1, source_target_pairs={{1,0},{3,2},{5,4},{7,6},{9,8},{11,10},{13,12},{15,14},{17,16},{19,... | collective-permute-start | bytes 688136 | tf_op jit(solution)/shard_map/ppermute | solution.py:33
  117.8 15.6 %collective-permute-start.4 = (f32[2,224,128]{2,1,0:T(8,128)}, f32[2,224,128]{2,1,0:T(8,128)S(1)}, u32[]{:S(2)}, u32[]{:S(2)}) collective-permute-start(f32[2,224,128]{2,1,0:T(8,128)} %get-tuple-element.57), channel_id=1, source_target_pairs={{0,1},{2,3},{4,5},{6,7},{8,9},{10,11},{12,13},{14,15},{16,17},{18,... | collective-permute-start | bytes 688136 | tf_op jit(solution)/shard_map/ppermute | solution.py:33
  122.6 8.8 %copy-start.7 = (f32[2,224,128]{2,1,0:T(8,128)S(1)}, f32[2,224,128]{2,1,0:T(8,128)}, u32[]{:S(2)}) copy-start(f32[2,224,128]{2,1,0:T(8,128)} %get-tuple-element.65) | copy-start | bytes 688132
  126.9 21.5 %collective-permute-start.5 = (f32[2,224,128]{2,1,0:T(8,128)}, f32[2,224,128]{2,1,0:T(8,128)S(1)}, u32[]{:S(2)}, u32[]{:S(2)}) collective-permute-start(f32[2,224,128]{2,1,0:T(8,128)} %collective-permute-done.2), channel_id=1, source_target_pairs={{0,2},{2,4},{4,6},{8,10},{10,12},{12,14},{16,18},{18,20},{20,22},{... | collective-permute-start | bytes 688136 | tf_op jit(solution)/shard_map/ppermute | solution.py:33
  131.4 18.0 %collective-permute-start.3 = (f32[2,224,128]{2,1,0:T(8,128)S(1)}, f32[2,224,128]{2,1,0:T(8,128)S(1)}, u32[]{:S(2)}, u32[]{:S(2)}) collective-permute-start(f32[2,224,128]{2,1,0:T(8,128)S(1)} %copy-done.7), channel_id=1, source_target_pairs={{0,1},{1,2},{2,3},{3,4},{4,5},{5,6},{6,7},{8,9},{9,10},{10,11},{11... | collective-permute-start | bytes 688136 | tf_op jit(solution)/shard_map/ppermute | solution.py:27

commit v6 on v5

--- a/solution.py
+++ b/solution.py
@@ -135,8 +135,8 @@
         ]
 
     def mine(slot):
-        past = positions_ref[slot, 1] + size > base + tiles * LANES
-        return past if not beyond else positions_ref[slot, 1] + size > base + (tiles - 1) * LANES
+        past = positions_ref[0, 1, slot] + size > base + tiles * LANES
+        return past if not beyond else positions_ref[0, 1, slot] + size > base + (tiles - 1) * LANES
 
     def live(slot):
         return mine(slot) if beyond else jnp.logical_not(mine(slot))
@@ -167,8 +167,8 @@
         return tables[which], tables[which + 1]
 
     def visit(slot, turned, uh, ul, vh, vl):
-        row = positions_ref[slot, 0]
-        col = positions_ref[slot, 1] - base
+        row = positions_ref[0, 0, slot]
+        col = positions_ref[0, 1, slot] - base
         first = pl.multiple_of(row // SUBLANES * SUBLANES, SUBLANES)
         row_rest = row - first
         wrap = pl.multiple_of(jnp.minimum(first + size, height - SUBLANES), SUBLANES)
@@ -460,7 +460,7 @@
 
         zero = jnp.zeros((rows + SUBLANES, LANES), jnp.float32)
         plain, weighted = lax.fori_loop(
-            0, depth, add_level, (zero[SUBLANES:], zero), unroll=8
+            0, depth, add_level, (zero[SUBLANES:], zero), unroll=16
         )
         return plain - weighted[SUBLANES:] + weighted[SUBLANES - 1 : SUBLANES - 1 + rows]
 
@@ -535,7 +535,7 @@
         main = cells.at[level, pl.ds(turned.margin, turned.length), :]
         return pltpu.make_async_copy(main, update.at[level], level_sems.at[level])
 
-    @pl.loop(0, depth)
+    @pl.loop(0, depth, unroll=2)
     def _(level):
         for at in range(0, turned.length, rows):
             plain = weighted = None
@@ -656,20 +656,19 @@
     axes = ("tilt", "tile")
     devices = lax.axis_size("tilt") * lax.axis_size("tile")
     turned = Turned(band, columns, width)
-    whole, frac = shift_tables(slope, depth)
     probe = (probe_re, probe_im)
 
-    within = (counts, positions[0], row_shift)
+    within = (counts, jnp.swapaxes(positions, 1, 2), row_shift)
 
     def exchanged(blocks):
         return lax.all_to_all(blocks, axes, split_axis=0, concat_axis=0, tiled=True)
 
     edge = passed_along(margins(*tile), "tile", -1)
     grad_left, begun, left = probe_phase(*within, tile, None, None, probe, intensity[0])
-    left, whole, frac = lax.optimization_barrier((left, whole, frac))
     left = exchanged(left.reshape(devices, band, LANES))
     grad_right, early, late, relayed, right = probe_phase(*within, tile, edge, begun, probe, intensity[0])
-    right, left, whole = lax.optimization_barrier((right, left, whole))
+    right, left, slope = lax.optimization_barrier((right, left, slope))
+    whole, frac = shift_tables(slope, depth)
     right = exchanged(right.reshape(devices, band, width))
     old = old_projection(turned, whole, frac, volume)
     right, early, old = lax.optimization_barrier((right, early, old))
@@ -687,7 +686,8 @@
     relayed, fresh, grad = lax.optimization_barrier((relayed, fresh, grad))
     relayed = straight + passed_by(relayed, "tile", 0, 2)
     late = jnp.concatenate([late, relayed], axis=1)
-    grad = grad.at[:, 0, rows:, :LANES].add(late)
+    late = (late + grad_left[:, rows:])[:, None]
+    grad = lax.dynamic_update_slice(grad, late, (0, 0, rows, 0))
     reprojection = jnp.roll(returned.reshape(height, width), -row_shift[0], axis=0)[None]
     return (fresh, reprojection, grad)
 

time: 155 us -> 153 us (0.987)
  Pallas kernels: 52.6 us -> 49.5 us
  starting transfers between devices: 45.9 us -> 48.2 us
    ppermute x3, waiting for transfers between devices: 0.94 us -> 7.92 us  [passed_along(): return lax.ppermute(block, axis, route)]
    all_to_all x3, waiting for transfers between devices: 26.3 us -> 20.6 us  [exchanged(): return lax.all_to_all(blocks, axes, split_axis=0, concat_axis=0, tiled=True)]
    all_to_all x3, starting transfers between devices: 25.9 us -> 28.2 us  [exchanged(): return lax.all_to_all(blocks, axes, split_axis=0, concat_axis=0, tiled=True)]
    scatter-add x1 -> x0, other arithmetic: 1.85 us -> none  [local(): grad = grad.at[:, 0, rows:, :LANES].add(late)]
    pallas_call x2, Pallas kernels: 16.2 us -> 14.5 us  [probe_phase(): pl.pallas_call(functools.partial(probe_kernel, base=base, beyond=beyond),...]
  transfers between devices with their start and end apart: 9 -> 9, of which waited for: 5 -> 6; matrix products, arithmetic and copies ran while one was open for 4% -> 3% of each run, Pallas kernels for 33% -> 31%
where the time goes in v6:
time: 153 us; the launch traced here: 152 us
  Pallas kernels  49.5 us (32%)
  starting transfers between devices  48.2 us (32%)
  waiting for transfers between devices  46 us (30%)
  other arithmetic  6.07 us (4%)
  between operations  2.14 us (1%)
    all_to_all x3, starting transfers between devices, exchanged(): return lax.all_to_all(blocks, axes, split_axis=0, concat_axis=0, tiled=True)  28.2 us
    all_to_all x3, waiting for transfers between devices, exchanged(): return lax.all_to_all(blocks, axes, split_axis=0, concat_axis=0, tiled=True)  20.6 us
    ppermute x3, waiting for transfers between devices, passed_by(): return lax.ppermute(block, axis, route)  17.5 us
    pallas_call x2, Pallas kernels, probe_phase(): pl.pallas_call(functools.partial(probe_kernel, base=base, beyond=beyond),...  14.5 us
    pallas_call x1, Pallas kernels, volume_step(): pl.pallas_call(functools.partial(step_kernel, turned), out_shape=(jax.Sha...  12.6 us
    pallas_call x1, Pallas kernels, old_projection(): pl.pallas_call(functools.partial(old_kernel, turned), out_shape=jax.Shape...  12.3 us
    ppermute x3, starting transfers between devices, passed_by(): return lax.ppermute(block, axis, route)  10.6 us
    ppermute x3, starting transfers between devices, passed_along(): return lax.ppermute(block, axis, route)  9.48 us
  transfers between devices with their start and end apart: 9, of which 6 were waited for; matrix products, arithmetic and copies ran while one was open for 3% of the time, Pallas kernels for 31%

profile of v6, /device:TPU:17, one launch (start us, length us, event | category | flops | bytes accessed | tf_op | source)
XLA Modules:
  0.0 151.9 jit_solution(12633911127202418674)
XLA Ops:
  0.6 1.9 %margins.1 = f32[2,1024,128]{2,1,0:T(8,128)} custom-call(f32[1024,384]{1,0:T(8,128)} %bitcast.22, f32[1024,384]{1,0:T(8,128)} %bitcast.25), custom_call_target="tpu_custom_call" | custom-call | tf_op jit(solution)/shard_map/margins/pallas_call | solution.py:357
  2.6 3.0 %collective-permute-start = (f32[2,1024,128]{2,1,0:T(8,128)}, f32[2,1024,128]{2,1,0:T(8,128)}, u32[]{:S(2)}, u32[]{:S(2)}) collective-permute-start(f32[2,1024,128]{2,1,0:T(8,128)} %margins.1), channel_id=1, source_target_pairs={{1,0},{2,1},{3,2},{4,3},{5,4},{6,5},{7,6},{9,8},{10,9},{11,10},{12... | collective-permute-start | bytes 3145736 | tf_op jit(solution)/shard_map/ppermute | solution.py:27
  6.9 5.5 %probes_within.1 = (f32[2,1024,128]{2,1,0:T(8,128)}, f32[2,2,1024,128]{3,2,1,0:T(8,128)}, f32[1024,128]{1,0:T(8,128)}) custom-call(s32[1,1]{1,0:T(1,128)S(6)} %copy.19.used_ref, s32[1,2,8]{2,1,0:T(2,128)} %bitcast.31, s32[1]{0:T(128)} %copy.20.shift_ref, f32[1024,384]{1,0:T(8,128)} %bitcast.23, f32[1024,384]{1,0:T(8,128)} %bitcast.26, f32[256,256]{1,0:T(8,128)} %refs_4_.1, ...), custom_call_target="tpu_custom_call" | custom-call | flops 3489660928 | bytes 6291456 | tf_op jit(solution)/shard_map/probes_within/pallas_call | solution.py:393
  12.5 11.8 %all-to-all-start = ((f32[32,32,128]{2,1,0:T(8,128)}), f32[32,32,128]{2,1,0:T(8,128)S(1)}, u32[]{:S(2)}, u32[]{:S(2)}) async-start(f32[32,32,128]{2,1,0:T(8,128)} %bitcast.28), calls=%async_computation | async-start | bytes 1048576 | tf_op jit(solution)/shard_map/all_to_all | solution.py:664
  24.3 7.0 %collective-permute-done.refs_2_ = f32[2,1024,128]{2,1,0:T(8,128)} collective-permute-done((f32[2,1024,128]{2,1,0:T(8,128)}, f32[2,1024,128]{2,1,0:T(8,128)}, u32[]{:S(2)}, u32[]{:S(2)}) %collective-permute-start) | collective-permute-done | bytes 1048608 | tf_op jit(solution)/shard_map/ppermute | solution.py:27
  31.3 9.0 %probes_beyond.1 = (f32[2,1024,256]{2,1,0:T(8,128)}, f32[2,576,128]{2,1,0:T(8,128)}, f32[2,224,128]{2,1,0:T(8,128)}, f32[2,224,128]{2,1,0:T(8,128)}, f32[1024,384]{1,0:T(8,128)}) custom-call(s32[1,1]{1,0:T(1,128)S(6)} %copy.19.used_ref, s32[1,2,8]{2,1,0:T(2,128)} %bitcast.32, s32[1]{0:T(128)} %copy.20.shift_ref, f32[1024,384]{1,0:T(8,128)} %bitcast.24, ...), custom_call_target="tpu_custom_call" | custom-call | flops 3489660928 | bytes 6291456 | tf_op jit(solution)/shard_map/probes_beyond/pallas_call | solution.py:393
  40.3 0.0 copy-start.4
  40.3 0.2 all-to-all-done.left_from
  40.5 0.0 copy-start.3
  40.5 8.2 %all-to-all-start.1 = ((f32[32,32,384]{2,1,0:T(8,128)}), f32[32,32,384]{2,1,0:T(8,128)S(1)}, u32[]{:S(2)}, u32[]{:S(2)}) async-start(f32[32,32,384]{2,1,0:T(8,128)} %bitcast.21), calls=%async_computation.1 | async-start | bytes 3145728 | tf_op jit(solution)/shard_map/all_to_all | solution.py:664
  48.8 0.0 copy-done.4
  48.8 0.7 add_select_fusion.whole
  49.4 0.6 convert_multiply_fusion.frac
  50.1 0.0 copy-start.5
  50.1 12.3 %old_projection.1.old = f32[4,768,128]{2,1,0:T(8,128)} custom-call(s32[4,16]{1,0:T(4,128)} %add_select_fusion.whole, f32[4,16]{1,0:T(4,128)} %convert_multiply_fusion.frac, f32[16,32,3072]{2,1,0:T(8,128)} %volume.3), custom_call_target="tpu_custom_call" | custom-call | flops 50331648 | bytes 6291456 | tf_op jit(solution)/shard_map/old_projection/pallas_call | solution.py:599
  62.4 0.0 copy-done.3
  62.4 20.3 %all-to-all-done.1.right_from = f32[32,32,384]{2,1,0:T(8,128)S(1)} async-done(((f32[32,32,384]{2,1,0:T(8,128)}), f32[32,32,384]{2,1,0:T(8,128)S(1)}, u32[]{:S(2)}, u32[]{:S(2)}) %all-to-all-start.1) | async-done | bytes 1572896 | tf_op jit(solution)/shard_map/all_to_all | solution.py:664
  82.7 0.0 copy-start
  82.7 0.0 copy-done.5
  82.7 4.5 %collective-permute-start.1 = (f32[2,576,128]{2,1,0:T(8,128)S(1)}, f32[2,576,128]{2,1,0:T(8,128)S(1)}, u32[]{:S(2)}, u32[]{:S(2)}) collective-permute-start(f32[2,576,128]{2,1,0:T(8,128)S(1)} %copy-done.5), channel_id=1, source_target_pairs={{0,1},{1,2},{2,3},{3,4},{4,5},{5,6},{6,7},{8,9},{9,10},{10,11},{11... | collective-permute-start | bytes 1769480 | tf_op jit(solution)/shard_map/ppermute | solution.py:27
  87.2 0.0 copy-done
  87.3 12.6 %volume_step.1 = (f32[32,32,384]{2,1,0:T(8,128)}, f32[16,768,128]{2,1,0:T(8,128)}) custom-call(s32[4,16]{1,0:T(4,128)} %add_select_fusion.whole, f32[4,16]{1,0:T(4,128)} %convert_multiply_fusion.frac, f32[32,32,128]{2,1,0:T(8,128)} %copy-done.3, f32[32,32,384]{2,1,0:T(8,128)} %copy-done, f32[4,768,128]{2,1,0:T(8,128)} %old_projection.1.old), custom_call_target="tpu_custom_call" | custom-call | flops 100663296 | bytes 6291456 | tf_op jit(solution)/shard_map/volume_step/pallas_call | solution.py:612
  99.9 0.0 collective-permute-done.1
  99.9 8.1 %all-to-all-start.2 = ((f32[32,32,384]{2,1,0:T(8,128)}), f32[32,32,384]{2,1,0:T(8,128)S(1)}, u32[]{:S(2)}, u32[]{:S(2)}) async-start(f32[32,32,384]{2,1,0:T(8,128)} %get-tuple-element.45), calls=%async_computation.2 | async-start | bytes 3145728 | tf_op jit(solution)/shard_map/all_to_all | solution.py:664
  108.0 0.0 copy-start.1
  108.0 8.1 %fresh_volume.1 = f32[16,32,3072]{2,1,0:T(8,128)} custom-call(f32[16,32,3072]{2,1,0:T(8,128)} %volume.3, f32[16,768,128]{2,1,0:T(8,128)} %get-tuple-element.40.update), custom_call_target="tpu_custom_call" | custom-call | flops 1572864 | bytes 18874368 | tf_op jit(solution)/shard_map/fresh_volume/pallas_call | solution.py:639
  116.1 0.0 copy-start.2
  116.1 1.4 collective-permute-start.2
  117.5 4.7 %collective-permute-start.4 = (f32[2,224,128]{2,1,0:T(8,128)}, f32[2,224,128]{2,1,0:T(8,128)S(1)}, u32[]{:S(2)}, u32[]{:S(2)}) collective-permute-start(f32[2,224,128]{2,1,0:T(8,128)} %get-tuple-element.39), channel_id=1, source_target_pairs={{0,1},{2,3},{4,5},{6,7},{8,9},{10,11},{12,13},{14,15},{16,17},{18,... | collective-permute-start | bytes 688136 | tf_op jit(solution)/shard_map/ppermute | solution.py:33
  122.2 0.0 copy-done.1
  122.2 0.1 pad_add_fusion
  122.3 0.0 copy-done.2
  122.3 1.9 %maximum_bitcast_fusion = f32[2,1,1024,384]{3,2,0,1:T(8,128)} fusion(f32[2,1024,256]{2,1,0:T(8,128)S(1)} %copy-done.2, f32[2,1024,128]{2,1,0:T(8,128)S(1)} %pad_add_fusion), kind=kLoop, calls=%fused_computation | loop fusion | flops 786432 | bytes 6291456 | tf_op jit(solution)/shard_map/broadcast_in_dim | solution.py:685
  124.2 2.5 %collective-permute-done.2 = f32[2,224,128]{2,1,0:T(8,128)} collective-permute-done((f32[2,224,128]{2,1,0:T(8,128)}, f32[2,224,128]{2,1,0:T(8,128)}, u32[]{:S(2)}, u32[]{:S(2)}) %collective-permute-start.2) | collective-permute-done | bytes 229408 | tf_op jit(solution)/shard_map/ppermute | solution.py:33
  126.6 4.5 %collective-permute-start.5 = (f32[2,224,128]{2,1,0:T(8,128)}, f32[2,224,128]{2,1,0:T(8,128)S(1)}, u32[]{:S(2)}, u32[]{:S(2)}) collective-permute-start(f32[2,224,128]{2,1,0:T(8,128)} %collective-permute-done.2), channel_id=1, source_target_pairs={{0,2},{2,4},{4,6},{8,10},{10,12},{12,14},{16,18},{18,20},{20,22},{... | collective-permute-start | bytes 688136 | tf_op jit(solution)/shard_map/ppermute | solution.py:33
  131.1 1.9 %collective-permute-start.3 = (f32[2,224,128]{2,1,0:T(8,128)}, f32[2,224,128]{2,1,0:T(8,128)S(1)}, u32[]{:S(2)}, u32[]{:S(2)}) collective-permute-start(f32[2,224,128]{2,1,0:T(8,128)} %get-tuple-element.47), channel_id=1, source_target_pairs={{0,1},{1,2},{2,3},{3,4},{4,5},{5,6},{6,7},{8,9},{9,10},{10,11},{11... | collective-permute-start | bytes 688136 | tf_op jit(solution)/shard_map/ppermute | solution.py:27
  133.1 0.0 collective-permute-done.4
  133.1 15.1 %collective-permute-done.5 = f32[2,224,128]{2,1,0:T(8,128)S(1)} collective-permute-done((f32[2,224,128]{2,1,0:T(8,128)}, f32[2,224,128]{2,1,0:T(8,128)S(1)}, u32[]{:S(2)}, u32[]{:S(2)}) %collective-permute-start.5) | collective-permute-done | bytes 229408 | tf_op jit(solution)/shard_map/ppermute | solution.py:33
  148.2 0.9 collective-permute-done.3
  149.1 0.8 fusion.3
  149.9 0.0 all-to-all-done.2
  149.9 2.0 %fusion.1 = f32[1,1024,384]{2,1,0:T(8,128)} fusion(s32[]{:T(128)S(6)} %select_n.20, f32[1024,384]{1,0:T(8,128)S(1)} %bitcast.19), kind=kLoop, calls=%fused_computation.4 | loop fusion | flops 393216 | bytes 3145732 | tf_op jit(solution)/shard_map/broadcast_in_dim | solution.py:691
  (1 shorter events, 0.0 us)
Async XLA Ops:
  2.6 28.7 %collective-permute-start = (f32[2,1024,128]{2,1,0:T(8,128)}, f32[2,1024,128]{2,1,0:T(8,128)}, u32[]{:S(2)}, u32[]{:S(2)}) collective-permute-start(f32[2,1024,128]{2,1,0:T(8,128)} %margins.1), channel_id=1, source_target_pairs={{1,0},{2,1},{3,2},{4,3},{5,4},{6,5},{7,6},{9,8},{10,9},{11,10},{12... | collective-permute-start | bytes 3145736 | tf_op jit(solution)/shard_map/ppermute | solution.py:27
  12.5 28.1 %all-to-all-start = ((f32[32,32,128]{2,1,0:T(8,128)}), f32[32,32,128]{2,1,0:T(8,128)S(1)}, u32[]{:S(2)}, u32[]{:S(2)}) async-start(f32[32,32,128]{2,1,0:T(8,128)} %bitcast.28), calls=%async_computation | async-start | bytes 1048576 | tf_op jit(solution)/shard_map/all_to_all | solution.py:664
  40.3 8.5 %copy-start.4 = (s32[4]{0:T(128)S(1)}, s32[4]{0:T(128)}, u32[]{:S(2)}) copy-start(s32[4]{0:T(128)} %param.22) | copy-start | bytes 52
  40.5 21.8 %copy-start.3 = (f32[32,32,128]{2,1,0:T(8,128)}, f32[32,32,128]{2,1,0:T(8,128)S(1)}, u32[]{:S(2)}) copy-start(f32[32,32,128]{2,1,0:T(8,128)S(1)} %all-to-all-done.left_from) | copy-start | bytes 1572868
  40.5 42.2 %all-to-all-start.1 = ((f32[32,32,384]{2,1,0:T(8,128)}), f32[32,32,384]{2,1,0:T(8,128)S(1)}, u32[]{:S(2)}, u32[]{:S(2)}) async-start(f32[32,32,384]{2,1,0:T(8,128)} %bitcast.21), calls=%async_computation.1 | async-start | bytes 3145728 | tf_op jit(solution)/shard_map/all_to_all | solution.py:664
  50.1 32.6 %copy-start.5 = (f32[2,576,128]{2,1,0:T(8,128)S(1)}, f32[2,576,128]{2,1,0:T(8,128)}, u32[]{:S(2)}) copy-start(f32[2,576,128]{2,1,0:T(8,128)} %get-tuple-element.36) | copy-start | bytes 1769476
  82.7 4.5 %copy-start = (f32[32,32,384]{2,1,0:T(8,128)}, f32[32,32,384]{2,1,0:T(8,128)S(1)}, u32[]{:S(2)}) copy-start(f32[32,32,384]{2,1,0:T(8,128)S(1)} %all-to-all-done.1.right_from) | copy-start | bytes 4718596
  82.7 17.1 %collective-permute-start.1 = (f32[2,576,128]{2,1,0:T(8,128)S(1)}, f32[2,576,128]{2,1,0:T(8,128)S(1)}, u32[]{:S(2)}, u32[]{:S(2)}) collective-permute-start(f32[2,576,128]{2,1,0:T(8,128)S(1)} %copy-done.5), channel_id=1, source_target_pairs={{0,1},{1,2},{2,3},{3,4},{4,5},{5,6},{6,7},{8,9},{9,10},{10,11},{11... | collective-permute-start | bytes 1769480 | tf_op jit(solution)/shard_map/ppermute | solution.py:27
  99.9 50.1 %all-to-all-start.2 = ((f32[32,32,384]{2,1,0:T(8,128)}), f32[32,32,384]{2,1,0:T(8,128)S(1)}, u32[]{:S(2)}, u32[]{:S(2)}) async-start(f32[32,32,384]{2,1,0:T(8,128)} %get-tuple-element.45), calls=%async_computation.2 | async-start | bytes 3145728 | tf_op jit(solution)/shard_map/all_to_all | solution.py:664
  108.0 14.2 %copy-start.1 = (f32[2,1024,128]{2,1,0:T(8,128)S(1)}, f32[2,1024,128]{2,1,0:T(8,128)}, u32[]{:S(2)}) copy-start(f32[2,1024,128]{2,1,0:T(8,128)} %get-tuple-element.41) | copy-start | bytes 3145732
  116.1 6.2 %copy-start.2 = (f32[2,1024,256]{2,1,0:T(8,128)S(1)}, f32[2,1024,256]{2,1,0:T(8,128)}, u32[]{:S(2)}) copy-start(f32[2,1024,256]{2,1,0:T(8,128)} %get-tuple-element.43) | copy-start | bytes 6291460
  116.1 10.6 %collective-permute-start.2 = (f32[2,224,128]{2,1,0:T(8,128)}, f32[2,224,128]{2,1,0:T(8,128)}, u32[]{:S(2)}, u32[]{:S(2)}) collective-permute-start(f32[2,224,128]{2,1,0:T(8,128)} %get-tuple-element.39), channel_id=1, source_target_pairs={{1,0},{3,2},{5,4},{7,6},{9,8},{11,10},{13,12},{15,14},{17,16},{19,... | collective-permute-start | bytes 688136 | tf_op jit(solution)/shard_map/ppermute | solution.py:33
  117.5 15.6 %collective-permute-start.4 = (f32[2,224,128]{2,1,0:T(8,128)}, f32[2,224,128]{2,1,0:T(8,128)S(1)}, u32[]{:S(2)}, u32[]{:S(2)}) collective-permute-start(f32[2,224,128]{2,1,0:T(8,128)} %get-tuple-element.39), channel_id=1, source_target_pairs={{0,1},{2,3},{4,5},{6,7},{8,9},{10,11},{12,13},{14,15},{16,17},{18,... | collective-permute-start | bytes 688136 | tf_op jit(solution)/shard_map/ppermute | solution.py:33
  126.6 21.5 %collective-permute-start.5 = (f32[2,224,128]{2,1,0:T(8,128)}, f32[2,224,128]{2,1,0:T(8,128)S(1)}, u32[]{:S(2)}, u32[]{:S(2)}) collective-permute-start(f32[2,224,128]{2,1,0:T(8,128)} %collective-permute-done.2), channel_id=1, source_target_pairs={{0,2},{2,4},{4,6},{8,10},{10,12},{12,14},{16,18},{18,20},{20,22},{... | collective-permute-start | bytes 688136 | tf_op jit(solution)/shard_map/ppermute | solution.py:33
  131.1 18.0 %collective-permute-start.3 = (f32[2,224,128]{2,1,0:T(8,128)}, f32[2,224,128]{2,1,0:T(8,128)S(1)}, u32[]{:S(2)}, u32[]{:S(2)}) collective-permute-start(f32[2,224,128]{2,1,0:T(8,128)} %get-tuple-element.47), channel_id=1, source_target_pairs={{0,1},{1,2},{2,3},{3,4},{4,5},{5,6},{6,7},{8,9},{9,10},{10,11},{11... | collective-permute-start | bytes 688136 | tf_op jit(solution)/shard_map/ppermute | solution.py:27

commit v7 on v6

--- a/solution.py
+++ b/solution.py
@@ -382,8 +382,7 @@
     if beyond:
         operands = (*tile, edge, begun)
         early = height * 9 // 16 // SUBLANES * SUBLANES
-        late = (height - early) // 2 // SUBLANES * SUBLANES
-        spills = [out(2, rows, LANES) for rows in (early, late, height - early - late)]
+        spills = [out(2, rows, LANES) for rows in (early, height - early)]
         outs = (out(2, height, width - LANES), *spills, out(height, width))
         base = LANES
     else:
@@ -485,26 +484,16 @@
 
 
 def step_kernel(
-    turned, whole, frac, left_from, right_from, old, parts, update,
-    near, cells, left, right, before, after, sems, level_sems,
+    turned, whole, frac, left, right, old, parts, update,
+    near, cells, before, after, sems, level_sems,
 ):
     old_copy = pltpu.make_async_copy(old, before, sems.at[0, 0])
     depth = cells.shape[0]
     tilts = near.shape[0]
-    tiles = right_from.shape[0] // tilts
-    own = right_from.shape[2] // LANES
+    tiles = right.shape[0] // tilts
+    own = right.shape[2] // LANES
     band = turned.band
 
-    def fetch(tilt):
-        block = pl.ds(tilt * tiles, tiles)
-        return [
-            pltpu.make_async_copy(source.at[block], target.at[block], sems.at[2 + n, tilt])
-            for n, (source, target) in enumerate(((left_from, left), (right_from, right)))
-        ]
-
-    for tilt in range(tilts):
-        for copy in fetch(tilt):
-            copy.start()
     old_copy.start()
 
     def place(block, segment):
@@ -512,8 +501,6 @@
 
     @pl.loop(0, tilts)
     def _(tilt):
-        for copy in fetch(tilt):
-            copy.wait()
         for block in range(turned.blocks):
             cut = []
             for segment in range(turned.segments):
@@ -615,19 +602,17 @@
             jax.ShapeDtypeStruct(right.shape, jnp.float32),
             jax.ShapeDtypeStruct((depth, turned.length, LANES), jnp.float32),
         ),
-        in_specs=[SMEM, SMEM, ANY, ANY, HBM],
+        in_specs=[SMEM, SMEM, VMEM, VMEM, HBM],
         out_specs=(HBM, HBM),
         scratch_shapes=[
             turned.scratch(tilts), turned.scratch(depth),
-            pltpu.VMEM(left.shape, jnp.float32),
-            pltpu.VMEM(right.shape, jnp.float32),
             pltpu.VMEM(old.shape, jnp.float32),
             pltpu.VMEM(right.shape, jnp.float32),
-            pltpu.SemaphoreType.DMA((4, tilts)),
+            pltpu.SemaphoreType.DMA((2, tilts)),
             pltpu.SemaphoreType.DMA((depth,)),
         ],
         name="volume_step",
-        **kernel_options(16 * depth * old.size, 4 * depth * turned.length * LANES, 9 / 10),
+        **kernel_options(16 * depth * old.size, 4 * depth * turned.length * LANES, 1),
     )(whole, frac, left, right, old)
 
 
@@ -666,28 +651,24 @@
     edge = passed_along(margins(*tile), "tile", -1)
     grad_left, begun, left = probe_phase(*within, tile, None, None, probe, intensity[0])
     left = exchanged(left.reshape(devices, band, LANES))
-    grad_right, early, late, relayed, right = probe_phase(*within, tile, edge, begun, probe, intensity[0])
+    grad_right, early, late, right = probe_phase(*within, tile, edge, begun, probe, intensity[0])
     right, left, slope = lax.optimization_barrier((right, left, slope))
     whole, frac = shift_tables(slope, depth)
     right = exchanged(right.reshape(devices, band, width))
     old = old_projection(turned, whole, frac, volume)
-    right, early, old = lax.optimization_barrier((right, early, old))
+    straight = passed_by(late, "tile", 0, 1)
+    back = passed_by(late, "tile", 1, -1)
+    right, early, old, straight, back = lax.optimization_barrier(
+        (right, early, old, straight, back)
+    )
     early = passed_along(early, "tile", 1)
+    relayed = passed_by(back, "tile", 0, 2)
     parts, update = volume_step(turned, whole, frac, left, right, old)
-    parts, early, late, relayed = lax.optimization_barrier((parts, early, late, relayed))
-    late = passed_along(late, "tile", 1)
-    straight = passed_by(relayed, "tile", 0, 1)
-    relayed = passed_by(relayed, "tile", 1, -1)
+    parts, early, relayed = lax.optimization_barrier((parts, early, relayed))
     returned = exchanged(parts)
     fresh = fresh_volume(turned, volume, update)
-    rows = early.shape[1]
-    early = jnp.pad(early, ((0, 0), (0, height - rows), (0, 0)))
-    grad = jnp.concatenate([grad_left + early, grad_right], axis=2)[:, None]
-    relayed, fresh, grad = lax.optimization_barrier((relayed, fresh, grad))
-    relayed = straight + passed_by(relayed, "tile", 0, 2)
-    late = jnp.concatenate([late, relayed], axis=1)
-    late = (late + grad_left[:, rows:])[:, None]
-    grad = lax.dynamic_update_slice(grad, late, (0, 0, rows, 0))
+    spill = jnp.concatenate([early, straight + relayed], axis=1)
+    grad = jnp.concatenate([grad_left + spill, grad_right], axis=2)[:, None]
     reprojection = jnp.roll(returned.reshape(height, width), -row_shift[0], axis=0)[None]
     return (fresh, reprojection, grad)
 

time: 153 us -> 153 us (level)
  the two profiles are of different devices: /device:TPU:17 before, /device:TPU:0 now
where the time goes in v7:
time: 153 us; the launch traced here: 155 us
  waiting for transfers between devices  58.8 us (38%)
  Pallas kernels  49.7 us (32%)
  starting transfers between devices  36 us (24%)
  other arithmetic  6.46 us (4%)
  between operations  2.14 us (1%)
  local copies, waits for them, and re-layouts  1.93 us (1%)
    all_to_all x3, waiting for transfers between devices, exchanged(): return lax.all_to_all(blocks, axes, split_axis=0, concat_axis=0, tiled=True)  39.8 us
    all_to_all x3, starting transfers between devices, exchanged(): return lax.all_to_all(blocks, axes, split_axis=0, concat_axis=0, tiled=True)  25.9 us
    pallas_call x2, Pallas kernels, probe_phase(): pl.pallas_call(functools.partial(probe_kernel, base=base, beyond=beyond),...  15.1 us
    pallas_call x1, Pallas kernels, volume_step(): pl.pallas_call(functools.partial(step_kernel, turned), out_shape=(jax.Sha...  12.3 us
    pallas_call x1, Pallas kernels, old_projection(): pl.pallas_call(functools.partial(old_kernel, turned), out_shape=jax.Shape...  12.3 us
    ppermute x2, waiting for transfers between devices, passed_along(): return lax.ppermute(block, axis, route)  9.83 us
    ppermute x3, waiting for transfers between devices, passed_by(): return lax.ppermute(block, axis, route)  9.18 us
    pallas_call x1, Pallas kernels, fresh_volume(): pl.pallas_call(functools.partial(fresh_kernel, turned), grid=(depth // le...  8.13 us
  transfers between devices with their start and end apart: 8, of which 6 were waited for; matrix products, arithmetic and copies ran while one was open for 3% of the time, Pallas kernels for 31%

profile of v7, /device:TPU:0, one launch (start us, length us, event | category | flops | bytes accessed | tf_op | source)
XLA Modules:
  0.0 155.1 jit_solution(11376961779181814907)
XLA Ops:
  0.6 1.9 %margins.1 = f32[2,1024,128]{2,1,0:T(8,128)} custom-call(f32[1024,384]{1,0:T(8,128)} %bitcast.18, f32[1024,384]{1,0:T(8,128)} %bitcast.21), custom_call_target="tpu_custom_call" | custom-call | tf_op jit(solution)/shard_map/margins/pallas_call | solution.py:357
  2.6 1.3 collective-permute-start
  5.2 7.6 %probes_within.1 = (f32[2,1024,128]{2,1,0:T(8,128)}, f32[2,2,1024,128]{3,2,1,0:T(8,128)}, f32[1024,128]{1,0:T(8,128)}) custom-call(s32[1,1]{1,0:T(1,128)S(6)} %copy.18.used_ref, s32[1,2,8]{2,1,0:T(2,128)} %bitcast.27, s32[1]{0:T(128)} %copy.19.shift_ref, f32[1024,384]{1,0:T(8,128)} %bitcast.19, f32[1024,384]{1,0:T(8,128)} %bitcast.22, f32[256,256]{1,0:T(8,128)} %refs_4_.1, ...), custom_call_target="tpu_custom_call" | custom-call | flops 3489660928 | bytes 6291456 | tf_op jit(solution)/shard_map/probes_within/pallas_call | solution.py:392
  12.7 12.7 %all-to-all-start = ((f32[32,32,128]{2,1,0:T(8,128)}), f32[32,32,128]{2,1,0:T(8,128)S(1)}, u32[]{:S(2)}, u32[]{:S(2)}) async-start(f32[32,32,128]{2,1,0:T(8,128)} %bitcast.24), calls=%async_computation | async-start | bytes 1048576 | tf_op jit(solution)/shard_map/all_to_all | solution.py:649
  25.4 9.8 %collective-permute-done.refs_2_ = f32[2,1024,128]{2,1,0:T(8,128)} collective-permute-done((f32[2,1024,128]{2,1,0:T(8,128)}, f32[2,1024,128]{2,1,0:T(8,128)}, u32[]{:S(2)}, u32[]{:S(2)}) %collective-permute-start) | collective-permute-done | bytes 1048608 | tf_op jit(solution)/shard_map/ppermute | solution.py:27
  35.2 7.5 %probes_beyond.1 = (f32[2,1024,256]{2,1,0:T(8,128)}, f32[2,576,128]{2,1,0:T(8,128)}, f32[2,448,128]{2,1,0:T(8,128)}, f32[1024,384]{1,0:T(8,128)}) custom-call(s32[1,1]{1,0:T(1,128)S(6)} %copy.18.used_ref, s32[1,2,8]{2,1,0:T(2,128)} %bitcast.28, s32[1]{0:T(128)} %copy.19.shift_ref, f32[1024,384]{1,0:T(8,128)} %bitcast.20, f32[1024,384]{1,0:T(8,128)} %bitcast.23, ...), custom_call_target="tpu_custom_call" | custom-call | flops 3489660928 | bytes 6291456 | tf_op jit(solution)/shard_map/probes_beyond/pallas_call | solution.py:392
  42.7 0.0 copy-start.8
  42.8 0.0 copy-start.7
  42.8 2.4 %all-to-all-done.left = f32[32,32,128]{2,1,0:T(8,128)S(1)} async-done(((f32[32,32,128]{2,1,0:T(8,128)}), f32[32,32,128]{2,1,0:T(8,128)S(1)}, u32[]{:S(2)}, u32[]{:S(2)}) %all-to-all-start) | async-done | bytes 524320 | tf_op jit(solution)/shard_map/all_to_all | solution.py:649
  45.2 0.0 copy-start.2
  45.2 9.7 %all-to-all-start.1 = ((f32[32,32,384]{2,1,0:T(8,128)}), f32[32,32,384]{2,1,0:T(8,128)S(1)}, u32[]{:S(2)}, u32[]{:S(2)}) async-start(f32[32,32,384]{2,1,0:T(8,128)} %bitcast.17), calls=%async_computation.1 | async-start | bytes 3145728 | tf_op jit(solution)/shard_map/all_to_all | solution.py:649
  54.8 0.0 copy-done.8
  54.9 3.7 %collective-permute-start.1 = (f32[2,448,128]{2,1,0:T(8,128)S(1)}, f32[2,448,128]{2,1,0:T(8,128)S(1)}, u32[]{:S(2)}, u32[]{:S(2)}) collective-permute-start(f32[2,448,128]{2,1,0:T(8,128)S(1)} %copy-done.8), channel_id=1, source_target_pairs={{0,1},{2,3},{4,5},{6,7},{8,9},{10,11},{12,13},{14,15},{16,17},{18,... | collective-permute-start | bytes 1376264 | tf_op jit(solution)/shard_map/ppermute | solution.py:33
  58.6 1.3 collective-permute-start.2
  59.9 0.0 copy-done.7
  59.9 0.6 add_select_fusion.whole
  60.5 0.7 convert_multiply_fusion.frac
  61.1 12.3 %old_projection.1.old = f32[4,768,128]{2,1,0:T(8,128)} custom-call(s32[4,16]{1,0:T(4,128)} %add_select_fusion.whole, f32[4,16]{1,0:T(4,128)} %convert_multiply_fusion.frac, f32[16,32,3072]{2,1,0:T(8,128)} %volume.3), custom_call_target="tpu_custom_call" | custom-call | flops 50331648 | bytes 6291456 | tf_op jit(solution)/shard_map/old_projection/pallas_call | solution.py:586
  73.4 0.0 copy-done.2
  73.4 4.6 %collective-permute-done.1 = f32[2,448,128]{2,1,0:T(8,128)S(1)} collective-permute-done((f32[2,448,128]{2,1,0:T(8,128)S(1)}, f32[2,448,128]{2,1,0:T(8,128)S(1)}, u32[]{:S(2)}, u32[]{:S(2)}) %collective-permute-start.1) | collective-permute-done | bytes 458784 | tf_op jit(solution)/shard_map/ppermute | solution.py:33
  78.1 0.0 copy-start.4
  78.1 0.8 copy-done.4
  78.8 4.5 %collective-permute-done.2 = f32[2,448,128]{2,1,0:T(8,128)S(1)} collective-permute-done((f32[2,448,128]{2,1,0:T(8,128)S(1)}, f32[2,448,128]{2,1,0:T(8,128)S(1)}, u32[]{:S(2)}, u32[]{:S(2)}) %collective-permute-start.2) | collective-permute-done | bytes 458784 | tf_op jit(solution)/shard_map/ppermute | solution.py:33
  83.4 10.3 %all-to-all-done.1.right = f32[32,32,384]{2,1,0:T(8,128)S(1)} async-done(((f32[32,32,384]{2,1,0:T(8,128)}), f32[32,32,384]{2,1,0:T(8,128)S(1)}, u32[]{:S(2)}, u32[]{:S(2)}) %all-to-all-start.1) | async-done | bytes 1572896 | tf_op jit(solution)/shard_map/all_to_all | solution.py:649
  93.7 0.0 copy-start
  93.7 2.3 %collective-permute-start.3 = (f32[2,576,128]{2,1,0:T(8,128)}, f32[2,576,128]{2,1,0:T(8,128)S(1)}, u32[]{:S(2)}, u32[]{:S(2)}) collective-permute-start(f32[2,576,128]{2,1,0:T(8,128)} %get-tuple-element.35), channel_id=1, source_target_pairs={{0,1},{1,2},{2,3},{3,4},{4,5},{5,6},{6,7},{8,9},{9,10},{10,11},{11... | collective-permute-start | bytes 1769480 | tf_op jit(solution)/shard_map/ppermute | solution.py:27
  96.0 1.5 collective-permute-start.4
  97.5 0.0 copy-done
  97.6 12.3 %volume_step.1 = (f32[32,32,384]{2,1,0:T(8,128)}, f32[16,768,128]{2,1,0:T(8,128)}) custom-call(s32[4,16]{1,0:T(4,128)} %add_select_fusion.whole, f32[4,16]{1,0:T(4,128)} %convert_multiply_fusion.frac, f32[32,32,128]{2,1,0:T(8,128)} %copy-done.2, f32[32,32,384]{2,1,0:T(8,128)} %copy-done, f32[4,768,128]{2,1,0:T(8,128)} %old_projection.1.old), custom_call_target="tpu_custom_call" | custom-call | flops 100663296 | bytes 6291456 | tf_op jit(solution)/shard_map/volume_step/pallas_call | solution.py:599
  109.9 0.0 collective-permute-done.4
  109.9 0.0 copy-start.6
  109.9 0.0 collective-permute-done.3
  109.9 0.7 copy-done.6
  110.7 3.6 %all-to-all-start.2 = ((f32[32,32,384]{2,1,0:T(8,128)}), f32[32,32,384]{2,1,0:T(8,128)S(1)}, u32[]{:S(2)}, u32[]{:S(2)}) async-start(f32[32,32,384]{2,1,0:T(8,128)} %get-tuple-element.37), calls=%async_computation.2 | async-start | bytes 3145728 | tf_op jit(solution)/shard_map/all_to_all | solution.py:649
  114.3 0.0 copy-start.5
  114.3 0.0 copy-start.3
  114.3 8.1 %fresh_volume.1 = f32[16,32,3072]{2,1,0:T(8,128)} custom-call(f32[16,32,3072]{2,1,0:T(8,128)} %volume.3, f32[16,768,128]{2,1,0:T(8,128)} %get-tuple-element.33.update), custom_call_target="tpu_custom_call" | custom-call | flops 1572864 | bytes 18874368 | tf_op jit(solution)/shard_map/fresh_volume/pallas_call | solution.py:624
  122.4 0.0 copy-done.5
  122.4 0.0 copy-start.1
  122.4 1.2 add.19
  123.6 0.0 copy-done.3
  123.6 0.1 maximum_add_fusion
  123.8 0.4 copy-done.1
  124.1 1.9 %maximum_bitcast_fusion = f32[2,1,1024,384]{3,2,1,0:T(8,128)} fusion(f32[2,1024,256]{2,1,0:T(8,128)S(1)} %copy-done.1, f32[2,1024,128]{2,1,0:T(8,128)S(1)} %maximum_add_fusion), kind=kLoop, calls=%fused_computation.2 | loop fusion | flops 786432 | bytes 6291456
  126.0 27.1 %all-to-all-done.2 = f32[32,32,384]{2,1,0:T(8,128)S(1)} async-done(((f32[32,32,384]{2,1,0:T(8,128)}), f32[32,32,384]{2,1,0:T(8,128)S(1)}, u32[]{:S(2)}, u32[]{:S(2)}) %all-to-all-start.2) | async-done | bytes 1572896 | tf_op jit(solution)/shard_map/all_to_all | solution.py:649
  153.1 2.0 %fusion.1 = f32[1,1024,384]{2,1,0:T(8,128)} fusion(s32[]{:T(128)S(6)} %select_n.20, f32[1024,384]{1,0:T(8,128)S(1)} %bitcast.16), kind=kLoop, calls=%fused_computation.4 | loop fusion | flops 393216 | bytes 3145732 | tf_op jit(solution)/shard_map/broadcast_in_dim | solution.py:672
Async XLA Ops:
  2.6 32.6 %collective-permute-start = (f32[2,1024,128]{2,1,0:T(8,128)}, f32[2,1024,128]{2,1,0:T(8,128)}, u32[]{:S(2)}, u32[]{:S(2)}) collective-permute-start(f32[2,1024,128]{2,1,0:T(8,128)} %margins.1), channel_id=1, source_target_pairs={{1,0},{2,1},{3,2},{4,3},{5,4},{6,5},{7,6},{9,8},{10,9},{11,10},{12... | collective-permute-start | bytes 3145736 | tf_op jit(solution)/shard_map/ppermute | solution.py:27
  12.7 32.4 %all-to-all-start = ((f32[32,32,128]{2,1,0:T(8,128)}), f32[32,32,128]{2,1,0:T(8,128)S(1)}, u32[]{:S(2)}, u32[]{:S(2)}) async-start(f32[32,32,128]{2,1,0:T(8,128)} %bitcast.24), calls=%async_computation | async-start | bytes 1048576 | tf_op jit(solution)/shard_map/all_to_all | solution.py:649
  42.7 12.1 %copy-start.8 = (f32[2,448,128]{2,1,0:T(8,128)S(1)}, f32[2,448,128]{2,1,0:T(8,128)}, u32[]{:S(2)}) copy-start(f32[2,448,128]{2,1,0:T(8,128)} %get-tuple-element.30) | copy-start | bytes 1376260
  42.8 17.1 %copy-start.7 = (s32[4]{0:T(128)S(1)}, s32[4]{0:T(128)}, u32[]{:S(2)}) copy-start(s32[4]{0:T(128)} %param.22) | copy-start | bytes 52
  45.2 28.3 %copy-start.2 = (f32[32,32,128]{2,1,0:T(8,128)}, f32[32,32,128]{2,1,0:T(8,128)S(1)}, u32[]{:S(2)}) copy-start(f32[32,32,128]{2,1,0:T(8,128)S(1)} %all-to-all-done.left) | copy-start | bytes 1572868
  45.2 48.5 %all-to-all-start.1 = ((f32[32,32,384]{2,1,0:T(8,128)}), f32[32,32,384]{2,1,0:T(8,128)S(1)}, u32[]{:S(2)}, u32[]{:S(2)}) async-start(f32[32,32,384]{2,1,0:T(8,128)} %bitcast.17), calls=%async_computation.1 | async-start | bytes 3145728 | tf_op jit(solution)/shard_map/all_to_all | solution.py:649
  54.9 23.2 %collective-permute-start.1 = (f32[2,448,128]{2,1,0:T(8,128)S(1)}, f32[2,448,128]{2,1,0:T(8,128)S(1)}, u32[]{:S(2)}, u32[]{:S(2)}) collective-permute-start(f32[2,448,128]{2,1,0:T(8,128)S(1)} %copy-done.8), channel_id=1, source_target_pairs={{0,1},{2,3},{4,5},{6,7},{8,9},{10,11},{12,13},{14,15},{16,17},{18,... | collective-permute-start | bytes 1376264 | tf_op jit(solution)/shard_map/ppermute | solution.py:33
  58.6 24.8 %collective-permute-start.2 = (f32[2,448,128]{2,1,0:T(8,128)S(1)}, f32[2,448,128]{2,1,0:T(8,128)S(1)}, u32[]{:S(2)}, u32[]{:S(2)}) collective-permute-start(f32[2,448,128]{2,1,0:T(8,128)S(1)} %copy-done.8), channel_id=1, source_target_pairs={{1,0},{3,2},{5,4},{7,6},{9,8},{11,10},{13,12},{15,14},{17,16},{19,... | collective-permute-start | bytes 1376264 | tf_op jit(solution)/shard_map/ppermute | solution.py:33
  78.1 0.8 copy-start.4
  93.7 3.9 %copy-start = (f32[32,32,384]{2,1,0:T(8,128)}, f32[32,32,384]{2,1,0:T(8,128)S(1)}, u32[]{:S(2)}) copy-start(f32[32,32,384]{2,1,0:T(8,128)S(1)} %all-to-all-done.1.right) | copy-start | bytes 4718596
  93.7 16.2 %collective-permute-start.3 = (f32[2,576,128]{2,1,0:T(8,128)}, f32[2,576,128]{2,1,0:T(8,128)S(1)}, u32[]{:S(2)}, u32[]{:S(2)}) collective-permute-start(f32[2,576,128]{2,1,0:T(8,128)} %get-tuple-element.35), channel_id=1, source_target_pairs={{0,1},{1,2},{2,3},{3,4},{4,5},{5,6},{6,7},{8,9},{9,10},{10,11},{11... | collective-permute-start | bytes 1769480 | tf_op jit(solution)/shard_map/ppermute | solution.py:27
  96.0 13.9 %collective-permute-start.4 = (f32[2,448,128]{2,1,0:T(8,128)S(1)}, f32[2,448,128]{2,1,0:T(8,128)S(1)}, u32[]{:S(2)}, u32[]{:S(2)}) collective-permute-start(f32[2,448,128]{2,1,0:T(8,128)S(1)} %collective-permute-done.2), channel_id=1, source_target_pairs={{0,2},{2,4},{4,6},{8,10},{10,12},{12,14},{16,18},{18,20},{20,22},{... | collective-permute-start | bytes 1376264 | tf_op jit(solution)/shard_map/ppermute | solution.py:33
  109.9 0.8 copy-start.6
  110.7 42.4 %all-to-all-start.2 = ((f32[32,32,384]{2,1,0:T(8,128)}), f32[32,32,384]{2,1,0:T(8,128)S(1)}, u32[]{:S(2)}, u32[]{:S(2)}) async-start(f32[32,32,384]{2,1,0:T(8,128)} %get-tuple-element.37), calls=%async_computation.2 | async-start | bytes 3145728 | tf_op jit(solution)/shard_map/all_to_all | solution.py:649
  114.3 8.1 %copy-start.5 = (f32[2,448,128]{2,1,0:T(8,128)S(1)}, f32[2,448,128]{2,1,0:T(8,128)}, u32[]{:S(2)}) copy-start(f32[2,448,128]{2,1,0:T(8,128)} %copy-done.4) | copy-start | bytes 1376260
  114.3 9.4 %copy-start.3 = (f32[2,1024,128]{2,1,0:T(8,128)S(1)}, f32[2,1024,128]{2,1,0:T(8,128)}, u32[]{:S(2)}) copy-start(f32[2,1024,128]{2,1,0:T(8,128)} %get-tuple-element.38) | copy-start | bytes 3145732
  122.4 1.7 %copy-start.1 = (f32[2,1024,256]{2,1,0:T(8,128)S(1)}, f32[2,1024,256]{2,1,0:T(8,128)}, u32[]{:S(2)}) copy-start(f32[2,1024,256]{2,1,0:T(8,128)} %get-tuple-element.42) | copy-start | bytes 6291460

commit v8 on v7

--- a/solution.py
+++ b/solution.py
@@ -277,13 +277,19 @@
 
     count = lax.fori_loop(0, used, enlist, 0)
 
-    @pl.loop(0, count // 2)
+    threes = jnp.logical_and(count % 2 == 1, count >= 3)
+
+    @pl.loop(0, count // 2 - threes.astype(jnp.int32))
     def _(pair):
         together(listed[2 * pair], listed[2 * pair + 1])
 
-    @pl.when(count % 2 == 1)
+    @pl.when(threes)
     def _():
-        together(listed[count - 1])
+        together(listed[count - 3], listed[count - 2], listed[count - 1])
+
+    @pl.when(count == 1)
+    def _():
+        together(listed[0])
 
     sent = []
 
@@ -400,8 +406,8 @@
             pltpu.VMEM((2, size, size), jnp.float32),
             pltpu.VMEM(tables.shape, SPLIT),
             plane,
-            pltpu.VMEM((2, 2, 2, size, LANES), jnp.float32),
-            pltpu.VMEM((2, 4, size, size), SPLIT),
+            pltpu.VMEM((3, 2, 2, size, LANES), jnp.float32),
+            pltpu.VMEM((3, 4, size, size), SPLIT),
             pltpu.VMEM((routing, 2 * height, LANES), jnp.float32),
             pltpu.VMEM((height, outs[-1].shape[1]), jnp.float32),
             pltpu.VMEM((2, columns - 1, height, LANES), jnp.float32),

time: 153 us -> 155 us (1.013); the launches traced: 155 us -> 153 us
  starting transfers between devices: 36 us -> 32.3 us
  waiting for transfers between devices: 58.8 us -> 60.5 us
    all_to_all x3, starting transfers between devices: 25.9 us -> 22.4 us  [exchanged(): return lax.all_to_all(blocks, axes, split_axis=0, concat_axis=0, tiled=True)]
    ppermute x2, waiting for transfers between devices: 9.83 us -> 12.1 us  [passed_along(): return lax.ppermute(block, axis, route)]
where the time goes in v8:
time: 155 us; the launch traced here: 153 us
  waiting for transfers between devices  60.5 us (39%)
  Pallas kernels  49.7 us (32%)
  starting transfers between devices  32.3 us (21%)
  other arithmetic  6.46 us (4%)
  between operations  2.14 us (1%)
  local copies, waits for them, and re-layouts  1.93 us (1%)
    all_to_all x3, waiting for transfers between devices, exchanged(): return lax.all_to_all(blocks, axes, split_axis=0, concat_axis=0, tiled=True)  39.2 us
    all_to_all x3, starting transfers between devices, exchanged(): return lax.all_to_all(blocks, axes, split_axis=0, concat_axis=0, tiled=True)  22.4 us
    pallas_call x2, Pallas kernels, probe_phase(): pl.pallas_call(functools.partial(probe_kernel, base=base, beyond=beyond),...  15 us
    pallas_call x1, Pallas kernels, volume_step(): pl.pallas_call(functools.partial(step_kernel, turned), out_shape=(jax.Sha...  12.3 us
    pallas_call x1, Pallas kernels, old_projection(): pl.pallas_call(functools.partial(old_kernel, turned), out_shape=jax.Shape...  12.2 us
    ppermute x2, waiting for transfers between devices, passed_along(): return lax.ppermute(block, axis, route)  12.1 us
    ppermute x3, waiting for transfers between devices, passed_by(): return lax.ppermute(block, axis, route)  9.22 us
    pallas_call x1, Pallas kernels, fresh_volume(): pl.pallas_call(functools.partial(fresh_kernel, turned), grid=(depth // le...  8.13 us
  transfers between devices with their start and end apart: 8, of which 6 were waited for; matrix products, arithmetic and copies ran while one was open for 3% of the time, Pallas kernels for 31%

profile of v8, /device:TPU:0, one launch (start us, length us, event | category | flops | bytes accessed | tf_op | source)
XLA Modules:
  0.0 153.0 jit_solution(7745693928782133772)
XLA Ops:
  0.6 1.9 %margins.1 = f32[2,1024,128]{2,1,0:T(8,128)} custom-call(f32[1024,384]{1,0:T(8,128)} %bitcast.18, f32[1024,384]{1,0:T(8,128)} %bitcast.21), custom_call_target="tpu_custom_call" | custom-call | tf_op jit(solution)/shard_map/margins/pallas_call | solution.py:363
  2.6 1.3 collective-permute-start
  5.2 7.5 %probes_within.1 = (f32[2,1024,128]{2,1,0:T(8,128)}, f32[2,2,1024,128]{3,2,1,0:T(8,128)}, f32[1024,128]{1,0:T(8,128)}) custom-call(s32[1,1]{1,0:T(1,128)S(6)} %copy.18.used_ref, s32[1,2,8]{2,1,0:T(2,128)} %bitcast.27, s32[1]{0:T(128)} %copy.19.shift_ref, f32[1024,384]{1,0:T(8,128)} %bitcast.19, f32[1024,384]{1,0:T(8,128)} %bitcast.22, f32[256,256]{1,0:T(8,128)} %refs_4_.1, ...), custom_call_target="tpu_custom_call" | custom-call | flops 3489660928 | bytes 6291456 | tf_op jit(solution)/shard_map/probes_within/pallas_call | solution.py:398
  12.7 11.0 %all-to-all-start = ((f32[32,32,128]{2,1,0:T(8,128)}), f32[32,32,128]{2,1,0:T(8,128)S(1)}, u32[]{:S(2)}, u32[]{:S(2)}) async-start(f32[32,32,128]{2,1,0:T(8,128)} %bitcast.24), calls=%async_computation | async-start | bytes 1048576 | tf_op jit(solution)/shard_map/all_to_all | solution.py:655
  23.8 12.1 %collective-permute-done.refs_2_ = f32[2,1024,128]{2,1,0:T(8,128)} collective-permute-done((f32[2,1024,128]{2,1,0:T(8,128)}, f32[2,1024,128]{2,1,0:T(8,128)}, u32[]{:S(2)}, u32[]{:S(2)}) %collective-permute-start) | collective-permute-done | bytes 1048608 | tf_op jit(solution)/shard_map/ppermute | solution.py:27
  35.8 7.5 %probes_beyond.1 = (f32[2,1024,256]{2,1,0:T(8,128)}, f32[2,576,128]{2,1,0:T(8,128)}, f32[2,448,128]{2,1,0:T(8,128)}, f32[1024,384]{1,0:T(8,128)}) custom-call(s32[1,1]{1,0:T(1,128)S(6)} %copy.18.used_ref, s32[1,2,8]{2,1,0:T(2,128)} %bitcast.28, s32[1]{0:T(128)} %copy.19.shift_ref, f32[1024,384]{1,0:T(8,128)} %bitcast.20, f32[1024,384]{1,0:T(8,128)} %bitcast.23, ...), custom_call_target="tpu_custom_call" | custom-call | flops 3489660928 | bytes 6291456 | tf_op jit(solution)/shard_map/probes_beyond/pallas_call | solution.py:398
  43.3 0.0 copy-start.8
  43.4 0.0 copy-start.7
  43.4 1.8 %all-to-all-done.left = f32[32,32,128]{2,1,0:T(8,128)S(1)} async-done(((f32[32,32,128]{2,1,0:T(8,128)}), f32[32,32,128]{2,1,0:T(8,128)S(1)}, u32[]{:S(2)}, u32[]{:S(2)}) %all-to-all-start) | async-done | bytes 524320 | tf_op jit(solution)/shard_map/all_to_all | solution.py:655
  45.2 0.0 copy-start.2
  45.2 7.6 %all-to-all-start.1 = ((f32[32,32,384]{2,1,0:T(8,128)}), f32[32,32,384]{2,1,0:T(8,128)S(1)}, u32[]{:S(2)}, u32[]{:S(2)}) async-start(f32[32,32,384]{2,1,0:T(8,128)} %bitcast.17), calls=%async_computation.1 | async-start | bytes 3145728 | tf_op jit(solution)/shard_map/all_to_all | solution.py:655
  52.8 0.0 copy-done.8
  52.8 3.7 %collective-permute-start.1 = (f32[2,448,128]{2,1,0:T(8,128)S(1)}, f32[2,448,128]{2,1,0:T(8,128)S(1)}, u32[]{:S(2)}, u32[]{:S(2)}) collective-permute-start(f32[2,448,128]{2,1,0:T(8,128)S(1)} %copy-done.8), channel_id=1, source_target_pairs={{0,1},{2,3},{4,5},{6,7},{8,9},{10,11},{12,13},{14,15},{16,17},{18,... | collective-permute-start | bytes 1376264 | tf_op jit(solution)/shard_map/ppermute | solution.py:33
  56.5 1.3 collective-permute-start.2
  57.8 0.0 copy-done.7
  57.8 0.6 add_select_fusion.whole
  58.4 0.7 convert_multiply_fusion.frac
  59.1 12.2 %old_projection.1.old = f32[4,768,128]{2,1,0:T(8,128)} custom-call(s32[4,16]{1,0:T(4,128)} %add_select_fusion.whole, f32[4,16]{1,0:T(4,128)} %convert_multiply_fusion.frac, f32[16,32,3072]{2,1,0:T(8,128)} %volume.3), custom_call_target="tpu_custom_call" | custom-call | flops 50331648 | bytes 6291456 | tf_op jit(solution)/shard_map/old_projection/pallas_call | solution.py:592
  71.3 0.0 copy-done.2
  71.3 4.7 %collective-permute-done.1 = f32[2,448,128]{2,1,0:T(8,128)S(1)} collective-permute-done((f32[2,448,128]{2,1,0:T(8,128)S(1)}, f32[2,448,128]{2,1,0:T(8,128)S(1)}, u32[]{:S(2)}, u32[]{:S(2)}) %collective-permute-start.1) | collective-permute-done | bytes 458784 | tf_op jit(solution)/shard_map/ppermute | solution.py:33
  76.0 0.0 copy-start.4
  76.0 0.8 copy-done.4
  76.8 4.5 %collective-permute-done.2 = f32[2,448,128]{2,1,0:T(8,128)S(1)} collective-permute-done((f32[2,448,128]{2,1,0:T(8,128)S(1)}, f32[2,448,128]{2,1,0:T(8,128)S(1)}, u32[]{:S(2)}, u32[]{:S(2)}) %collective-permute-start.2) | collective-permute-done | bytes 458784 | tf_op jit(solution)/shard_map/ppermute | solution.py:33
  81.3 10.3 %all-to-all-done.1.right = f32[32,32,384]{2,1,0:T(8,128)S(1)} async-done(((f32[32,32,384]{2,1,0:T(8,128)}), f32[32,32,384]{2,1,0:T(8,128)S(1)}, u32[]{:S(2)}, u32[]{:S(2)}) %all-to-all-start.1) | async-done | bytes 1572896 | tf_op jit(solution)/shard_map/all_to_all | solution.py:655
  91.6 0.0 copy-start
  91.6 2.3 %collective-permute-start.3 = (f32[2,576,128]{2,1,0:T(8,128)}, f32[2,576,128]{2,1,0:T(8,128)S(1)}, u32[]{:S(2)}, u32[]{:S(2)}) collective-permute-start(f32[2,576,128]{2,1,0:T(8,128)} %get-tuple-element.35), channel_id=1, source_target_pairs={{0,1},{1,2},{2,3},{3,4},{4,5},{5,6},{6,7},{8,9},{9,10},{10,11},{11... | collective-permute-start | bytes 1769480 | tf_op jit(solution)/shard_map/ppermute | solution.py:27
  94.0 1.3 collective-permute-start.4
  95.3 0.0 copy-done
  95.3 12.3 %volume_step.1 = (f32[32,32,384]{2,1,0:T(8,128)}, f32[16,768,128]{2,1,0:T(8,128)}) custom-call(s32[4,16]{1,0:T(4,128)} %add_select_fusion.whole, f32[4,16]{1,0:T(4,128)} %convert_multiply_fusion.frac, f32[32,32,128]{2,1,0:T(8,128)} %copy-done.2, f32[32,32,384]{2,1,0:T(8,128)} %copy-done, f32[4,768,128]{2,1,0:T(8,128)} %old_projection.1.old), custom_call_target="tpu_custom_call" | custom-call | flops 100663296 | bytes 6291456 | tf_op jit(solution)/shard_map/volume_step/pallas_call | solution.py:605
  107.6 0.0 collective-permute-done.4
  107.6 0.0 copy-start.6
  107.7 0.0 collective-permute-done.3
  107.7 0.7 copy-done.6
  108.4 3.7 %all-to-all-start.2 = ((f32[32,32,384]{2,1,0:T(8,128)}), f32[32,32,384]{2,1,0:T(8,128)S(1)}, u32[]{:S(2)}, u32[]{:S(2)}) async-start(f32[32,32,384]{2,1,0:T(8,128)} %get-tuple-element.37), calls=%async_computation.2 | async-start | bytes 3145728 | tf_op jit(solution)/shard_map/all_to_all | solution.py:655
  112.2 0.0 copy-start.5
  112.2 0.0 copy-start.3
  112.2 8.1 %fresh_volume.1 = f32[16,32,3072]{2,1,0:T(8,128)} custom-call(f32[16,32,3072]{2,1,0:T(8,128)} %volume.3, f32[16,768,128]{2,1,0:T(8,128)} %get-tuple-element.33.update), custom_call_target="tpu_custom_call" | custom-call | flops 1572864 | bytes 18874368 | tf_op jit(solution)/shard_map/fresh_volume/pallas_call | solution.py:630
  120.3 0.0 copy-done.5
  120.3 0.0 copy-start.1
  120.3 1.2 add.19
  121.6 0.0 copy-done.3
  121.6 0.1 maximum_add_fusion
  121.7 0.4 copy-done.1
  122.1 1.9 %maximum_bitcast_fusion = f32[2,1,1024,384]{3,2,1,0:T(8,128)} fusion(f32[2,1024,256]{2,1,0:T(8,128)S(1)} %copy-done.1, f32[2,1024,128]{2,1,0:T(8,128)S(1)} %maximum_add_fusion), kind=kLoop, calls=%fused_computation.2 | loop fusion | flops 786432 | bytes 6291456
  123.9 27.1 %all-to-all-done.2 = f32[32,32,384]{2,1,0:T(8,128)S(1)} async-done(((f32[32,32,384]{2,1,0:T(8,128)}), f32[32,32,384]{2,1,0:T(8,128)S(1)}, u32[]{:S(2)}, u32[]{:S(2)}) %all-to-all-start.2) | async-done | bytes 1572896 | tf_op jit(solution)/shard_map/all_to_all | solution.py:655
  151.0 2.0 %fusion.1 = f32[1,1024,384]{2,1,0:T(8,128)} fusion(s32[]{:T(128)S(6)} %select_n.20, f32[1024,384]{1,0:T(8,128)S(1)} %bitcast.16), kind=kLoop, calls=%fused_computation.4 | loop fusion | flops 393216 | bytes 3145732 | tf_op jit(solution)/shard_map/broadcast_in_dim | solution.py:678
Async XLA Ops:
  2.6 33.3 %collective-permute-start = (f32[2,1024,128]{2,1,0:T(8,128)}, f32[2,1024,128]{2,1,0:T(8,128)}, u32[]{:S(2)}, u32[]{:S(2)}) collective-permute-start(f32[2,1024,128]{2,1,0:T(8,128)} %margins.1), channel_id=1, source_target_pairs={{1,0},{2,1},{3,2},{4,3},{5,4},{6,5},{7,6},{9,8},{10,9},{11,10},{12... | collective-permute-start | bytes 3145736 | tf_op jit(solution)/shard_map/ppermute | solution.py:27
  12.7 32.4 %all-to-all-start = ((f32[32,32,128]{2,1,0:T(8,128)}), f32[32,32,128]{2,1,0:T(8,128)S(1)}, u32[]{:S(2)}, u32[]{:S(2)}) async-start(f32[32,32,128]{2,1,0:T(8,128)} %bitcast.24), calls=%async_computation | async-start | bytes 1048576 | tf_op jit(solution)/shard_map/all_to_all | solution.py:655
  43.3 9.4 %copy-start.8 = (f32[2,448,128]{2,1,0:T(8,128)S(1)}, f32[2,448,128]{2,1,0:T(8,128)}, u32[]{:S(2)}) copy-start(f32[2,448,128]{2,1,0:T(8,128)} %get-tuple-element.30) | copy-start | bytes 1376260
  43.4 14.4 %copy-start.7 = (s32[4]{0:T(128)S(1)}, s32[4]{0:T(128)}, u32[]{:S(2)}) copy-start(s32[4]{0:T(128)} %param.22) | copy-start | bytes 52
  45.2 26.1 %copy-start.2 = (f32[32,32,128]{2,1,0:T(8,128)}, f32[32,32,128]{2,1,0:T(8,128)S(1)}, u32[]{:S(2)}) copy-start(f32[32,32,128]{2,1,0:T(8,128)S(1)} %all-to-all-done.left) | copy-start | bytes 1572868
  45.2 46.5 %all-to-all-start.1 = ((f32[32,32,384]{2,1,0:T(8,128)}), f32[32,32,384]{2,1,0:T(8,128)S(1)}, u32[]{:S(2)}, u32[]{:S(2)}) async-start(f32[32,32,384]{2,1,0:T(8,128)} %bitcast.17), calls=%async_computation.1 | async-start | bytes 3145728 | tf_op jit(solution)/shard_map/all_to_all | solution.py:655
  52.8 23.2 %collective-permute-start.1 = (f32[2,448,128]{2,1,0:T(8,128)S(1)}, f32[2,448,128]{2,1,0:T(8,128)S(1)}, u32[]{:S(2)}, u32[]{:S(2)}) collective-permute-start(f32[2,448,128]{2,1,0:T(8,128)S(1)} %copy-done.8), channel_id=1, source_target_pairs={{0,1},{2,3},{4,5},{6,7},{8,9},{10,11},{12,13},{14,15},{16,17},{18,... | collective-permute-start | bytes 1376264 | tf_op jit(solution)/shard_map/ppermute | solution.py:33
  56.5 24.8 %collective-permute-start.2 = (f32[2,448,128]{2,1,0:T(8,128)S(1)}, f32[2,448,128]{2,1,0:T(8,128)S(1)}, u32[]{:S(2)}, u32[]{:S(2)}) collective-permute-start(f32[2,448,128]{2,1,0:T(8,128)S(1)} %copy-done.8), channel_id=1, source_target_pairs={{1,0},{3,2},{5,4},{7,6},{9,8},{11,10},{13,12},{15,14},{17,16},{19,... | collective-permute-start | bytes 1376264 | tf_op jit(solution)/shard_map/ppermute | solution.py:33
  76.0 0.8 copy-start.4
  91.6 3.7 %copy-start = (f32[32,32,384]{2,1,0:T(8,128)}, f32[32,32,384]{2,1,0:T(8,128)S(1)}, u32[]{:S(2)}) copy-start(f32[32,32,384]{2,1,0:T(8,128)S(1)} %all-to-all-done.1.right) | copy-start | bytes 4718596
  91.6 16.0 %collective-permute-start.3 = (f32[2,576,128]{2,1,0:T(8,128)}, f32[2,576,128]{2,1,0:T(8,128)S(1)}, u32[]{:S(2)}, u32[]{:S(2)}) collective-permute-start(f32[2,576,128]{2,1,0:T(8,128)} %get-tuple-element.35), channel_id=1, source_target_pairs={{0,1},{1,2},{2,3},{3,4},{4,5},{5,6},{6,7},{8,9},{9,10},{10,11},{11... | collective-permute-start | bytes 1769480 | tf_op jit(solution)/shard_map/ppermute | solution.py:27
  94.0 13.7 %collective-permute-start.4 = (f32[2,448,128]{2,1,0:T(8,128)S(1)}, f32[2,448,128]{2,1,0:T(8,128)S(1)}, u32[]{:S(2)}, u32[]{:S(2)}) collective-permute-start(f32[2,448,128]{2,1,0:T(8,128)S(1)} %collective-permute-done.2), channel_id=1, source_target_pairs={{0,2},{2,4},{4,6},{8,10},{10,12},{12,14},{16,18},{18,20},{20,22},{... | collective-permute-start | bytes 1376264 | tf_op jit(solution)/shard_map/ppermute | solution.py:33
  107.6 0.8 copy-start.6
  108.4 42.6 %all-to-all-start.2 = ((f32[32,32,384]{2,1,0:T(8,128)}), f32[32,32,384]{2,1,0:T(8,128)S(1)}, u32[]{:S(2)}, u32[]{:S(2)}) async-start(f32[32,32,384]{2,1,0:T(8,128)} %get-tuple-element.37), calls=%async_computation.2 | async-start | bytes 3145728 | tf_op jit(solution)/shard_map/all_to_all | solution.py:655
  112.2 8.1 %copy-start.5 = (f32[2,448,128]{2,1,0:T(8,128)S(1)}, f32[2,448,128]{2,1,0:T(8,128)}, u32[]{:S(2)}) copy-start(f32[2,448,128]{2,1,0:T(8,128)} %copy-done.4) | copy-start | bytes 1376260
  112.2 9.4 %copy-start.3 = (f32[2,1024,128]{2,1,0:T(8,128)S(1)}, f32[2,1024,128]{2,1,0:T(8,128)}, u32[]{:S(2)}) copy-start(f32[2,1024,128]{2,1,0:T(8,128)} %get-tuple-element.38) | copy-start | bytes 3145732
  120.3 1.7 %copy-start.1 = (f32[2,1024,256]{2,1,0:T(8,128)S(1)}, f32[2,1024,256]{2,1,0:T(8,128)}, u32[]{:S(2)}) copy-start(f32[2,1024,256]{2,1,0:T(8,128)} %get-tuple-element.42) | copy-start | bytes 6291460

commit v9 on v8

--- a/solution.py
+++ b/solution.py
@@ -387,7 +387,7 @@
 
     if beyond:
         operands = (*tile, edge, begun)
-        early = height * 9 // 16 // SUBLANES * SUBLANES
+        early = height // 2 // SUBLANES * SUBLANES
         spills = [out(2, rows, LANES) for rows in (early, height - early)]
         outs = (out(2, height, width - LANES), *spills, out(height, width))
         base = LANES

time: 155 us -> 151 us (0.974); the launches traced: 153 us -> 152 us
  transfers between devices with their start and end apart: 8 -> 8, of which waited for: 6 -> 6; matrix products, arithmetic and copies ran while one was open for 3% -> 3% of each run, Pallas kernels for 31% -> 32%
where the time goes in v9:
time: 151 us; the launch traced here: 152 us
  waiting for transfers between devices  59 us (39%)
  Pallas kernels  50.2 us (33%)
  starting transfers between devices  32.2 us (21%)
  other arithmetic  6.48 us (4%)
  between operations  2.13 us (1%)
  local copies, waits for them, and re-layouts  1.97 us (1%)
    all_to_all x3, waiting for transfers between devices, exchanged(): return lax.all_to_all(blocks, axes, split_axis=0, concat_axis=0, tiled=True)  37.7 us
    all_to_all x3, starting transfers between devices, exchanged(): return lax.all_to_all(blocks, axes, split_axis=0, concat_axis=0, tiled=True)  22.2 us
    pallas_call x2, Pallas kernels, probe_phase(): pl.pallas_call(functools.partial(probe_kernel, base=base, beyond=beyond),...  15.5 us
    pallas_call x1, Pallas kernels, volume_step(): pl.pallas_call(functools.partial(step_kernel, turned), out_shape=(jax.Sha...  12.4 us
    pallas_call x1, Pallas kernels, old_projection(): pl.pallas_call(functools.partial(old_kernel, turned), out_shape=jax.Shape...  12.3 us
    ppermute x2, waiting for transfers between devices, passed_along(): return lax.ppermute(block, axis, route)  10.7 us
    ppermute x3, waiting for transfers between devices, passed_by(): return lax.ppermute(block, axis, route)  10.6 us
    pallas_call x1, Pallas kernels, fresh_volume(): pl.pallas_call(functools.partial(fresh_kernel, turned), grid=(depth // le...  8.13 us
  transfers between devices with their start and end apart: 8, of which 6 were waited for; matrix products, arithmetic and copies ran while one was open for 3% of the time, Pallas kernels for 32%

profile of v9, /device:TPU:0, one launch (start us, length us, event | category | flops | bytes accessed | tf_op | source)
XLA Modules:
  0.0 151.9 jit_solution(14755283667749188814)
XLA Ops:
  0.6 1.9 %margins.1 = f32[2,1024,128]{2,1,0:T(8,128)} custom-call(f32[1024,384]{1,0:T(8,128)} %bitcast.18, f32[1024,384]{1,0:T(8,128)} %bitcast.21), custom_call_target="tpu_custom_call" | custom-call | tf_op jit(solution)/shard_map/margins/pallas_call | solution.py:363
  2.6 1.3 collective-permute-start
  5.2 7.6 %probes_within.1 = (f32[2,1024,128]{2,1,0:T(8,128)}, f32[2,2,1024,128]{3,2,1,0:T(8,128)}, f32[1024,128]{1,0:T(8,128)}) custom-call(s32[1,1]{1,0:T(1,128)S(6)} %copy.18.used_ref, s32[1,2,8]{2,1,0:T(2,128)} %bitcast.27, s32[1]{0:T(128)} %copy.19.shift_ref, f32[1024,384]{1,0:T(8,128)} %bitcast.19, f32[1024,384]{1,0:T(8,128)} %bitcast.22, f32[256,256]{1,0:T(8,128)} %refs_4_.1, ...), custom_call_target="tpu_custom_call" | custom-call | flops 3489660928 | bytes 6291456 | tf_op jit(solution)/shard_map/probes_within/pallas_call | solution.py:398
  12.8 12.1 %all-to-all-start = ((f32[32,32,128]{2,1,0:T(8,128)}), f32[32,32,128]{2,1,0:T(8,128)S(1)}, u32[]{:S(2)}, u32[]{:S(2)}) async-start(f32[32,32,128]{2,1,0:T(8,128)} %bitcast.24), calls=%async_computation | async-start | bytes 1048576 | tf_op jit(solution)/shard_map/all_to_all | solution.py:655
  24.8 10.7 %collective-permute-done.refs_2_ = f32[2,1024,128]{2,1,0:T(8,128)} collective-permute-done((f32[2,1024,128]{2,1,0:T(8,128)}, f32[2,1024,128]{2,1,0:T(8,128)}, u32[]{:S(2)}, u32[]{:S(2)}) %collective-permute-start) | collective-permute-done | bytes 1048608 | tf_op jit(solution)/shard_map/ppermute | solution.py:27
  35.5 7.9 %probes_beyond.1 = (f32[2,1024,256]{2,1,0:T(8,128)}, f32[2,512,128]{2,1,0:T(8,128)}, f32[2,512,128]{2,1,0:T(8,128)}, f32[1024,384]{1,0:T(8,128)}) custom-call(s32[1,1]{1,0:T(1,128)S(6)} %copy.18.used_ref, s32[1,2,8]{2,1,0:T(2,128)} %bitcast.28, s32[1]{0:T(128)} %copy.19.shift_ref, f32[1024,384]{1,0:T(8,128)} %bitcast.20, f32[1024,384]{1,0:T(8,128)} %bitcast.23, ...), custom_call_target="tpu_custom_call" | custom-call | flops 3489660928 | bytes 6291456 | tf_op jit(solution)/shard_map/probes_beyond/pallas_call | solution.py:398
  43.4 0.0 copy-start.7
  43.4 1.7 %all-to-all-done.left = f32[32,32,128]{2,1,0:T(8,128)S(1)} async-done(((f32[32,32,128]{2,1,0:T(8,128)}), f32[32,32,128]{2,1,0:T(8,128)S(1)}, u32[]{:S(2)}, u32[]{:S(2)}) %all-to-all-start) | async-done | bytes 524320 | tf_op jit(solution)/shard_map/all_to_all | solution.py:655
  45.2 0.0 copy-start.2
  45.2 6.9 %all-to-all-start.1 = ((f32[32,32,384]{2,1,0:T(8,128)}), f32[32,32,384]{2,1,0:T(8,128)S(1)}, u32[]{:S(2)}, u32[]{:S(2)}) async-start(f32[32,32,384]{2,1,0:T(8,128)} %bitcast.17), calls=%async_computation.1 | async-start | bytes 3145728 | tf_op jit(solution)/shard_map/all_to_all | solution.py:655
  52.1 3.7 %collective-permute-start.1 = (f32[2,512,128]{2,1,0:T(8,128)}, f32[2,512,128]{2,1,0:T(8,128)S(1)}, u32[]{:S(2)}, u32[]{:S(2)}) collective-permute-start(f32[2,512,128]{2,1,0:T(8,128)} %get-tuple-element.30), channel_id=1, source_target_pairs={{0,1},{2,3},{4,5},{6,7},{8,9},{10,11},{12,13},{14,15},{16,17},{18,... | collective-permute-start | bytes 1572872 | tf_op jit(solution)/shard_map/ppermute | solution.py:33
  55.8 1.3 collective-permute-start.2
  57.1 0.0 copy-done.7
  57.1 0.6 add_select_fusion.whole
  57.7 0.7 convert_multiply_fusion.frac
  58.4 12.3 %old_projection.1.old = f32[4,768,128]{2,1,0:T(8,128)} custom-call(s32[4,16]{1,0:T(4,128)} %add_select_fusion.whole, f32[4,16]{1,0:T(4,128)} %convert_multiply_fusion.frac, f32[16,32,3072]{2,1,0:T(8,128)} %volume.3), custom_call_target="tpu_custom_call" | custom-call | flops 50331648 | bytes 6291456 | tf_op jit(solution)/shard_map/old_projection/pallas_call | solution.py:592
  70.6 0.0 copy-done.2
  70.6 6.2 %collective-permute-done.1 = f32[2,512,128]{2,1,0:T(8,128)S(1)} collective-permute-done((f32[2,512,128]{2,1,0:T(8,128)}, f32[2,512,128]{2,1,0:T(8,128)S(1)}, u32[]{:S(2)}, u32[]{:S(2)}) %collective-permute-start.1) | collective-permute-done | bytes 524320 | tf_op jit(solution)/shard_map/ppermute | solution.py:33
  76.8 0.0 copy-start.4
  76.8 0.8 copy-done.4
  77.6 4.4 %collective-permute-done.2 = f32[2,512,128]{2,1,0:T(8,128)S(1)} collective-permute-done((f32[2,512,128]{2,1,0:T(8,128)}, f32[2,512,128]{2,1,0:T(8,128)S(1)}, u32[]{:S(2)}, u32[]{:S(2)}) %collective-permute-start.2) | collective-permute-done | bytes 524320 | tf_op jit(solution)/shard_map/ppermute | solution.py:33
  82.0 0.0 copy-start.8
  82.0 8.9 %all-to-all-done.1.right = f32[32,32,384]{2,1,0:T(8,128)S(1)} async-done(((f32[32,32,384]{2,1,0:T(8,128)}), f32[32,32,384]{2,1,0:T(8,128)S(1)}, u32[]{:S(2)}, u32[]{:S(2)}) %all-to-all-start.1) | async-done | bytes 1572896 | tf_op jit(solution)/shard_map/all_to_all | solution.py:655
  90.9 0.0 copy-start
  90.9 0.0 copy-done.8
  90.9 2.3 %collective-permute-start.3 = (f32[2,512,128]{2,1,0:T(8,128)}, f32[2,512,128]{2,1,0:T(8,128)S(1)}, u32[]{:S(2)}, u32[]{:S(2)}) collective-permute-start(f32[2,512,128]{2,1,0:T(8,128)} %get-tuple-element.35), channel_id=1, source_target_pairs={{0,1},{1,2},{2,3},{3,4},{4,5},{5,6},{6,7},{8,9},{9,10},{10,11},{11... | collective-permute-start | bytes 1572872 | tf_op jit(solution)/shard_map/ppermute | solution.py:27
  93.3 1.3 collective-permute-start.4
  94.6 0.0 copy-done
  94.6 12.4 %volume_step.1 = (f32[32,32,384]{2,1,0:T(8,128)}, f32[16,768,128]{2,1,0:T(8,128)}) custom-call(s32[4,16]{1,0:T(4,128)} %add_select_fusion.whole, f32[4,16]{1,0:T(4,128)} %convert_multiply_fusion.frac, f32[32,32,128]{2,1,0:T(8,128)} %copy-done.2, f32[32,32,384]{2,1,0:T(8,128)} %copy-done, f32[4,768,128]{2,1,0:T(8,128)} %old_projection.1.old), custom_call_target="tpu_custom_call" | custom-call | flops 100663296 | bytes 6291456 | tf_op jit(solution)/shard_map/volume_step/pallas_call | solution.py:605
  107.0 0.0 collective-permute-done.3
  107.0 0.0 copy-start.6
  107.0 0.0 collective-permute-done.4
  107.0 0.8 copy-done.6
  107.8 3.3 %all-to-all-start.2 = ((f32[32,32,384]{2,1,0:T(8,128)}), f32[32,32,384]{2,1,0:T(8,128)S(1)}, u32[]{:S(2)}, u32[]{:S(2)}) async-start(f32[32,32,384]{2,1,0:T(8,128)} %get-tuple-element.37), calls=%async_computation.2 | async-start | bytes 3145728 | tf_op jit(solution)/shard_map/all_to_all | solution.py:655
  111.1 0.0 copy-start.5
  111.1 0.0 copy-start.3
  111.1 8.1 %fresh_volume.1 = f32[16,32,3072]{2,1,0:T(8,128)} custom-call(f32[16,32,3072]{2,1,0:T(8,128)} %volume.3, f32[16,768,128]{2,1,0:T(8,128)} %get-tuple-element.33.update), custom_call_target="tpu_custom_call" | custom-call | flops 1572864 | bytes 18874368 | tf_op jit(solution)/shard_map/fresh_volume/pallas_call | solution.py:630
  119.3 0.0 copy-done.5
  119.3 0.0 copy-start.1
  119.3 0.1 add.19
  119.3 0.0 copy-done.3
  119.3 1.3 maximum_add_fusion
  120.7 0.4 copy-done.1
  121.0 1.9 %maximum_bitcast_fusion = f32[2,1,1024,384]{3,2,1,0:T(8,128)} fusion(f32[2,1024,256]{2,1,0:T(8,128)S(1)} %copy-done.1, f32[2,1024,128]{2,1,0:T(8,128)S(1)} %maximum_add_fusion), kind=kLoop, calls=%fused_computation.2 | loop fusion | flops 786432 | bytes 6291456
  122.9 27.1 %all-to-all-done.2 = f32[32,32,384]{2,1,0:T(8,128)S(1)} async-done(((f32[32,32,384]{2,1,0:T(8,128)}), f32[32,32,384]{2,1,0:T(8,128)S(1)}, u32[]{:S(2)}, u32[]{:S(2)}) %all-to-all-start.2) | async-done | bytes 1572896 | tf_op jit(solution)/shard_map/all_to_all | solution.py:655
  149.9 2.0 %fusion.1 = f32[1,1024,384]{2,1,0:T(8,128)} fusion(s32[]{:T(128)S(6)} %select_n.20, f32[1024,384]{1,0:T(8,128)S(1)} %bitcast.16), kind=kLoop, calls=%fused_computation.4 | loop fusion | flops 393216 | bytes 3145732 | tf_op jit(solution)/shard_map/broadcast_in_dim | solution.py:678
Async XLA Ops:
  2.6 32.9 %collective-permute-start = (f32[2,1024,128]{2,1,0:T(8,128)}, f32[2,1024,128]{2,1,0:T(8,128)}, u32[]{:S(2)}, u32[]{:S(2)}) collective-permute-start(f32[2,1024,128]{2,1,0:T(8,128)} %margins.1), channel_id=1, source_target_pairs={{1,0},{2,1},{3,2},{4,3},{5,4},{6,5},{7,6},{9,8},{10,9},{11,10},{12... | collective-permute-start | bytes 3145736 | tf_op jit(solution)/shard_map/ppermute | solution.py:27
  12.8 32.4 %all-to-all-start = ((f32[32,32,128]{2,1,0:T(8,128)}), f32[32,32,128]{2,1,0:T(8,128)S(1)}, u32[]{:S(2)}, u32[]{:S(2)}) async-start(f32[32,32,128]{2,1,0:T(8,128)} %bitcast.24), calls=%async_computation | async-start | bytes 1048576 | tf_op jit(solution)/shard_map/all_to_all | solution.py:655
  43.4 13.7 %copy-start.7 = (s32[4]{0:T(128)S(1)}, s32[4]{0:T(128)}, u32[]{:S(2)}) copy-start(s32[4]{0:T(128)} %param.22) | copy-start | bytes 52
  45.2 25.5 %copy-start.2 = (f32[32,32,128]{2,1,0:T(8,128)}, f32[32,32,128]{2,1,0:T(8,128)S(1)}, u32[]{:S(2)}) copy-start(f32[32,32,128]{2,1,0:T(8,128)S(1)} %all-to-all-done.left) | copy-start | bytes 1572868
  45.2 45.7 %all-to-all-start.1 = ((f32[32,32,384]{2,1,0:T(8,128)}), f32[32,32,384]{2,1,0:T(8,128)S(1)}, u32[]{:S(2)}, u32[]{:S(2)}) async-start(f32[32,32,384]{2,1,0:T(8,128)} %bitcast.17), calls=%async_computation.1 | async-start | bytes 3145728 | tf_op jit(solution)/shard_map/all_to_all | solution.py:655
  52.1 24.7 %collective-permute-start.1 = (f32[2,512,128]{2,1,0:T(8,128)}, f32[2,512,128]{2,1,0:T(8,128)S(1)}, u32[]{:S(2)}, u32[]{:S(2)}) collective-permute-start(f32[2,512,128]{2,1,0:T(8,128)} %get-tuple-element.30), channel_id=1, source_target_pairs={{0,1},{2,3},{4,5},{6,7},{8,9},{10,11},{12,13},{14,15},{16,17},{18,... | collective-permute-start | bytes 1572872 | tf_op jit(solution)/shard_map/ppermute | solution.py:33
  55.8 26.2 %collective-permute-start.2 = (f32[2,512,128]{2,1,0:T(8,128)}, f32[2,512,128]{2,1,0:T(8,128)S(1)}, u32[]{:S(2)}, u32[]{:S(2)}) collective-permute-start(f32[2,512,128]{2,1,0:T(8,128)} %get-tuple-element.30), channel_id=1, source_target_pairs={{1,0},{3,2},{5,4},{7,6},{9,8},{11,10},{13,12},{15,14},{17,16},{19,... | collective-permute-start | bytes 1572872 | tf_op jit(solution)/shard_map/ppermute | solution.py:33
  76.8 0.8 copy-start.4
  82.0 8.9 %copy-start.8 = (f32[2,512,128]{2,1,0:T(8,128)}, f32[2,512,128]{2,1,0:T(8,128)S(1)}, u32[]{:S(2)}) copy-start(f32[2,512,128]{2,1,0:T(8,128)S(1)} %collective-permute-done.2) | copy-start | bytes 1572868
  90.9 3.7 %copy-start = (f32[32,32,384]{2,1,0:T(8,128)}, f32[32,32,384]{2,1,0:T(8,128)S(1)}, u32[]{:S(2)}) copy-start(f32[32,32,384]{2,1,0:T(8,128)S(1)} %all-to-all-done.1.right) | copy-start | bytes 4718596
  90.9 16.1 %collective-permute-start.3 = (f32[2,512,128]{2,1,0:T(8,128)}, f32[2,512,128]{2,1,0:T(8,128)S(1)}, u32[]{:S(2)}, u32[]{:S(2)}) collective-permute-start(f32[2,512,128]{2,1,0:T(8,128)} %get-tuple-element.35), channel_id=1, source_target_pairs={{0,1},{1,2},{2,3},{3,4},{4,5},{5,6},{6,7},{8,9},{9,10},{10,11},{11... | collective-permute-start | bytes 1572872 | tf_op jit(solution)/shard_map/ppermute | solution.py:27
  93.3 13.8 %collective-permute-start.4 = (f32[2,512,128]{2,1,0:T(8,128)}, f32[2,512,128]{2,1,0:T(8,128)S(1)}, u32[]{:S(2)}, u32[]{:S(2)}) collective-permute-start(f32[2,512,128]{2,1,0:T(8,128)} %copy-done.8), channel_id=1, source_target_pairs={{0,2},{2,4},{4,6},{8,10},{10,12},{12,14},{16,18},{18,20},{20,22},{... | collective-permute-start | bytes 1572872 | tf_op jit(solution)/shard_map/ppermute | solution.py:33
  107.0 0.8 copy-start.6
  107.8 42.1 %all-to-all-start.2 = ((f32[32,32,384]{2,1,0:T(8,128)}), f32[32,32,384]{2,1,0:T(8,128)S(1)}, u32[]{:S(2)}, u32[]{:S(2)}) async-start(f32[32,32,384]{2,1,0:T(8,128)} %get-tuple-element.37), calls=%async_computation.2 | async-start | bytes 3145728 | tf_op jit(solution)/shard_map/all_to_all | solution.py:655
  111.1 8.2 %copy-start.5 = (f32[2,512,128]{2,1,0:T(8,128)S(1)}, f32[2,512,128]{2,1,0:T(8,128)}, u32[]{:S(2)}) copy-start(f32[2,512,128]{2,1,0:T(8,128)} %copy-done.4) | copy-start | bytes 1572868
  111.1 8.2 %copy-start.3 = (f32[2,1024,128]{2,1,0:T(8,128)S(1)}, f32[2,1024,128]{2,1,0:T(8,128)}, u32[]{:S(2)}) copy-start(f32[2,1024,128]{2,1,0:T(8,128)} %get-tuple-element.38) | copy-start | bytes 3145732
  119.3 1.7 %copy-start.1 = (f32[2,1024,256]{2,1,0:T(8,128)S(1)}, f32[2,1024,256]{2,1,0:T(8,128)}, u32[]{:S(2)}) copy-start(f32[2,1024,256]{2,1,0:T(8,128)} %get-tuple-element.42) | copy-start | bytes 6291460
